TPU v7x, 32 devices: a whole 2x2x4 slice. The times are simulated.
32 devices in a mesh: groups: 2 (over y), seq: 4 (over z), wloop: 2 (over x), heads: 2 (over core).
Axes of the slice: x: 2, y: 2, z: 4, core: 2. Of those that a mesh axis runs over, the one named last changes fastest.
Arguments:
- activations: bfloat16 [4, 2048, 2048], P(('groups', 'wloop'), 'seq'), parts along dimension 0, may hold values from -6 to 6
- norm_gain: float32 [2048], replicated, may hold values from 0.1 to 1.9
- w_query: bfloat16 [2048, 2048], P('wloop', 'heads'), may hold values from -0.125 to 0.125
- w_keyvalue: bfloat16 [2048, 2, 2048], P('wloop', None, 'heads'), may hold values from -0.125 to 0.125
- w_output: bfloat16 [2048, 2048], P('heads', 'wloop'), may hold values from -0.125 to 0.125
- log_retain: float32 [4, 16, 2048], P(('groups', 'wloop'), 'heads', 'seq'), parts along dimension 0, may hold values from -3 to 0, as said below
- resets: int32 [4, 4], P(('groups', 'wloop'), 'seq'), parts along dimension 0, may hold values 0 or 1
Outputs:
- layer_out: bfloat16 [4, 2048, 2048], P(('groups', 'wloop'), 'seq', 'heads'), parts along dimension 0
There are 2 independent parts, one for each index of `groups`. A program takes and returns all parts, laid end to end along the dimension named above; an argument that names none is the same for every part. Nothing has to cross between parts.
Inputs may be any that keep to these rules, and one draw needn't show every extreme that they name: `log_retain`: log retention per token and head, never above zero.
All inputs are finite; a program needn't handle non-finite values. No bound on the sum of `resets` on one device may be relied on, other than what follows from the above.
Results may differ from a plain program's by a relative error of at most 0.02.
Values may be sent and summed in bfloat16 or wider, within the bound.
A program may use at most 128 MiB of HBM per device.

v0:
```python
import math

import jax
import jax.numpy as jnp
from jax import lax
from jax.sharding import PartitionSpec as P

SCORE_SCALE = 2.0


def shifted(value, axis, steps):
    count = lax.axis_size(axis)
    initial, last = (max(0, -steps), min(count, count - steps))
    return lax.ppermute(value, axis, [(source, source + steps) for source in range(initial, last)])


def rms_rows(values, eps):
    return values * lax.rsqrt(jnp.mean(values * values, axis=-1, keepdims=True) + eps)


def window_mix(queries, lookup_vectors, values, prior_keys, prior_values, allow, scale):
    own = (
        jnp.einsum("bihd,bjhd->bhij", queries, lookup_vectors, preferred_element_type=jnp.float32)
        * scale
    )
    prior = (
        jnp.einsum("bihd,bjhd->bhij", queries, prior_keys, preferred_element_type=jnp.float32)
        * scale
    )
    span = queries.shape[1]
    row_pos = lax.broadcasted_iota(jnp.int32, (span, span), 0)
    column_pos = lax.broadcasted_iota(jnp.int32, (span, span), 1)
    own_w = jnp.where(column_pos <= row_pos, jnp.exp(own), 0.0)
    prior_w = jnp.where((column_pos > row_pos) & allow[:, None, None, None], jnp.exp(prior), 0.0)
    total = jnp.sum(own_w, axis=-1, keepdims=True) + jnp.sum(prior_w, axis=-1, keepdims=True)
    own_p = (own_w / total).astype(jnp.bfloat16)
    prior_p = (prior_w / total).astype(jnp.bfloat16)
    return jnp.einsum(
        "bhij,bjhd->bihd", own_p, values, preferred_element_type=jnp.float32
    ) + jnp.einsum("bhij,bjhd->bihd", prior_p, prior_values, preferred_element_type=jnp.float32)


def shards(activations, norm_gain, w_query, w_keyvalue, w_output, log_retain, resets):
    trajs, span, width = activations.shape
    heads_here = log_retain.shape[1]
    inner_here = w_query.shape[1]
    head_dim = inner_here // heads_here
    scale = SCORE_SCALE / math.sqrt(head_dim)
    count = trajs * span
    normed = (rms_rows(activations.astype(jnp.float32), 1e-05) * norm_gain).astype(jnp.bfloat16)
    normed = normed.reshape(count, width)
    columns = normed
    query_raw = jnp.dot(
        columns,
        lax.all_gather(w_query, "wloop", axis=0, tiled=True),
        preferred_element_type=jnp.float32,
    )
    columns = normed
    pair_raw = jnp.einsum(
        "td,dje->jte",
        columns,
        lax.all_gather(w_keyvalue, "wloop", axis=0, tiled=True),
        preferred_element_type=jnp.float32,
    )
    lookup_vectors = rms_rows(pair_raw[0].reshape(trajs, span, heads_here, head_dim), 1e-06).astype(
        jnp.bfloat16
    )
    values = pair_raw[1].reshape(trajs, span, heads_here, head_dim).astype(jnp.bfloat16)
    prior_keys, prior_values = shifted(
        (lookup_vectors.reshape(trajs, span, inner_here), values.reshape(trajs, span, inner_here)),
        "seq",
        1,
    )
    queries = rms_rows(query_raw.reshape(trajs, span, heads_here, head_dim), 1e-06).astype(
        jnp.bfloat16
    )
    keep = (1 - resets[:, 0]).astype(jnp.float32)
    climb = jnp.cumsum(log_retain, axis=-1)
    whole = climb[:, :, -1]
    factor = jnp.exp(whole) * keep[:, None]
    weight = jnp.exp(whole[:, :, None] - climb)
    local_state = jnp.einsum(
        "bht,bthd,bthe->bhde",
        weight,
        lookup_vectors.astype(jnp.float32),
        values.astype(jnp.float32),
        precision=lax.Precision.HIGHEST,
    )
    local_mass = jnp.sum(weight * weight, axis=-1)

    def relay_turn(turn, carry):
        state, mass = carry
        return (
            shifted(
                (factor[:, :, None, None] * state + local_state).astype(jnp.bfloat16), "seq", 1
            ).astype(jnp.float32),
            shifted((factor * factor * mass + local_mass).astype(jnp.bfloat16), "seq", 1).astype(
                jnp.float32
            ),
        )

    entering, entering_mass = lax.fori_loop(
        0,
        lax.axis_size("seq") - 1,
        relay_turn,
        (jnp.zeros_like(local_state), jnp.zeros_like(local_mass)),
    )
    entering = entering * keep[:, None, None, None]
    entering_mass = entering_mass * keep[:, None]
    read = jnp.einsum(
        "bthd,bhde->bthe", queries.astype(jnp.float32), entering, precision=lax.Precision.HIGHEST
    )
    read = read * jnp.exp(climb).transpose(0, 2, 1)[..., None]
    read = read / jnp.sqrt(head_dim * (1.0 + entering_mass))[:, None, :, None]
    allow = (keep > 0.5) & (lax.axis_index("seq") > 0)
    window = window_mix(
        queries,
        lookup_vectors,
        values,
        prior_keys.reshape(trajs, span, heads_here, head_dim),
        prior_values.reshape(trajs, span, heads_here, head_dim),
        allow,
        scale,
    )
    attended = (window + read).astype(jnp.bfloat16).reshape(count, inner_here)
    partial_out = jnp.dot(
        attended,
        lax.all_gather(w_output, "wloop", axis=1, tiled=True),
        preferred_element_type=jnp.float32,
    )
    summed = lax.psum_scatter(
        partial_out.astype(jnp.bfloat16), "heads", scatter_dimension=1, tiled=True
    ).astype(jnp.float32)
    share = summed.shape[1]
    residual = lax.dynamic_slice_in_dim(
        activations.reshape(count, width), lax.axis_index("heads") * share, share, 1
    )
    return (residual.astype(jnp.float32) + summed).astype(jnp.bfloat16).reshape(trajs, span, share)


def solution(mesh):
    placed = (
        P(("groups", "wloop"), "seq", None),
        P(),
        P("wloop", "heads"),
        P("wloop", None, "heads"),
        P("heads", "wloop"),
        P(("groups", "wloop"), "heads", "seq"),
        P(("groups", "wloop"), "seq"),
    )
    return jax.shard_map(
        shards,
        mesh=mesh,
        in_specs=placed,
        out_specs=P(("groups", "wloop"), "seq", "heads"),
        check_vma=False,
    )
```

profile of v0, /device:TPU:0, one launch (start us, length us, event | category | flops | bytes accessed | tf_op | source)
XLA Modules:
  0.0 323.1 jit_solution(7021560980977442523)
XLA Ops:
  6.5 0.7 all-gather.6.cloned.1.call-update
  7.3 0.0 all-gather.4.cloned.1.call-start
  7.3 5.5 %copy.60 = bf16[1024,2,1024]{2,0,1:T(8,128)(2,1)} copy(bf16[1024,2,1024]{2,1,0:T(2,128)(2,1)} %param.12) | data formatting | bytes 8388608 | tf_op args[3]
  12.8 0.0 all-gather.8.cloned.1.call-start
  12.9 0.7 all-gather.8.cloned.1.call-update
  13.6 0.0 reduce-scatter.2.cloned.1.call-start
  13.6 1.1 reduce-window.6
  14.8 0.2 slice_reduce_fusion
  15.0 0.1 exponential_bitcast_fusion
  15.7 0.2 slice_reduce_fusion.1
  15.9 0.1 fusion.42
  16.0 0.2 multiply_reduce_fusion
  16.2 0.8 iota_compare_fusion.1
  17.0 0.5 fusion.7
  17.5 0.8 fusion.30
  18.3 50.1 %all-gather.6.cloned.1.call-done = bf16[2048,1024]{1,0:T(8,128)(2,1)} async-done(((bf16[1024,1024]{1,0:T(8,128)(2,1)}), bf16[2048,1024]{1,0:T(8,128)(2,1)}) %all-gather.6.cloned.1.call-update) | async-done | bytes 4194320 | tf_op jit(solution)/shard_map/all_gather | solution.py:55
  68.4 4.6 %fusion.18 = f32[512,1024]{1,0:T(8,128)S(1)} fusion(bf16[2048,1024]{1,0:T(8,128)(2,1)} %all-gather.6.cloned.1.call-done, bf16[1,512,2048]{2,1,0:T(8,128)(2,1)S(1)} %copy-done.2, f32[2048]{0:T(1024)S(1)} %copy-done.12, f32[512]{0:T(512)S(1)} %add_rsqrt_fusion.2), kind=kOutput, calls=%fused_computation.32 | convolution fusion | flops 2151677952 | bytes 8398848 | tf_op jit(solution)/shard_map/dot_general | solution.py:53
  73.0 0.3 multiply_bitcast_fusion.1
  73.3 1.1 copy-done.1
  74.3 0.5 copy.83
  74.8 0.6 reduce_sum.57
  75.4 0.1 copy.61
  75.5 3.2 fusion.12
  78.7 95.2 %all-gather.4.cloned.1.call-done = bf16[2048,2,1024]{2,0,1:T(8,128)(2,1)} async-done(((bf16[1024,2,1024]{2,0,1:T(8,128)(2,1)}), bf16[2048,2,1024]{2,0,1:T(8,128)(2,1)}) %all-gather.4.cloned.1.call-update) | async-done | bytes 8388624 | tf_op jit(solution)/shard_map/all_gather | solution.py:62
  174.0 6.9 %convolution_bitcast_fusion = f32[2,512,1024]{2,1,0:T(8,128)S(1)} fusion(bf16[2048,2,1024]{2,0,1:T(8,128)(2,1)} %all-gather.4.cloned.1.call-done, bf16[1,512,2048]{2,1,0:T(8,128)(2,1)S(1)} %copy-done.3, f32[2048]{0:T(1024)S(1)} %copy-done.12, f32[512]{0:T(512)S(1)} %add_rsqrt_fusion.2), kind=kOutput, calls=%fused_computation.21 | convolution fusion | flops 4299161600 | bytes 14690304 | tf_op jit(solution)/shard_map/td,dje->jte/dot_general | solution.py:59
  180.9 0.3 multiply_bitcast_fusion
  181.2 1.5 slice_bitcast_fusion.1
  182.7 0.6 copy-done
  183.4 1.2 slice.31
  184.5 0.5 copy.84
  185.0 0.6 reduce_sum.58
  185.6 0.1 copy.63
  185.7 1.6 mul.196
  187.3 2.1 copy.79
  189.4 3.9 %multiply_convert_fusion = (bf16[1,512,1024]{2,1,0:T(8,128)(2,1)}, f32[1,512,1024]{2,1,0:T(8,128)}) fusion(f32[1,512,1024]{2,1,0:T(8,128)S(1)} %copy.79, f32[2,512,1024]{2,1,0:T(8,128)} %copy-done), kind=kLoop, calls=%fused_computation.37 | loop fusion | flops 1048576 | bytes 7340032 | tf_op jit(solution)/shard_map/convert_element_type | solution.py:65
  193.3 1.9 copy.78
  195.2 1.5 copy.82
  196.7 4.4 %collective-permute-start.2 = (bf16[1,512,1024]{2,1,0:T(8,128)(2,1)}, bf16[1,512,1024]{2,1,0:T(8,128)(2,1)}, u32[]{:S(2)}, u32[]{:S(2)}) collective-permute-start(bf16[1,512,1024]{2,1,0:T(8,128)(2,1)} %get-tuple-element.111), channel_id=1, source_target_pairs={{0,4},{4,8},{8,12},{1,5},{5,9},{9,13},{2,6},{6,10},{10,14},{3,7},{... | collective-permute-start | bytes 3145736 | tf_op jit(solution)/shard_map/ppermute | solution.py:14
  201.1 3.5 %collective-permute-start.3 = (bf16[1,512,1024]{2,1,0:T(8,128)(2,1)}, bf16[1,512,1024]{2,1,0:T(8,128)(2,1)}, u32[]{:S(2)}, u32[]{:S(2)}) collective-permute-start(bf16[1,512,1024]{2,1,0:T(8,128)(2,1)} %slice.31), channel_id=1, source_target_pairs={{0,4},{4,8},{8,12},{1,5},{5,9},{9,13},{2,6},{6,10},{10,14},{3,7},{... | collective-permute-start | bytes 3145736 | tf_op jit(solution)/shard_map/ppermute | solution.py:14
  204.6 1.4 fusion.23
  205.9 65.0 %while.14 = (s32[]{:T(128)}, f32[1,8,128,128]{3,2,1,0:T(8,128)S(1)}, f32[1,8]{1,0:T(1,128)S(1)}, f32[1,8]{1,0:T(1,128)S(1)}, f32[1,8,128,128]{3,2,1,0:T(8,128)S(...) while((s32[]{:T(128)}, f32[1,8,128,128]{3,2,1,0:T(8,128)S(1)}, ...), condition=%wide.region_9.10_spmd.clone, body=%wide.region_8.9_spmd.clone.sunk | while | flops 655403 | bytes 3146168 | solution.py:102
  206.1 0.8 fusion.58
  206.9 2.3 collective-permute-start
  209.3 1.9 collective-permute-start.1
  211.2 39.6 %collective-permute-done.1 = bf16[1,8]{1,0:T(2,128)(2,1)S(1)} collective-permute-done((bf16[1,8]{1,0:T(2,128)(2,1)S(1)}, bf16[1,8]{1,0:T(2,128)(2,1)S(1)}, u32[]{:S(2)}, u32[]{:S(2)}) %collective-permute-start.1) | collective-permute-done | bytes 48 | tf_op jit(solution)/shard_map/while/body/eval_jaxpr/ppermute | solution.py:14
  250.9 0.8 fusion.58
  251.7 4.3 %collective-permute-start = (bf16[1,8,128,128]{3,2,1,0:T(8,128)(2,1)}, bf16[1,8,128,128]{3,2,1,0:T(8,128)(2,1)S(1)}, u32[]{:S(2)}, u32[]{:S(2)}) collective-permute-start(bf16[1,8,128,128]{3,2,1,0:T(8,128)(2,1)} %fusion.58), channel_id=1, source_target_pairs={{0,4},{4,8},{8,12},{1,5},{5,9},{9,13},{2,6},{6,10},{10,14},{3,7},{... | collective-permute-start | bytes 786440 | tf_op jit(solution)/shard_map/while/body/eval_jaxpr/ppermute | solution.py:14
  256.1 3.4 %collective-permute-start.1 = (bf16[1,8]{1,0:T(2,128)(2,1)S(1)}, bf16[1,8]{1,0:T(2,128)(2,1)S(1)}, u32[]{:S(2)}, u32[]{:S(2)}) collective-permute-start(bf16[1,8]{1,0:T(2,128)(2,1)S(1)} %fusion.59), channel_id=1, source_target_pairs={{0,4},{4,8},{8,12},{1,5},{5,9},{9,13},{2,6},{6,10},{10,14},{3,7},{... | collective-permute-start | bytes 56 | tf_op jit(solution)/shard_map/while/body/eval_jaxpr/ppermute | solution.py:14
  259.5 1.5 collective-permute-done.1
  261.0 0.8 fusion.58
  261.8 4.3 %collective-permute-start = (bf16[1,8,128,128]{3,2,1,0:T(8,128)(2,1)}, bf16[1,8,128,128]{3,2,1,0:T(8,128)(2,1)S(1)}, u32[]{:S(2)}, u32[]{:S(2)}) collective-permute-start(bf16[1,8,128,128]{3,2,1,0:T(8,128)(2,1)} %fusion.58), channel_id=1, source_target_pairs={{0,4},{4,8},{8,12},{1,5},{5,9},{9,13},{2,6},{6,10},{10,14},{3,7},{... | collective-permute-start | bytes 786440 | tf_op jit(solution)/shard_map/while/body/eval_jaxpr/ppermute | solution.py:14
  266.2 3.4 %collective-permute-start.1 = (bf16[1,8]{1,0:T(2,128)(2,1)S(1)}, bf16[1,8]{1,0:T(2,128)(2,1)S(1)}, u32[]{:S(2)}, u32[]{:S(2)}) collective-permute-start(bf16[1,8]{1,0:T(2,128)(2,1)S(1)} %fusion.59), channel_id=1, source_target_pairs={{0,4},{4,8},{8,12},{1,5},{5,9},{9,13},{2,6},{6,10},{10,14},{3,7},{... | collective-permute-start | bytes 56 | tf_op jit(solution)/shard_map/while/body/eval_jaxpr/ppermute | solution.py:14
  269.6 1.3 collective-permute-done.1
  270.9 3.7 %fusion.35 = f32[8,128,512]{2,1,0:T(8,128)} fusion(bf16[512,8,128]{2,0,1:T(8,128)(2,1)} %fusion.12, f32[1,8,128,128]{3,2,1,0:T(8,128)S(1)} %get-tuple-element.67, f32[]{:T(128)} %bitcast.16), kind=kOutput, calls=%fused_computation.51 | convolution fusion | flops 805437440 | bytes 3670020 | tf_op jit(solution)/shard_map/bthd,bhde->bthe/dot_general | solution.py:110
  274.6 5.5 %fusion.5 = (f32[8,512]{1,0:T(8,128)S(1)}, f32[8,512,512]{1,2,0:T(8,128)}) fusion(pred[512,512]{0,1:T(8,128)(4,1)S(1)} %copy-done.9, bf16[512,8,128]{2,0,1:T(8,128)(2,1)S(1)} %copy-done.7, f32[512,8,128]{0,2,1:T(8,128)S(1)} %bitcast.104, f32[512,8]{0,1:T(8,128)S(1)} %add_rsqrt_fusion), kind=kOutput, calls=%fused_computation.11 | convolution fusion | flops 544206848 | bytes 11829248 | tf_op jit(solution)/shard_map/bihd,bjhd->bhij/dot_general | solution.py:23
  280.1 1.5 copy.85
  281.7 5.2 %fusion.6 = (f32[8,512]{1,0:T(8,128)S(1)}, f32[8,512,512]{1,2,0:T(8,128)}) fusion(pred[512,512]{0,1:T(8,128)(4,1)S(1)} %copy-done.10, bf16[512,8,128]{2,0,1:T(8,128)(2,1)S(1)} %copy-done.7, bf16[512,8,128]{2,1,0:T(8,128)(2,1)S(1)} %bitcast.111), kind=kOutput, calls=%fused_computation.12 | convolution fusion | flops 543158272 | bytes 10764288 | tf_op jit(solution)/shard_map/bihd,bjhd->bhij/dot_general | solution.py:27
  286.9 1.6 copy.80
  288.5 4.8 %fusion.10 = f32[8,128,512]{2,1,0:T(8,128)S(1)} fusion(f32[8,512,512]{1,2,0:T(8,128)} %get-tuple-element.114, f32[8,512]{1,0:T(8,128)S(1)} %add.75, pred[512,512]{0,1:T(8,128)(4,1)S(1)} %copy-done.9, bf16[512,8,128]{2,1,0:T(8,128)(2,1)S(1)} %bitcast.109), kind=kOutput, calls=%fused_computation.18 | convolution fusion | flops 545259520 | bytes 11812864 | tf_op jit(solution)/shard_map/bhij,bjhd->bihd/dot_general | solution.py:38
  293.4 1.6 copy-done.13
  295.0 2.5 fusion.15
  297.6 5.9 %convolution_convert_fusion = bf16[512,2048]{1,0:T(8,128)(2,1)} fusion(bf16[512,1024]{0,1:T(8,128)(2,1)S(1)} %bitcast.117, bf16[1024,2048]{1,0:T(8,128)(2,1)} %all-gather.8.cloned.1.call-done), kind=kOutput, calls=%fused_computation.20 | convolution fusion | flops 2148532224 | bytes 7340032 | tf_op jit(solution)/shard_map/dot_general | solution.py:126
  303.5 10.4 %reduce-scatter.2.cloned.1.call-done = bf16[512,1024]{1,0:T(8,128)(2,1)} async-done(((bf16[512,2048]{1,0:T(8,128)(2,1)}), bf16[512,1024]{1,0:T(8,128)(2,1)}) %reduce-scatter.2.cloned.1.call-update) | async-done | bytes 1048592 | tf_op jit(solution)/shard_map/reduce_scatter | solution.py:131
  313.9 2.6 fusion.26
  (53 shorter events, 0.4 us)
Async XLA Ops:
  6.5 61.9 %all-gather.6.cloned.1.call-start = ((), (), s32[]{:S(2)}) async-start(), calls=%async_computation.2 | async-start | bytes 6291456 | tf_op jit(solution)/shard_map/all_gather | solution.py:55
  7.3 166.7 %all-gather.4.cloned.1.call-start = ((), (), s32[]{:S(2)}) async-start(), calls=%async_computation.1 | async-start | bytes 12582912 | tf_op jit(solution)/shard_map/all_gather | solution.py:62
  12.8 0.8 copy-start.11
  12.8 4.2 %copy-start.2 = (bf16[1,512,2048]{2,1,0:T(8,128)(2,1)S(1)}, bf16[1,512,2048]{2,1,0:T(8,128)(2,1)}, u32[]{:S(2)}) copy-start(bf16[1,512,2048]{2,1,0:T(8,128)(2,1)} %param.9) | copy-start | bytes 6291460
  12.8 55.6 %copy-start.12 = (f32[2048]{0:T(1024)S(1)}, f32[2048]{0:T(1024)}, u32[]{:S(2)}) copy-start(f32[2048]{0:T(1024)} %param.10) | copy-start | bytes 24580
  12.8 284.7 %all-gather.8.cloned.1.call-start = ((), (), s32[]{:S(2)}) async-start(), calls=%async_computation.3 | async-start | bytes 6291456 | tf_op jit(solution)/shard_map/all_gather | solution.py:128
  13.6 300.4 %reduce-scatter.2.cloned.1.call-start = ((), (), s32[]{:S(2)}) async-start(), calls=%async_computation.4 | async-start | bytes 3145728 | tf_op jit(solution)/shard_map/reduce_scatter | solution.py:131
  73.0 1.3 copy-start.1
  75.4 98.6 %copy-start.3 = (bf16[1,512,2048]{2,1,0:T(8,128)(2,1)S(1)}, bf16[1,512,2048]{2,1,0:T(8,128)(2,1)}, u32[]{:S(2)}) copy-start(bf16[1,512,2048]{2,1,0:T(8,128)(2,1)} %param.9) | copy-start | bytes 6291460
  180.9 2.5 copy-start
  196.7 7.9 %copy-start.5 = (bf16[64,8,8,128]{3,2,1,0:T(8,128)(2,1)}, bf16[64,8,8,128]{3,2,1,0:T(8,128)(2,1)S(1)}, u32[]{:S(2)}) copy-start(bf16[64,8,8,128]{3,2,1,0:T(8,128)(2,1)S(1)} %copy.82) | copy-start | bytes 3145732
  196.7 83.4 %collective-permute-start.2 = (bf16[1,512,1024]{2,1,0:T(8,128)(2,1)}, bf16[1,512,1024]{2,1,0:T(8,128)(2,1)}, u32[]{:S(2)}, u32[]{:S(2)}) collective-permute-start(bf16[1,512,1024]{2,1,0:T(8,128)(2,1)} %get-tuple-element.111), channel_id=1, source_target_pairs={{0,4},{4,8},{8,12},{1,5},{5,9},{9,13},{2,6},{6,10},{10,14},{3,7},{... | collective-permute-start | bytes 3145736 | tf_op jit(solution)/shard_map/ppermute | solution.py:14
  201.1 85.8 %collective-permute-start.3 = (bf16[1,512,1024]{2,1,0:T(8,128)(2,1)}, bf16[1,512,1024]{2,1,0:T(8,128)(2,1)}, u32[]{:S(2)}, u32[]{:S(2)}) collective-permute-start(bf16[1,512,1024]{2,1,0:T(8,128)(2,1)} %slice.31), channel_id=1, source_target_pairs={{0,4},{4,8},{8,12},{1,5},{5,9},{9,13},{2,6},{6,10},{10,14},{3,7},{... | collective-permute-start | bytes 3145736 | tf_op jit(solution)/shard_map/ppermute | solution.py:14
  206.9 43.9 %collective-permute-start = (bf16[1,8,128,128]{3,2,1,0:T(8,128)(2,1)}, bf16[1,8,128,128]{3,2,1,0:T(8,128)(2,1)S(1)}, u32[]{:S(2)}, u32[]{:S(2)}) collective-permute-start(bf16[1,8,128,128]{3,2,1,0:T(8,128)(2,1)} %fusion.58), channel_id=1, source_target_pairs={{0,4},{4,8},{8,12},{1,5},{5,9},{9,13},{2,6},{6,10},{10,14},{3,7},{... | collective-permute-start | bytes 786440 | tf_op jit(solution)/shard_map/while/body/eval_jaxpr/ppermute | solution.py:14
  209.3 41.5 %collective-permute-start.1 = (bf16[1,8]{1,0:T(2,128)(2,1)S(1)}, bf16[1,8]{1,0:T(2,128)(2,1)S(1)}, u32[]{:S(2)}, u32[]{:S(2)}) collective-permute-start(bf16[1,8]{1,0:T(2,128)(2,1)S(1)} %fusion.59), channel_id=1, source_target_pairs={{0,4},{4,8},{8,12},{1,5},{5,9},{9,13},{2,6},{6,10},{10,14},{3,7},{... | collective-permute-start | bytes 56 | tf_op jit(solution)/shard_map/while/body/eval_jaxpr/ppermute | solution.py:14
  251.7 9.2 %collective-permute-start = (bf16[1,8,128,128]{3,2,1,0:T(8,128)(2,1)}, bf16[1,8,128,128]{3,2,1,0:T(8,128)(2,1)S(1)}, u32[]{:S(2)}, u32[]{:S(2)}) collective-permute-start(bf16[1,8,128,128]{3,2,1,0:T(8,128)(2,1)} %fusion.58), channel_id=1, source_target_pairs={{0,4},{4,8},{8,12},{1,5},{5,9},{9,13},{2,6},{6,10},{10,14},{3,7},{... | collective-permute-start | bytes 786440 | tf_op jit(solution)/shard_map/while/body/eval_jaxpr/ppermute | solution.py:14
  256.1 4.8 %collective-permute-start.1 = (bf16[1,8]{1,0:T(2,128)(2,1)S(1)}, bf16[1,8]{1,0:T(2,128)(2,1)S(1)}, u32[]{:S(2)}, u32[]{:S(2)}) collective-permute-start(bf16[1,8]{1,0:T(2,128)(2,1)S(1)} %fusion.59), channel_id=1, source_target_pairs={{0,4},{4,8},{8,12},{1,5},{5,9},{9,13},{2,6},{6,10},{10,14},{3,7},{... | collective-permute-start | bytes 56 | tf_op jit(solution)/shard_map/while/body/eval_jaxpr/ppermute | solution.py:14
  261.8 9.0 %collective-permute-start = (bf16[1,8,128,128]{3,2,1,0:T(8,128)(2,1)}, bf16[1,8,128,128]{3,2,1,0:T(8,128)(2,1)S(1)}, u32[]{:S(2)}, u32[]{:S(2)}) collective-permute-start(bf16[1,8,128,128]{3,2,1,0:T(8,128)(2,1)} %fusion.58), channel_id=1, source_target_pairs={{0,4},{4,8},{8,12},{1,5},{5,9},{9,13},{2,6},{6,10},{10,14},{3,7},{... | collective-permute-start | bytes 786440 | tf_op jit(solution)/shard_map/while/body/eval_jaxpr/ppermute | solution.py:14
  266.2 4.6 %collective-permute-start.1 = (bf16[1,8]{1,0:T(2,128)(2,1)S(1)}, bf16[1,8]{1,0:T(2,128)(2,1)S(1)}, u32[]{:S(2)}, u32[]{:S(2)}) collective-permute-start(bf16[1,8]{1,0:T(2,128)(2,1)S(1)} %fusion.59), channel_id=1, source_target_pairs={{0,4},{4,8},{8,12},{1,5},{5,9},{9,13},{2,6},{6,10},{10,14},{3,7},{... | collective-permute-start | bytes 56 | tf_op jit(solution)/shard_map/while/body/eval_jaxpr/ppermute | solution.py:14
  270.9 3.7 %copy-start.7 = (bf16[512,8,128]{2,0,1:T(8,128)(2,1)S(1)}, bf16[512,8,128]{2,0,1:T(8,128)(2,1)}, u32[]{:S(2)}) copy-start(bf16[512,8,128]{2,0,1:T(8,128)(2,1)} %fusion.12) | copy-start | bytes 3145732
  270.9 3.7 %copy-start.9 = (pred[512,512]{0,1:T(8,128)(4,1)S(1)}, pred[512,512]{0,1:T(8,128)(4,1)}, u32[]{:S(2)}) copy-start(pred[512,512]{0,1:T(8,128)(4,1)} %iota_compare_fusion.1) | copy-start | bytes 786436
  280.1 1.5 copy-start.10
  286.9 1.6 copy-start.6
  288.5 4.9 %copy-start.8 = (f32[8,128,512]{2,1,0:T(8,128)S(1)}, f32[8,128,512]{2,1,0:T(8,128)}, u32[]{:S(2)}) copy-start(f32[8,128,512]{2,1,0:T(8,128)} %fusion.35) | copy-start | bytes 6291460
  288.5 6.5 %copy-start.13 = (f32[8,512,512]{1,2,0:T(8,128)S(1)}, f32[8,512,512]{1,2,0:T(8,128)}, u32[]{:S(2)}) copy-start(f32[8,512,512]{1,2,0:T(8,128)} %get-tuple-element.116) | copy-start | bytes 25165828
  303.5 10.4 %copy-start.4 = (bf16[1,512,2048]{2,1,0:T(8,128)(2,1)S(1)}, bf16[1,512,2048]{2,1,0:T(8,128)(2,1)}, u32[]{:S(2)}) copy-start(bf16[1,512,2048]{2,1,0:T(8,128)(2,1)} %param.9) | copy-start | bytes 6291460
Sparse Core Ops, SparseCore 0:
  8.9 59.4 all-gather.5
  69.9 103.9 all-gather.3
  175.5 56.7 all-gather.7
  303.6 10.2 reduce-scatter.1
where the time goes:
time: 324 us; the launch traced here: 323 us
  waiting for transfers between devices  200 us (62%)
  matrix products  40.6 us (13%)
  starting transfers between devices  27.6 us (9%)
  local copies, waits for them, and re-layouts  23 us (7%)
  other arithmetic  17.9 us (6%)
  between operations  14.1 us (4%)
    all_gather x1, waiting for transfers between devices, shards(): lax.all_gather(w_keyvalue, 'wloop', axis=0, tiled=True)  95.2 us
    all_gather x1, waiting for transfers between devices, shards(): lax.all_gather(w_query, 'wloop', axis=0, tiled=True)  50.1 us
    ppermute x8, waiting for transfers between devices, shifted(): lax.ppermute(value, axis, [(source, source + steps) for source in range(i...  42.4 us
    ppermute x8, starting transfers between devices, shifted(): lax.ppermute(value, axis, [(source, source + steps) for source in range(i...  27.5 us
    unnamed x34, local copies, waits for them, and re-layouts  14.3 us
    reduce_scatter x1, waiting for transfers between devices, shards(): lax.psum_scatter(partial_out.astype(jnp.bfloat16), 'heads', scatter_dimen...  10.4 us
    dot_general x1, matrix products, shards(): jnp.einsum('td,dje->jte', columns, lax.all_gather(w_keyvalue, 'wloop', ax...  6.94 us
  transfers between devices with their start and end apart: 12, of which 6 were waited for; matrix products, arithmetic and copies ran while one was open for 22% of the time, Pallas kernels for 0%

commit v1 on v0

--- a/solution.py
+++ b/solution.py
@@ -75,7 +75,9 @@
         jnp.bfloat16
     )
     keep = (1 - resets[:, 0]).astype(jnp.float32)
-    climb = jnp.cumsum(log_retain, axis=-1)
+    upto = jnp.triu(jnp.ones((span, span), jnp.float32))
+    climb = jnp.dot(log_retain.reshape(trajs * heads_here, span), upto, precision=lax.Precision.HIGHEST)
+    climb = climb.reshape(trajs, heads_here, span)
     whole = climb[:, :, -1]
     factor = jnp.exp(whole) * keep[:, None]
     weight = jnp.exp(whole[:, :, None] - climb)

time: 324 us -> 323 us (level)
  transfers between devices with their start and end apart: 12 -> 12, of which waited for: 6 -> 6; matrix products, arithmetic and copies ran while one was open for 22% -> 21% of each run, Pallas kernels for 0% -> 0%
where the time goes in v1:
time: 323 us; the launch traced here: 322 us
  waiting for transfers between devices  199 us (62%)
  matrix products  42.7 us (13%)
  starting transfers between devices  27.9 us (9%)
  local copies, waits for them, and re-layouts  22 us (7%)
  other arithmetic  16.4 us (5%)
  between operations  14.1 us (4%)
    all_gather x1, waiting for transfers between devices, shards(): lax.all_gather(w_keyvalue, 'wloop', axis=0, tiled=True)  95.3 us
    all_gather x1, waiting for transfers between devices, shards(): lax.all_gather(w_query, 'wloop', axis=0, tiled=True)  50.7 us
    ppermute x8, waiting for transfers between devices, shifted(): lax.ppermute(value, axis, [(source, source + steps) for source in range(i...  41.3 us
    ppermute x8, starting transfers between devices, shifted(): lax.ppermute(value, axis, [(source, source + steps) for source in range(i...  27.8 us
    unnamed x34, local copies, waits for them, and re-layouts  13.6 us
    reduce_scatter x1, waiting for transfers between devices, shards(): lax.psum_scatter(partial_out.astype(jnp.bfloat16), 'heads', scatter_dimen...  10.2 us
    dot_general x1, matrix products, shards(): jnp.einsum('td,dje->jte', columns, lax.all_gather(w_keyvalue, 'wloop', ax...  6.94 us
  transfers between devices with their start and end apart: 12, of which 6 were waited for; matrix products, arithmetic and copies ran while one was open for 21% of the time, Pallas kernels for 0%

profile of v1, /device:TPU:0, one launch (start us, length us, event | category | flops | bytes accessed | tf_op | source)
XLA Modules:
  0.0 322.3 jit_solution(344072900616083198)
XLA Ops:
  6.5 0.7 all-gather.6.cloned.1.call-update
  7.3 0.0 all-gather.4.cloned.1.call-start
  7.3 5.5 %copy.46 = bf16[1024,2,1024]{2,0,1:T(8,128)(2,1)} copy(bf16[1024,2,1024]{2,1,0:T(2,128)(2,1)} %param.12) | data formatting | bytes 8388608 | tf_op args[3]
  12.8 0.0 all-gather.4.cloned.1.call-update
  12.8 0.0 all-gather.8.cloned.1.call-start
  12.9 0.7 all-gather.8.cloned.1.call-update
  13.6 0.0 reduce-scatter.2.cloned.1.call-start
  13.6 0.8 iota_compare_fusion.2
  14.4 0.5 fusion.7
  15.6 0.9 fusion.30
  16.5 0.2 slice_reduce_fusion
  16.7 0.2 multiply_reduce_fusion
  16.9 0.8 fusion.32
  17.7 50.7 %all-gather.6.cloned.1.call-done = bf16[2048,1024]{1,0:T(8,128)(2,1)} async-done(((bf16[1024,1024]{1,0:T(8,128)(2,1)}), bf16[2048,1024]{1,0:T(8,128)(2,1)}) %all-gather.6.cloned.1.call-update) | async-done | bytes 4194320 | tf_op jit(solution)/shard_map/all_gather | solution.py:55
  68.4 4.6 %fusion.18 = f32[512,1024]{1,0:T(8,128)S(1)} fusion(bf16[2048,1024]{1,0:T(8,128)(2,1)} %all-gather.6.cloned.1.call-done, bf16[1,512,2048]{2,1,0:T(8,128)(2,1)S(1)} %copy-done.4, f32[2048]{0:T(1024)S(1)} %copy-done.12, f32[512]{0:T(512)S(1)} %add_rsqrt_fusion.2), kind=kOutput, calls=%fused_computation.32 | convolution fusion | flops 2151677952 | bytes 8398848 | tf_op jit(solution)/shard_map/dot_general | solution.py:53
  73.0 0.3 multiply_bitcast_fusion.1
  73.3 1.1 copy-done.3
  74.3 0.5 copy.69
  74.8 0.6 reduce_sum.57
  75.4 0.1 copy.47
  75.5 3.2 fusion.12
  78.7 95.3 %all-gather.4.cloned.1.call-done = bf16[2048,2,1024]{2,0,1:T(8,128)(2,1)} async-done(((bf16[1024,2,1024]{2,0,1:T(8,128)(2,1)}), bf16[2048,2,1024]{2,0,1:T(8,128)(2,1)}) %all-gather.4.cloned.1.call-update) | async-done | bytes 8388624 | tf_op jit(solution)/shard_map/all_gather | solution.py:62
  174.0 6.9 %convolution_bitcast_fusion = f32[2,512,1024]{2,1,0:T(8,128)S(1)} fusion(bf16[2048,2,1024]{2,0,1:T(8,128)(2,1)} %all-gather.4.cloned.1.call-done, bf16[1,512,2048]{2,1,0:T(8,128)(2,1)S(1)} %copy-done.5, f32[2048]{0:T(1024)S(1)} %copy-done.12, f32[512]{0:T(512)S(1)} %add_rsqrt_fusion.2), kind=kOutput, calls=%fused_computation.21 | convolution fusion | flops 4299161600 | bytes 14690304 | tf_op jit(solution)/shard_map/td,dje->jte/dot_general | solution.py:59
  181.0 0.2 slice_bitcast_fusion
  181.2 0.3 multiply_bitcast_fusion
  181.5 1.5 copy-done.2
  183.0 1.2 slice.20
  184.1 1.3 copy.68
  185.4 0.5 copy.70
  185.9 0.6 reduce_sum.58
  186.5 0.1 copy.49
  186.6 1.6 mul.189
  188.2 2.0 copy.65
  190.2 3.8 %multiply_convert_fusion = (bf16[1,512,1024]{2,1,0:T(8,128)(2,1)}, f32[1,512,1024]{2,1,0:T(8,128)}) fusion(f32[1,512,1024]{2,1,0:T(8,128)S(1)} %copy.65, f32[2,512,1024]{2,1,0:T(8,128)} %copy-done.2), kind=kLoop, calls=%fused_computation.37 | loop fusion | flops 1048576 | bytes 7340032 | tf_op jit(solution)/shard_map/convert_element_type | solution.py:65
  194.0 1.9 copy.64
  195.9 4.4 %collective-permute-start.2 = (bf16[1,512,1024]{2,1,0:T(8,128)(2,1)}, bf16[1,512,1024]{2,1,0:T(8,128)(2,1)}, u32[]{:S(2)}, u32[]{:S(2)}) collective-permute-start(bf16[1,512,1024]{2,1,0:T(8,128)(2,1)} %get-tuple-element.109), channel_id=1, source_target_pairs={{0,4},{4,8},{8,12},{1,5},{5,9},{9,13},{2,6},{6,10},{10,14},{3,7},{... | collective-permute-start | bytes 3145736 | tf_op jit(solution)/shard_map/ppermute | solution.py:14
  200.3 3.5 %collective-permute-start.3 = (bf16[1,512,1024]{2,1,0:T(8,128)(2,1)}, bf16[1,512,1024]{2,1,0:T(8,128)(2,1)}, u32[]{:S(2)}, u32[]{:S(2)}) collective-permute-start(bf16[1,512,1024]{2,1,0:T(8,128)(2,1)} %slice.20), channel_id=1, source_target_pairs={{0,4},{4,8},{8,12},{1,5},{5,9},{9,13},{2,6},{6,10},{10,14},{3,7},{... | collective-permute-start | bytes 3145736 | tf_op jit(solution)/shard_map/ppermute | solution.py:14
  203.8 2.6 fusion.23
  206.4 63.9 %while.14 = (s32[]{:T(128)}, f32[1,8,128,128]{3,2,1,0:T(8,128)S(1)}, f32[1,8]{1,0:T(1,128)S(1)}, f32[1,8]{1,0:T(1,128)S(1)}, f32[1,8,128,128]{3,2,1,0:T(8,128)S(...) while((s32[]{:T(128)}, f32[1,8,128,128]{3,2,1,0:T(8,128)S(1)}, ...), condition=%wide.region_7.8_spmd.clone, body=%wide.region_6.7_spmd.clone.sunk | while | flops 655403 | bytes 3146168 | solution.py:104
  206.4 0.8 fusion.66
  207.2 2.5 collective-permute-start
  209.8 1.9 collective-permute-start.1
  211.7 38.5 %collective-permute-done.1 = bf16[1,8]{1,0:T(2,128)(2,1)S(1)} collective-permute-done((bf16[1,8]{1,0:T(2,128)(2,1)S(1)}, bf16[1,8]{1,0:T(2,128)(2,1)S(1)}, u32[]{:S(2)}, u32[]{:S(2)}) %collective-permute-start.1) | collective-permute-done | bytes 48 | tf_op jit(solution)/shard_map/while/body/eval_jaxpr/ppermute | solution.py:14
  250.2 0.8 fusion.66
  251.0 4.3 %collective-permute-start = (bf16[1,8,128,128]{3,2,1,0:T(8,128)(2,1)}, bf16[1,8,128,128]{3,2,1,0:T(8,128)(2,1)S(1)}, u32[]{:S(2)}, u32[]{:S(2)}) collective-permute-start(bf16[1,8,128,128]{3,2,1,0:T(8,128)(2,1)} %fusion.66), channel_id=1, source_target_pairs={{0,4},{4,8},{8,12},{1,5},{5,9},{9,13},{2,6},{6,10},{10,14},{3,7},{... | collective-permute-start | bytes 786440 | tf_op jit(solution)/shard_map/while/body/eval_jaxpr/ppermute | solution.py:14
  255.4 3.4 %collective-permute-start.1 = (bf16[1,8]{1,0:T(2,128)(2,1)S(1)}, bf16[1,8]{1,0:T(2,128)(2,1)S(1)}, u32[]{:S(2)}, u32[]{:S(2)}) collective-permute-start(bf16[1,8]{1,0:T(2,128)(2,1)S(1)} %fusion.67), channel_id=1, source_target_pairs={{0,4},{4,8},{8,12},{1,5},{5,9},{9,13},{2,6},{6,10},{10,14},{3,7},{... | collective-permute-start | bytes 56 | tf_op jit(solution)/shard_map/while/body/eval_jaxpr/ppermute | solution.py:14
  258.8 1.5 collective-permute-done.1
  260.4 0.8 fusion.66
  261.2 4.3 %collective-permute-start = (bf16[1,8,128,128]{3,2,1,0:T(8,128)(2,1)}, bf16[1,8,128,128]{3,2,1,0:T(8,128)(2,1)S(1)}, u32[]{:S(2)}, u32[]{:S(2)}) collective-permute-start(bf16[1,8,128,128]{3,2,1,0:T(8,128)(2,1)} %fusion.66), channel_id=1, source_target_pairs={{0,4},{4,8},{8,12},{1,5},{5,9},{9,13},{2,6},{6,10},{10,14},{3,7},{... | collective-permute-start | bytes 786440 | tf_op jit(solution)/shard_map/while/body/eval_jaxpr/ppermute | solution.py:14
  265.6 3.4 %collective-permute-start.1 = (bf16[1,8]{1,0:T(2,128)(2,1)S(1)}, bf16[1,8]{1,0:T(2,128)(2,1)S(1)}, u32[]{:S(2)}, u32[]{:S(2)}) collective-permute-start(bf16[1,8]{1,0:T(2,128)(2,1)S(1)} %fusion.67), channel_id=1, source_target_pairs={{0,4},{4,8},{8,12},{1,5},{5,9},{9,13},{2,6},{6,10},{10,14},{3,7},{... | collective-permute-start | bytes 56 | tf_op jit(solution)/shard_map/while/body/eval_jaxpr/ppermute | solution.py:14
  269.0 1.3 collective-permute-done.1
  270.3 3.7 %fusion.37 = f32[8,128,512]{2,1,0:T(8,128)} fusion(bf16[512,8,128]{2,0,1:T(8,128)(2,1)} %fusion.12, f32[1,8,128,128]{3,2,1,0:T(8,128)S(1)} %get-tuple-element.67, f32[]{:T(128)} %bitcast.15), kind=kOutput, calls=%fused_computation.54 | convolution fusion | flops 805437440 | bytes 3670020 | tf_op jit(solution)/shard_map/bthd,bhde->bthe/dot_general | solution.py:112
  274.0 5.5 %fusion.5 = (f32[8,512]{1,0:T(8,128)S(1)}, f32[8,512,512]{1,2,0:T(8,128)}) fusion(pred[512,512]{0,1:T(8,128)(4,1)S(1)} %copy-done.10, bf16[512,8,128]{2,0,1:T(8,128)(2,1)S(1)} %copy-done.8, f32[512,8,128]{0,2,1:T(8,128)S(1)} %bitcast.102, f32[512,8]{0,1:T(8,128)S(1)} %add_rsqrt_fusion), kind=kOutput, calls=%fused_computation.11 | convolution fusion | flops 544206848 | bytes 11829248 | tf_op jit(solution)/shard_map/bihd,bjhd->bhij/dot_general | solution.py:23
  279.5 1.5 copy.71
  281.1 5.3 %fusion.6 = (f32[8,512]{1,0:T(8,128)S(1)}, f32[8,512,512]{1,2,0:T(8,128)}) fusion(pred[512,512]{0,1:T(8,128)(4,1)S(1)} %copy-done.11, bf16[512,8,128]{2,0,1:T(8,128)(2,1)S(1)} %copy-done.8, bf16[512,8,128]{2,1,0:T(8,128)(2,1)S(1)} %bitcast.109), kind=kOutput, calls=%fused_computation.12 | convolution fusion | flops 543158272 | bytes 10764288 | tf_op jit(solution)/shard_map/bihd,bjhd->bhij/dot_general | solution.py:27
  286.3 1.6 copy.66
  287.9 4.8 %fusion.10 = f32[8,128,512]{2,1,0:T(8,128)S(1)} fusion(f32[8,512,512]{1,2,0:T(8,128)} %get-tuple-element.115, f32[8,512]{1,0:T(8,128)S(1)} %add.84, pred[512,512]{0,1:T(8,128)(4,1)S(1)} %copy-done.10, bf16[512,8,128]{2,1,0:T(8,128)(2,1)S(1)} %bitcast.107), kind=kOutput, calls=%fused_computation.18 | convolution fusion | flops 545259520 | bytes 11812864 | tf_op jit(solution)/shard_map/bhij,bjhd->bihd/dot_general | solution.py:38
  292.8 1.6 copy-done.13
  294.4 2.5 fusion.15
  296.9 0.0 all-gather.8.cloned.1.call-done
  297.0 5.9 %convolution_convert_fusion = bf16[512,2048]{1,0:T(8,128)(2,1)} fusion(bf16[512,1024]{0,1:T(8,128)(2,1)S(1)} %bitcast.114, bf16[1024,2048]{1,0:T(8,128)(2,1)} %all-gather.8.cloned.1.call-done), kind=kOutput, calls=%fused_computation.20 | convolution fusion | flops 2148532224 | bytes 7340032 | tf_op jit(solution)/shard_map/dot_general | solution.py:128
  302.9 0.0 reduce-scatter.2.cloned.1.call-update
  302.9 10.2 %reduce-scatter.2.cloned.1.call-done = bf16[512,1024]{1,0:T(8,128)(2,1)} async-done(((bf16[512,2048]{1,0:T(8,128)(2,1)}), bf16[512,1024]{1,0:T(8,128)(2,1)}) %reduce-scatter.2.cloned.1.call-update) | async-done | bytes 1048592 | tf_op jit(solution)/shard_map/reduce_scatter | solution.py:133
  313.2 2.6 fusion.26
  (49 shorter events, 0.3 us)
Async XLA Ops:
  6.5 9.0 %copy-start = (f32[1,8,512]{2,1,0:T(8,128)S(1)}, f32[1,8,512]{2,1,0:T(8,128)}, u32[]{:S(2)}) copy-start(f32[1,8,512]{2,1,0:T(8,128)} %param.14) | copy-start | bytes 49156
  6.5 61.9 %all-gather.6.cloned.1.call-start = ((), (), s32[]{:S(2)}) async-start(), calls=%async_computation.2 | async-start | bytes 6291456 | tf_op jit(solution)/shard_map/all_gather | solution.py:55
  7.3 166.8 %all-gather.4.cloned.1.call-start = ((), (), s32[]{:S(2)}) async-start(), calls=%async_computation.1 | async-start | bytes 12582912 | tf_op jit(solution)/shard_map/all_gather | solution.py:62
  12.8 1.6 copy-start.4
  12.8 284.2 %all-gather.8.cloned.1.call-start = ((), (), s32[]{:S(2)}) async-start(), calls=%async_computation.3 | async-start | bytes 6291456 | tf_op jit(solution)/shard_map/all_gather | solution.py:130
  13.5 54.9 %copy-start.12 = (f32[2048]{0:T(1024)S(1)}, f32[2048]{0:T(1024)}, u32[]{:S(2)}) copy-start(f32[2048]{0:T(1024)} %param.10) | copy-start | bytes 24580
  13.6 299.6 %reduce-scatter.2.cloned.1.call-start = ((), (), s32[]{:S(2)}) async-start(), calls=%async_computation.4 | async-start | bytes 3145728 | tf_op jit(solution)/shard_map/reduce_scatter | solution.py:133
  73.0 1.3 copy-start.3
  75.4 98.6 %copy-start.5 = (bf16[1,512,2048]{2,1,0:T(8,128)(2,1)S(1)}, bf16[1,512,2048]{2,1,0:T(8,128)(2,1)}, u32[]{:S(2)}) copy-start(bf16[1,512,2048]{2,1,0:T(8,128)(2,1)} %param.9) | copy-start | bytes 6291460
  181.0 2.0 copy-start.2
  195.9 83.6 %collective-permute-start.2 = (bf16[1,512,1024]{2,1,0:T(8,128)(2,1)}, bf16[1,512,1024]{2,1,0:T(8,128)(2,1)}, u32[]{:S(2)}, u32[]{:S(2)}) collective-permute-start(bf16[1,512,1024]{2,1,0:T(8,128)(2,1)} %get-tuple-element.109), channel_id=1, source_target_pairs={{0,4},{4,8},{8,12},{1,5},{5,9},{9,13},{2,6},{6,10},{10,14},{3,7},{... | collective-permute-start | bytes 3145736 | tf_op jit(solution)/shard_map/ppermute | solution.py:14
  200.3 86.0 %collective-permute-start.3 = (bf16[1,512,1024]{2,1,0:T(8,128)(2,1)}, bf16[1,512,1024]{2,1,0:T(8,128)(2,1)}, u32[]{:S(2)}, u32[]{:S(2)}) collective-permute-start(bf16[1,512,1024]{2,1,0:T(8,128)(2,1)} %slice.20), channel_id=1, source_target_pairs={{0,4},{4,8},{8,12},{1,5},{5,9},{9,13},{2,6},{6,10},{10,14},{3,7},{... | collective-permute-start | bytes 3145736 | tf_op jit(solution)/shard_map/ppermute | solution.py:14
  207.2 43.0 %collective-permute-start = (bf16[1,8,128,128]{3,2,1,0:T(8,128)(2,1)}, bf16[1,8,128,128]{3,2,1,0:T(8,128)(2,1)S(1)}, u32[]{:S(2)}, u32[]{:S(2)}) collective-permute-start(bf16[1,8,128,128]{3,2,1,0:T(8,128)(2,1)} %fusion.66), channel_id=1, source_target_pairs={{0,4},{4,8},{8,12},{1,5},{5,9},{9,13},{2,6},{6,10},{10,14},{3,7},{... | collective-permute-start | bytes 786440 | tf_op jit(solution)/shard_map/while/body/eval_jaxpr/ppermute | solution.py:14
  209.8 40.4 %collective-permute-start.1 = (bf16[1,8]{1,0:T(2,128)(2,1)S(1)}, bf16[1,8]{1,0:T(2,128)(2,1)S(1)}, u32[]{:S(2)}, u32[]{:S(2)}) collective-permute-start(bf16[1,8]{1,0:T(2,128)(2,1)S(1)} %fusion.67), channel_id=1, source_target_pairs={{0,4},{4,8},{8,12},{1,5},{5,9},{9,13},{2,6},{6,10},{10,14},{3,7},{... | collective-permute-start | bytes 56 | tf_op jit(solution)/shard_map/while/body/eval_jaxpr/ppermute | solution.py:14
  251.0 9.3 %collective-permute-start = (bf16[1,8,128,128]{3,2,1,0:T(8,128)(2,1)}, bf16[1,8,128,128]{3,2,1,0:T(8,128)(2,1)S(1)}, u32[]{:S(2)}, u32[]{:S(2)}) collective-permute-start(bf16[1,8,128,128]{3,2,1,0:T(8,128)(2,1)} %fusion.66), channel_id=1, source_target_pairs={{0,4},{4,8},{8,12},{1,5},{5,9},{9,13},{2,6},{6,10},{10,14},{3,7},{... | collective-permute-start | bytes 786440 | tf_op jit(solution)/shard_map/while/body/eval_jaxpr/ppermute | solution.py:14
  255.4 4.9 %collective-permute-start.1 = (bf16[1,8]{1,0:T(2,128)(2,1)S(1)}, bf16[1,8]{1,0:T(2,128)(2,1)S(1)}, u32[]{:S(2)}, u32[]{:S(2)}) collective-permute-start(bf16[1,8]{1,0:T(2,128)(2,1)S(1)} %fusion.67), channel_id=1, source_target_pairs={{0,4},{4,8},{8,12},{1,5},{5,9},{9,13},{2,6},{6,10},{10,14},{3,7},{... | collective-permute-start | bytes 56 | tf_op jit(solution)/shard_map/while/body/eval_jaxpr/ppermute | solution.py:14
  261.2 9.0 %collective-permute-start = (bf16[1,8,128,128]{3,2,1,0:T(8,128)(2,1)}, bf16[1,8,128,128]{3,2,1,0:T(8,128)(2,1)S(1)}, u32[]{:S(2)}, u32[]{:S(2)}) collective-permute-start(bf16[1,8,128,128]{3,2,1,0:T(8,128)(2,1)} %fusion.66), channel_id=1, source_target_pairs={{0,4},{4,8},{8,12},{1,5},{5,9},{9,13},{2,6},{6,10},{10,14},{3,7},{... | collective-permute-start | bytes 786440 | tf_op jit(solution)/shard_map/while/body/eval_jaxpr/ppermute | solution.py:14
  265.6 4.7 %collective-permute-start.1 = (bf16[1,8]{1,0:T(2,128)(2,1)S(1)}, bf16[1,8]{1,0:T(2,128)(2,1)S(1)}, u32[]{:S(2)}, u32[]{:S(2)}) collective-permute-start(bf16[1,8]{1,0:T(2,128)(2,1)S(1)} %fusion.67), channel_id=1, source_target_pairs={{0,4},{4,8},{8,12},{1,5},{5,9},{9,13},{2,6},{6,10},{10,14},{3,7},{... | collective-permute-start | bytes 56 | tf_op jit(solution)/shard_map/while/body/eval_jaxpr/ppermute | solution.py:14
  270.3 3.7 %copy-start.8 = (bf16[512,8,128]{2,0,1:T(8,128)(2,1)S(1)}, bf16[512,8,128]{2,0,1:T(8,128)(2,1)}, u32[]{:S(2)}) copy-start(bf16[512,8,128]{2,0,1:T(8,128)(2,1)} %fusion.12) | copy-start | bytes 3145732
  270.3 3.7 %copy-start.10 = (pred[512,512]{0,1:T(8,128)(4,1)S(1)}, pred[512,512]{0,1:T(8,128)(4,1)}, u32[]{:S(2)}) copy-start(pred[512,512]{0,1:T(8,128)(4,1)} %iota_compare_fusion.2) | copy-start | bytes 786436
  279.5 1.5 copy-start.11
  286.3 1.6 copy-start.7
  287.9 4.9 %copy-start.9 = (f32[8,128,512]{2,1,0:T(8,128)S(1)}, f32[8,128,512]{2,1,0:T(8,128)}, u32[]{:S(2)}) copy-start(f32[8,128,512]{2,1,0:T(8,128)} %fusion.37) | copy-start | bytes 6291460
  287.9 6.5 %copy-start.13 = (f32[8,512,512]{1,2,0:T(8,128)S(1)}, f32[8,512,512]{1,2,0:T(8,128)}, u32[]{:S(2)}) copy-start(f32[8,512,512]{1,2,0:T(8,128)} %get-tuple-element.117) | copy-start | bytes 25165828
  302.9 10.3 %copy-start.6 = (bf16[1,512,2048]{2,1,0:T(8,128)(2,1)S(1)}, bf16[1,512,2048]{2,1,0:T(8,128)(2,1)}, u32[]{:S(2)}) copy-start(bf16[1,512,2048]{2,1,0:T(8,128)(2,1)} %param.9) | copy-start | bytes 6291460
  302.9 12.8 %copy-start.1 = (f32[1,8,512]{2,1,0:T(8,128)S(1)}, f32[1,8,512]{2,1,0:T(8,128)}, u32[]{:S(2)}) copy-start(f32[1,8,512]{2,1,0:T(8,128)} %param.14) | copy-start | bytes 49156
Sparse Core Ops, SparseCore 0:
  8.9 59.4 all-gather.5
  70.0 103.9 all-gather.3
  175.6 56.7 all-gather.7
  303.0 10.0 reduce-scatter.1

commit v2 on v0

v2 whole, which is shorter than its diff:
```python
import functools
import math

import jax
import jax.numpy as jnp
from jax import lax
from jax.experimental import pallas as pl
from jax.experimental.pallas import tpu as pltpu
from jax.sharding import PartitionSpec as P

SCORE_SCALE = 2.0
F32, BF16 = jnp.float32, jnp.bfloat16


def around(value, axis):
    count = lax.axis_size(axis)
    return lax.ppermute(value, axis, [(i, (i + 1) % count) for i in range(count)])


def shifted(value, axis):
    count = lax.axis_size(axis)
    return lax.ppermute(value, axis, [(i, i + 1) for i in range(count - 1)])


def rms_rows(values, eps):
    return values * lax.rsqrt(jnp.mean(values * values, axis=-1, keepdims=True) + eps)


def other_half(block):
    group = lax.axis_index("groups")
    rows = block.shape[0] // 2
    first = around(lax.dynamic_slice_in_dim(block, group * rows, rows, 0), "wloop")
    second = around(first, "groups")
    return jnp.concatenate(
        [jnp.where(group == 0, first, second), jnp.where(group == 0, second, first)], axis=0
    )


def window_kernel(scale, allow_ref, q_ref, k_ref, v_ref, out_ref):
    span = q_ref.shape[0]
    query = q_ref[...]
    product = functools.partial(
        lax.dot_general, dimension_numbers=(((1,), (1,)), ((), ())), preferred_element_type=F32
    )
    prior = product(query, k_ref[:span, :])
    own = product(query, k_ref[span:, :])
    lower = lax.broadcasted_iota(jnp.int32, (span, span), 1) <= lax.broadcasted_iota(
        jnp.int32, (span, span), 0
    )
    weight = jnp.exp(jnp.where(lower, own, prior) * scale)
    own_w = jnp.where(lower, weight, 0.0)
    prior_w = jnp.where(lower, 0.0, weight) * allow_ref[0, 0]
    total = jnp.sum(own_w + prior_w, axis=-1, keepdims=True)
    mixed = jnp.dot(own_w.astype(BF16), v_ref[span:, :], preferred_element_type=F32)
    mixed += jnp.dot(prior_w.astype(BF16), v_ref[:span, :], preferred_element_type=F32)
    out_ref[...] = mixed / total


def window_mix(queries, keys, values, allow, head_dim, scale):
    span, inner = queries.shape
    return pl.pallas_call(
        functools.partial(window_kernel, scale),
        grid=(inner // head_dim,),
        in_specs=[
            pl.BlockSpec(memory_space=pltpu.SMEM),
            pl.BlockSpec((span, head_dim), lambda h: (0, h)),
            pl.BlockSpec((2 * span, head_dim), lambda h: (0, h)),
            pl.BlockSpec((2 * span, head_dim), lambda h: (0, h)),
        ],
        out_specs=pl.BlockSpec((span, head_dim), lambda h: (0, h)),
        out_shape=jax.ShapeDtypeStruct((span, inner), F32),
        compiler_params=pltpu.CompilerParams(vmem_limit_bytes=32 << 20),
        cost_estimate=pl.CostEstimate(
            flops=8 * span * span * inner, bytes_accessed=14 * span * inner, transcendentals=0
        ),
    )(allow, queries, keys, values)


def read_kernel(q_ref, state_ref, decay_ref, window_ref, out_ref):
    head = pl.program_id(0)
    decay = decay_ref[...]
    column = lax.broadcasted_iota(jnp.int32, decay.shape, 1)
    mine = jnp.sum(jnp.where(column == head, decay, 0.0), axis=-1, keepdims=True)
    read = jnp.dot(q_ref[...], state_ref[0], preferred_element_type=F32)
    out_ref[...] = (window_ref[...] + mine * read).astype(BF16)


def add_read(queries, states, decay, window):
    span, inner = queries.shape
    heads, head_dim = states.shape[:2]
    block = pl.BlockSpec((span, head_dim), lambda h: (0, h))
    return pl.pallas_call(
        read_kernel,
        grid=(heads,),
        in_specs=[
            block,
            pl.BlockSpec((1, head_dim, head_dim), lambda h: (h, 0, 0)),
            pl.BlockSpec((span, heads), lambda h: (0, 0)),
            block,
        ],
        out_specs=block,
        out_shape=jax.ShapeDtypeStruct((span, inner), BF16),
    )(queries, states, decay, window)


def shards(activations, norm_gain, w_query, w_keyvalue, w_output, log_retain, resets):
    trajs, span, width = activations.shape
    heads_here = log_retain.shape[1]
    inner_here = w_query.shape[1]
    head_dim = inner_here // heads_here
    scale = SCORE_SCALE / math.sqrt(head_dim)
    side, core, seg = lax.axis_index("wloop"), lax.axis_index("heads"), lax.axis_index("seq")
    segments = lax.axis_size("seq")
    paired = lax.axis_size("wloop") == 2 and lax.axis_size("groups") == 2
    acts = activations.reshape(span, width)

    def whole_rows(block):
        if not paired:
            return lax.all_gather(block, "wloop", axis=0, tiled=True)
        other = other_half(block)
        return jnp.concatenate(
            [jnp.where(side == 0, block, other), jnp.where(side == 0, other, block)], axis=0
        )

    normed = (rms_rows(acts.astype(F32), 1e-05) * norm_gain).astype(BF16)
    both = jnp.concatenate([shifted(normed, "seq"), normed], axis=0)
    w_key, w_value = w_keyvalue[:, 0, :], w_keyvalue[:, 1, :]
    w_key, w_value, w_query = whole_rows(w_key), whole_rows(w_value), whole_rows(w_query)

    def headed(raw):
        return rms_rows(raw.reshape(-1, heads_here, head_dim), 1e-06).astype(BF16)

    keys = headed(jnp.dot(both, w_key, preferred_element_type=F32)).reshape(2 * span, inner_here)
    values = jnp.dot(both, w_value, preferred_element_type=F32).astype(BF16)
    queries = headed(jnp.dot(normed, w_query, preferred_element_type=F32)).reshape(span, inner_here)

    keep = (1 - resets[0, 0]).astype(F32)
    upto = jnp.triu(jnp.ones((span, span), F32))
    climb = jnp.dot(log_retain[0], upto, precision=lax.Precision.HIGHEST)
    whole = climb[:, -1]
    factor = jnp.exp(whole) * keep
    weight = jnp.exp(whole[:, None] - climb)
    faded = (
        keys[span:].reshape(span, heads_here, head_dim).astype(F32) * weight.T[:, :, None]
    ).astype(BF16)
    local_state = jnp.einsum(
        "thd,the->hde",
        faded,
        values[span:].reshape(span, heads_here, head_dim),
        preferred_element_type=F32,
    )
    local_mass = jnp.sum(weight * weight, axis=-1)
    states = lax.all_gather(local_state.astype(BF16), "seq")
    small = lax.all_gather(jnp.stack([factor, local_mass]), "seq")
    state, mass = jnp.zeros_like(local_state), jnp.zeros_like(local_mass)
    for j in range(segments - 1):
        fac, add_mass = small[j, 0], small[j, 1]
        past = j < seg
        state = jnp.where(past, fac[:, None, None] * state + states[j].astype(F32), state)
        mass = jnp.where(past, fac * fac * mass + add_mass, mass)
    entering = (state * keep).astype(BF16)
    decay = jnp.exp(climb) / jnp.sqrt(head_dim * (1.0 + mass * keep))[:, None]
    allow = ((keep > 0.5) & (seg > 0)).astype(F32).reshape(1, 1)
    window = window_mix(queries, keys, values, allow, head_dim, scale)
    attended = add_read(queries, entering, decay.T, window)

    if paired:
        other = other_half(w_output)
        mine = jnp.where(side == core, w_output, other)
        theirs = jnp.where(side == core, other, w_output)
    else:
        full = lax.all_gather(w_output, "wloop", axis=1, tiled=True)
        share = width // 2
        mine = lax.dynamic_slice_in_dim(full, core * share, share, 1)
        theirs = lax.dynamic_slice_in_dim(full, (1 - core) * share, share, 1)
    sent = around(jnp.dot(attended, theirs, preferred_element_type=F32).astype(BF16), "heads")
    share = mine.shape[1]
    summed = jnp.dot(attended, mine, preferred_element_type=F32) + sent.astype(F32)
    residual = lax.dynamic_slice_in_dim(acts, core * share, share, 1)
    return (residual.astype(F32) + summed).astype(BF16).reshape(trajs, span, share)


def solution(mesh):
    placed = (
        P(("groups", "wloop"), "seq", None),
        P(),
        P("wloop", "heads"),
        P("wloop", None, "heads"),
        P("heads", "wloop"),
        P(("groups", "wloop"), "heads", "seq"),
        P(("groups", "wloop"), "seq"),
    )
    return jax.shard_map(
        shards,
        mesh=mesh,
        in_specs=placed,
        out_specs=P(("groups", "wloop"), "seq", "heads"),
        check_vma=False,
    )
```

time: 324 us -> 211 us (0.65)
  waiting for transfers between devices: 200 us -> 25.4 us
  blocking collectives: 0 us -> 40.7 us
  local copies, waits for them, and re-layouts: 23 us -> 41.5 us
  Pallas kernels: 0 us -> 17 us
  starting transfers between devices: 27.6 us -> 15 us
  matrix products: 40.6 us -> 30.3 us
  other arithmetic: 17.9 us -> 25.8 us
    all_gather x3 -> x1, waiting for transfers between devices: 145 us -> 0.01 us  [shards(): states = lax.all_gather(local_state.astype(BF16), 'seq')]
    all_gather x0 -> x1, blocking collectives: none -> 40.7 us  [shards(): small = lax.all_gather(jnp.stack([factor, local_mass]), 'seq')]
    ppermute x8 -> x10, waiting for transfers between devices: 42.4 us -> 25.4 us  [the longest x9 25.4 us: around(): lax.ppermute(value, axis, [(i, (i + 1) % count) for i in range(count)])]
    pallas_call x0 -> x2, Pallas kernels: none -> 17 us  [the longest x1 10.4 us: window_mix(): pl.pallas_call(functools.partial(window_kernel, scale), grid=(inner // he...]
    ppermute x8 -> x10, starting transfers between devices: 27.5 us -> 15 us  [the longest x9 10.2 us: around(): lax.ppermute(value, axis, [(i, (i + 1) % count) for i in range(count)])]
    select_n x0 -> x7, other arithmetic: none -> 11.9 us  [the longest x4 7.54 us: other_half(): jnp.where(group == 0, first, second)]
    dot_general x0 -> x2, local copies, waits for them, and re-layouts: none -> 11.9 us  [the longest x1 6.5 us: shards(): jnp.dot(normed, w_query, preferred_element_type=F32)]
    reduce_scatter x1 -> x0, waiting for transfers between devices: 10.4 us -> none  [shards(): lax.psum_scatter(partial_out.astype(jnp.bfloat16), 'heads', scatter_dimen...]
  transfers between devices with their start and end apart: 12 -> 11, of which waited for: 6 -> 3; matrix products, arithmetic and copies ran while one was open for 22% -> 38% of each run, Pallas kernels for 0% -> 5%
where the time goes in v2:
time: 211 us; the launch traced here: 210 us
  local copies, waits for them, and re-layouts  41.5 us (20%)
  blocking collectives  40.7 us (19%)
  matrix products  30.3 us (14%)
  other arithmetic  25.8 us (12%)
  waiting for transfers between devices  25.4 us (12%)
  Pallas kernels  17 us (8%)
  starting transfers between devices  15 us (7%)
  between operations  14.5 us (7%)
    all_gather x1, blocking collectives, shards(): small = lax.all_gather(jnp.stack([factor, local_mass]), 'seq')  40.7 us
    ppermute x9, waiting for transfers between devices, around(): lax.ppermute(value, axis, [(i, (i + 1) % count) for i in range(count)])  25.4 us
    pallas_call x1, Pallas kernels, window_mix(): pl.pallas_call(functools.partial(window_kernel, scale), grid=(inner // he...  10.4 us
    ppermute x9, starting transfers between devices, around(): lax.ppermute(value, axis, [(i, (i + 1) % count) for i in range(count)])  10.2 us
    slice x1, local copies, waits for them, and re-layouts, shards(): w_key, w_value = (w_keyvalue[:, 0, :], w_keyvalue[:, 1, :])  9.08 us
    mul x2, local copies, waits for them, and re-layouts, rms_rows(): values * lax.rsqrt(jnp.mean(values * values, axis=-1, keepdims=True) + eps)  8 us
    select_n x4, other arithmetic, other_half(): jnp.where(group == 0, first, second)  7.54 us
    convert_element_type x2, other arithmetic, headed(): return rms_rows(raw.reshape(-1, heads_here, head_dim), 1e-06).astype(BF16)  7.03 us
  transfers between devices with their start and end apart: 11, of which 3 were waited for; matrix products, arithmetic and copies ran while one was open for 38% of the time, Pallas kernels for 5%

profile of v2, /device:TPU:0, one launch (start us, length us, event | category | flops | bytes accessed | tf_op | source)
XLA Modules:
  0.0 210.2 jit_solution(4029162599276868974)
XLA Ops:
  6.5 1.3 constant_dynamic-slice_fusion.1
  7.8 3.0 %collective-permute-start = (bf16[512,1024]{1,0:T(8,128)(2,1)S(1)}, bf16[512,1024]{1,0:T(8,128)(2,1)}, u32[]{:S(2)}, u32[]{:S(2)}) collective-permute-start(bf16[512,1024]{1,0:T(8,128)(2,1)S(1)} %constant_dynamic-slice_fusion.1), channel_id=1, source_target_pairs={{0,2},{2,0},{1,3},{3,1},{4,6},{6,4},{5,7},{7,5},{8,10},{10,8},{9,1... | collective-permute-start | bytes 3145736 | tf_op jit(solution)/shard_map/ppermute | solution.py:17
  10.9 9.1 %fusion.67 = (bf16[1024,1,1024]{2,1,0:T(2,128)(2,1)S(1)}, bf16[1024,1,1024]{2,1,0:T(2,128)(2,1)S(1)}) fusion(bf16[1024,2,1024]{2,1,0:T(2,128)(2,1)} %param.10), kind=kLoop, calls=%fused_computation.116 | loop fusion | bytes 8388608 | tf_op jit(solution)/shard_map/slice | solution.py:127
  20.0 0.8 copy.47
  20.8 0.0 copy-start.8
  20.8 0.0 copy-start.17
  20.8 1.0 dynamic-slice_bitcast_fusion.1
  21.9 0.0 collective-permute-start.3
  21.9 2.0 copy-done.8
  23.9 0.5 fusion.2
  24.4 0.5 fusion.4
  25.0 4.8 %collective-permute-start.2 = (bf16[512,2048]{1,0:T(8,128)(2,1)S(1)}, bf16[512,2048]{1,0:T(8,128)(2,1)}, u32[]{:S(2)}, u32[]{:S(2)}) collective-permute-start(bf16[512,2048]{1,0:T(8,128)(2,1)S(1)} %fusion.4), channel_id=1, source_target_pairs={{0,4},{4,8},{8,12},{1,5},{5,9},{9,13},{2,6},{6,10},{10,14},{3,7},{... | collective-permute-start | bytes 6291464 | tf_op jit(solution)/shard_map/ppermute | solution.py:22
  29.8 0.8 copy.48
  30.6 0.0 copy-start.14
  30.7 1.2 dynamic-slice_bitcast_fusion
  31.8 0.5 collective-permute-start.5
  32.4 0.3 copy-done.14
  32.6 1.0 constant_dynamic-slice_fusion
  33.7 1.2 collective-permute-start.7
  35.6 0.9 fusion.44
  36.5 0.2 multiply_reduce_fusion.3
  36.7 0.0 collective-permute-done
  36.7 1.6 collective-permute-start.1
  38.3 0.2 multiply_reduce_fusion.2
  38.5 40.7 %all-gather.2 = f32[4,2,8]{2,1,0:T(2,128)S(1)} all-gather(f32[1,2,8]{2,1,0:T(2,128)S(1)} %maximum_bitcast_fusion.1), channel_id=2, replica_groups=mesh['groups'=2,'seq'=4,'wloop'=2,'heads'=2] {'seq'}, dimensions={0}, use_global_device_ids=true | all-gather | bytes 320 | tf_op jit(solution)/shard_map/all_gather | solution.py:154
  79.3 0.1 fusion.68
  79.4 0.1 copy.41
  79.5 0.7 broadcast_divide_fusion.decay_ref
  80.3 0.0 collective-permute-done.3
  80.3 1.5 collective-permute-start.4
  81.8 0.0 collective-permute-done.5
  81.8 0.5 collective-permute-start.6
  82.3 19.2 %collective-permute-done.7 = bf16[512,1024]{1,0:T(8,128)(2,1)} collective-permute-done((bf16[512,1024]{1,0:T(8,128)(2,1)}, bf16[512,1024]{1,0:T(8,128)(2,1)}, u32[]{:S(2)}, u32[]{:S(2)}) %collective-permute-start.7) | collective-permute-done | bytes 1048608 | tf_op jit(solution)/shard_map/ppermute | solution.py:17
  101.5 1.8 collective-permute-start.8
  103.3 1.7 broadcast_select_fusion.9
  105.0 1.2 broadcast_select_fusion.1
  106.2 2.4 %maximum_bitcast_fusion = bf16[1024,2048]{0,1:T(8,128)(2,1)} fusion(bf16[1024,1024]{1,0:T(8,128)(2,1)S(1)} %get-tuple-element.14, bf16[1024,1024]{1,0:T(8,128)(2,1)S(1)} %get-tuple-element.13), kind=kLoop, calls=%fused_computation.9 | loop fusion | flops 8388608 | bytes 8388608 | tf_op jit(solution)/shard_map/dot_general | solution.py:135
  108.6 6.5 %copy.35 = bf16[1024,2048]{1,0:T(8,128)(2,1)} copy(bf16[1024,2048]{0,1:T(8,128)(2,1)} %maximum_bitcast_fusion) | data formatting | bytes 8388608 | tf_op jit(solution)/shard_map/dot_general | solution.py:135
  115.1 1.8 broadcast_select_fusion.7
  117.0 1.0 copy-done.7
  117.9 1.6 bitcast_select_fusion.3
  119.5 6.4 %multiply_reduce_fusion = (f32[1024,8]{0,1:T(8,128)S(1)}, f32[1024,1024]{0,1:T(8,128)S(1)}) fusion(bf16[1024,1024]{1,0:T(8,128)(2,1)S(1)} %get-tuple-element.12, bf16[1024,1024]{1,0:T(8,128)(2,1)S(1)} %get-tuple-element.11, bf16[512,2048]{1,0:T(8,128)(2,1)S(1)} %fusion.4, bf16[512,2048]{1,0:T(8,128)(2,1)} %collective-permute-done.2), kind=kOutput, calls=%fused_computation.20 | convolution fusion | flops 4313833472 | bytes 12615680 | tf_op jit(solution)/shard_map/dot_general | solution.py:133
  126.0 3.1 %collective-permute-done.6 = bf16[512,1024]{1,0:T(8,128)(2,1)} collective-permute-done((bf16[512,1024]{1,0:T(8,128)(2,1)S(1)}, bf16[512,1024]{1,0:T(8,128)(2,1)}, u32[]{:S(2)}, u32[]{:S(2)}) %collective-permute-start.6) | collective-permute-done | bytes 1048608 | tf_op jit(solution)/shard_map/ppermute | solution.py:17
  129.2 1.4 broadcast_select_fusion.5
  130.5 1.6 bitcast_select_fusion.1
  132.2 6.1 %fusion.28.v_ref = bf16[1024,1024]{1,0:T(8,128)(2,1)S(1)} fusion(bf16[1024,1024]{1,0:T(8,128)(2,1)S(1)} %get-tuple-element.8, bf16[1024,1024]{1,0:T(8,128)(2,1)S(1)} %get-tuple-element.7, bf16[512,2048]{1,0:T(8,128)(2,1)S(1)} %copy-done.13, bf16[512,2048]{1,0:T(8,128)(2,1)} %collective-permute-done.2), kind=kOutput, calls=%fused_computation.48 | convolution fusion | flops 4312793088 | bytes 10485760 | tf_op jit(solution)/shard_map/dot_general | solution.py:134
  138.3 1.3 convolution_convert_fusion
  139.6 0.0 all-gather.5.cloned.1.call-update
  139.6 6.8 %multiply_reduce_fusion.1 = (f32[512,8]{0,1:T(8,128)S(1)}, f32[512,8,128]{0,2,1:T(8,128)}) fusion(bf16[8,128,2048]{2,1,0:T(8,128)(2,1)} %bitcast.97, bf16[1,512,2048]{2,1,0:T(8,128)(2,1)} %param.7, f32[2048]{0:T(1024)S(1)} %copy-done.17, f32[512]{0:T(512)S(1)} %add_rsqrt_fusion.2), kind=kOutput, calls=%fused_computation.41 | convolution fusion | flops 2152722432 | bytes 8415232 | tf_op jit(solution)/shard_map/dot_general | solution.py:135
  146.4 5.4 %copy.43 = f32[1024,1024]{1,0:T(8,128)} copy(f32[1024,1024]{0,1:T(8,128)} %copy-done.11) | data formatting | bytes 8388608 | tf_op jit(solution)/shard_map/dot_general | solution.py:133
  151.8 2.8 %multiply_convert_fusion.2 = bf16[512,8,128]{0,2,1:T(8,128)(2,1)} fusion(f32[512,8,128]{0,2,1:T(8,128)} %get-tuple-element.29, f32[512,8]{0,1:T(8,128)S(1)} %add_rsqrt_fusion.1), kind=kLoop, calls=%fused_computation.40 | loop fusion | flops 1048576 | bytes 3162112 | tf_op jit(solution)/shard_map/convert_element_type | solution.py:131
  154.6 1.5 copy.45.q_ref
  156.1 0.0 copy-start.2
  156.1 2.5 %mul.217 = f32[1024,8,128]{0,2,1:T(8,128)} broadcast(f32[1024,8]{0,1:T(8,128)S(1)} %copy-done.16), dimensions={0,1} | broadcast | bytes 4227072 | tf_op jit(solution)/shard_map/mul | solution.py:26
  158.7 5.5 %copy.46 = f32[1024,1024]{1,0:T(8,128)} copy(f32[1024,1024]{0,1:T(8,128)} %bitcast.95) | data formatting | bytes 8388608 | tf_op jit(solution)/shard_map/mul | solution.py:26
  164.2 4.2 %multiply_convert_fusion.k_ref = bf16[1024,1024]{1,0:T(8,128)(2,1)S(1)} fusion(f32[1024,1024]{1,0:T(8,128)} %copy.43, f32[1024,1024]{1,0:T(8,128)} %copy.46), kind=kLoop, calls=%fused_computation.19 | loop fusion | flops 2097152 | bytes 10485760 | tf_op jit(solution)/shard_map/convert_element_type | solution.py:131
  168.4 10.4 %shard_map.73.window_ref = f32[512,1024]{1,0:T(8,128)S(1)} custom-call(f32[1,1]{1,0:T(1,128)} %bitcast.23.allow_ref, bf16[512,1024]{1,0:T(8,128)(2,1)S(1)} %copy.45.q_ref, bf16[1024,1024]{1,0:T(8,128)(2,1)S(1)} %multiply_convert_fusion.k_ref, bf16[1024,1024]{1,0:T(8,128)(2,1)S(1)} %fusion.28.v_ref), custom_call_target="tpu_custom_call" | custom-call | flops 2147483648 | bytes 7340032 | tf_op jit(solution)/shard_map/pallas_call | solution.py:61
  178.8 1.3 copy-done.3
  180.2 2.7 %broadcast_select_fusion.3 = (bf16[512,1024]{1,0:T(8,128)(2,1)S(1)}, bf16[512,1024]{1,0:T(8,128)(2,1)}) fusion(bf16[512,1024]{1,0:T(8,128)(2,1)} %collective-permute-done.7, bf16[512,1024]{1,0:T(8,128)(2,1)} %collective-permute-done.8, pred[]{:T(512)S(6)} %eq.7), kind=kLoop, calls=%fused_computation.63 | loop fusion | flops 1048576 | bytes 4194305 | tf_op jit(solution)/shard_map/jit(_where)/select_n | solution.py:35
  182.8 2.2 %fusion.48.state_ref = bf16[8,128,128]{2,1,0:T(8,128)(2,1)} fusion(bf16[32,128,128]{2,1,0:T(8,128)(2,1)} %all-gather.5.cloned.1.call-done, f32[]{:T(128)} %bitcast.9, f32[8]{0:T(128)S(1)} %get-tuple-element.26, f32[8]{0:T(128)S(1)} %get-tuple-element.27, f32[8]{0:T(128)S(1)} %get-tuple-element.25, pred[]{:T(512)S(6)} %gt.15, pred[]{:T(512)S(6)} %gt.14, ...), kind=kLoop, calls=%fused_computation.73 | loop fusion | flops 1703936 | bytes 1048679 | tf_op jit(solution)/shard_map/convert_element_type | solution.py:161
  185.0 6.5 %shard_map.74 = bf16[512,1024]{1,0:T(8,128)(2,1)} custom-call(bf16[512,1024]{1,0:T(8,128)(2,1)} %copy-done.2, bf16[8,128,128]{2,1,0:T(8,128)(2,1)} %fusion.48.state_ref, f32[512,8]{1,0:T(8,128)} %broadcast_divide_fusion.decay_ref, f32[512,1024]{1,0:T(8,128)} %copy-done.3), custom_call_target="tpu_custom_call" | custom-call | tf_op jit(solution)/shard_map/pallas_call | solution.py:92
  191.5 3.9 %fusion.31 = bf16[512,1024]{1,0:T(8,128)(2,1)} fusion(bf16[512,1024]{1,0:T(8,128)(2,1)} %shard_map.74, bf16[1024,1024]{1,0:T(8,128)(2,1)} %param.11, pred[]{:T(512)S(6)} %eq.8, bf16[512,1024]{1,0:T(8,128)(2,1)} %get-tuple-element.16, bf16[512,1024]{1,0:T(8,128)(2,1)S(1)} %get-tuple-element.15), kind=kOutput, calls=%fused_computation.49 | convolution fusion | flops 1079508992 | bytes 6291457 | tf_op jit(solution)/shard_map/dot_general | solution.py:176
  195.5 3.0 %collective-permute-done.9 = bf16[512,1024]{1,0:T(8,128)(2,1)} collective-permute-done((bf16[512,1024]{1,0:T(8,128)(2,1)}, bf16[512,1024]{1,0:T(8,128)(2,1)}, u32[]{:S(2)}, u32[]{:S(2)}) %collective-permute-start.9) | collective-permute-done | bytes 1048608 | tf_op jit(solution)/shard_map/ppermute | solution.py:17
  198.5 4.8 %fusion.36 = bf16[1,512,1024]{2,1,0:T(8,128)(2,1)} fusion(bf16[512,1024]{1,0:T(8,128)(2,1)} %collective-permute-done.9, bf16[512,1024]{1,0:T(8,128)(2,1)} %shard_map.74, bf16[1024,1024]{1,0:T(8,128)(2,1)} %param.11, pred[]{:T(512)S(6)} %eq.8, bf16[512,1024]{1,0:T(8,128)(2,1)} %get-tuple-element.16, bf16[512,1024]{1,0:T(8,128)(2,1)S(1)} %get-tuple-element.15, ...), kind=kOutput, calls=%fused_computation.50 | convolution fusion | flops 1081606144 | bytes 8388613 | tf_op jit(solution)/shard_map/dot_general | solution.py:178
  (44 shorter events, 0.1 us)
Async XLA Ops:
  6.5 29.0 %copy-start = (f32[1,8,512]{2,1,0:T(8,128)S(1)}, f32[1,8,512]{2,1,0:T(8,128)}, u32[]{:S(2)}) copy-start(f32[1,8,512]{2,1,0:T(8,128)} %param.12) | copy-start | bytes 49156
  6.5 176.3 %all-gather.5.cloned.1.call-start = ((), (), s32[]{:S(2)}) async-start(), calls=%async_computation | async-start | bytes 1310720 | tf_op jit(solution)/shard_map/all_gather | solution.py:153
  7.8 28.9 %collective-permute-start = (bf16[512,1024]{1,0:T(8,128)(2,1)S(1)}, bf16[512,1024]{1,0:T(8,128)(2,1)}, u32[]{:S(2)}, u32[]{:S(2)}) collective-permute-start(bf16[512,1024]{1,0:T(8,128)(2,1)S(1)} %constant_dynamic-slice_fusion.1), channel_id=1, source_target_pairs={{0,2},{2,0},{1,3},{3,1},{4,6},{6,4},{5,7},{7,5},{8,10},{10,8},{9,1... | collective-permute-start | bytes 3145736 | tf_op jit(solution)/shard_map/ppermute | solution.py:17
  19.9 5.0 %copy-start.6 = (bf16[1024,1,1024]{2,1,0:T(2,128)(2,1)}, bf16[1024,1,1024]{2,1,0:T(2,128)(2,1)S(1)}, u32[]{:S(2)}) copy-start(bf16[1024,1,1024]{2,1,0:T(2,128)(2,1)S(1)} %get-tuple-element.10) | copy-start | bytes 6291460
  19.9 9.9 %copy-start.4 = (bf16[1024,1,1024]{2,1,0:T(2,128)(2,1)}, bf16[1024,1,1024]{2,1,0:T(2,128)(2,1)S(1)}, u32[]{:S(2)}) copy-start(bf16[1024,1,1024]{2,1,0:T(2,128)(2,1)S(1)} %get-tuple-element.9) | copy-start | bytes 6291460
  20.8 3.1 %copy-start.8 = (bf16[1,512,2048]{2,1,0:T(8,128)(2,1)S(1)}, bf16[1,512,2048]{2,1,0:T(8,128)(2,1)}, u32[]{:S(2)}) copy-start(bf16[1,512,2048]{2,1,0:T(8,128)(2,1)} %param.7) | copy-start | bytes 6291460
  20.8 3.6 %copy-start.17 = (f32[2048]{0:T(1024)S(1)}, f32[2048]{0:T(1024)}, u32[]{:S(2)}) copy-start(f32[2048]{0:T(1024)} %param.8) | copy-start | bytes 24580
  21.9 58.4 %collective-permute-start.3 = (bf16[512,1024]{1,0:T(8,128)(2,1)}, bf16[512,1024]{1,0:T(8,128)(2,1)}, u32[]{:S(2)}, u32[]{:S(2)}) collective-permute-start(bf16[512,1024]{1,0:T(8,128)(2,1)} %dynamic-slice_bitcast_fusion.1), channel_id=1, source_target_pairs={{0,2},{2,0},{1,3},{3,1},{4,6},{6,4},{5,7},{7,5},{8,10},{10,8},{9,1... | collective-permute-start | bytes 3145736 | tf_op jit(solution)/shard_map/ppermute | solution.py:17
  25.0 94.5 %copy-start.12 = (bf16[512,2048]{1,0:T(8,128)(2,1)}, bf16[512,2048]{1,0:T(8,128)(2,1)S(1)}, u32[]{:S(2)}) copy-start(bf16[512,2048]{1,0:T(8,128)(2,1)S(1)} %fusion.4) | copy-start | bytes 6291460
  25.0 94.5 %collective-permute-start.2 = (bf16[512,2048]{1,0:T(8,128)(2,1)S(1)}, bf16[512,2048]{1,0:T(8,128)(2,1)}, u32[]{:S(2)}, u32[]{:S(2)}) collective-permute-start(bf16[512,2048]{1,0:T(8,128)(2,1)S(1)} %fusion.4), channel_id=1, source_target_pairs={{0,4},{4,8},{8,12},{1,5},{5,9},{9,13},{2,6},{6,10},{10,14},{3,7},{... | collective-permute-start | bytes 6291464 | tf_op jit(solution)/shard_map/ppermute | solution.py:22
  30.6 2.0 copy-start.14
  31.8 50.0 %collective-permute-start.5 = (bf16[512,1024]{1,0:T(8,128)(2,1)}, bf16[512,1024]{1,0:T(8,128)(2,1)S(1)}, u32[]{:S(2)}, u32[]{:S(2)}) collective-permute-start(bf16[512,1024]{1,0:T(8,128)(2,1)} %dynamic-slice_bitcast_fusion), channel_id=1, source_target_pairs={{0,2},{2,0},{1,3},{3,1},{4,6},{6,4},{5,7},{7,5},{8,10},{10,8},{9,1... | collective-permute-start | bytes 3145736 | tf_op jit(solution)/shard_map/ppermute | solution.py:17
  33.7 67.9 %collective-permute-start.7 = (bf16[512,1024]{1,0:T(8,128)(2,1)}, bf16[512,1024]{1,0:T(8,128)(2,1)}, u32[]{:S(2)}, u32[]{:S(2)}) collective-permute-start(bf16[512,1024]{1,0:T(8,128)(2,1)} %constant_dynamic-slice_fusion), channel_id=1, source_target_pairs={{0,2},{2,0},{1,3},{3,1},{4,6},{6,4},{5,7},{7,5},{8,10},{10,8},{9,1... | collective-permute-start | bytes 3145736 | tf_op jit(solution)/shard_map/ppermute | solution.py:17
  36.7 66.6 %collective-permute-start.1 = (bf16[512,1024]{1,0:T(8,128)(2,1)}, bf16[512,1024]{1,0:T(8,128)(2,1)}, u32[]{:S(2)}, u32[]{:S(2)}) collective-permute-start(bf16[512,1024]{1,0:T(8,128)(2,1)} %collective-permute-done), channel_id=1, source_target_pairs={{0,16},{16,0},{1,17},{17,1},{2,18},{18,2},{3,19},{19,3},{4,20},{20... | collective-permute-start | bytes 3145736 | tf_op jit(solution)/shard_map/ppermute | solution.py:17
  80.3 24.7 %copy-start.10 = (bf16[1024,1024]{1,0:T(8,128)(2,1)S(1)}, bf16[1024,1024]{1,0:T(8,128)(2,1)}, u32[]{:S(2)}) copy-start(bf16[1024,1024]{1,0:T(8,128)(2,1)} %param.9) | copy-start | bytes 6291460
  80.3 34.9 %collective-permute-start.4 = (bf16[512,1024]{1,0:T(8,128)(2,1)}, bf16[512,1024]{1,0:T(8,128)(2,1)}, u32[]{:S(2)}, u32[]{:S(2)}) collective-permute-start(bf16[512,1024]{1,0:T(8,128)(2,1)} %collective-permute-done.3), channel_id=1, source_target_pairs={{0,16},{16,0},{1,17},{17,1},{2,18},{18,2},{3,19},{19,3},{4,20},{20... | collective-permute-start | bytes 3145736 | tf_op jit(solution)/shard_map/ppermute | solution.py:17
  81.8 47.4 %collective-permute-start.6 = (bf16[512,1024]{1,0:T(8,128)(2,1)S(1)}, bf16[512,1024]{1,0:T(8,128)(2,1)}, u32[]{:S(2)}, u32[]{:S(2)}) collective-permute-start(bf16[512,1024]{1,0:T(8,128)(2,1)S(1)} %collective-permute-done.5), channel_id=1, source_target_pairs={{0,16},{16,0},{1,17},{17,1},{2,18},{18,2},{3,19},{19,3},{4,20},{20... | collective-permute-start | bytes 3145736 | tf_op jit(solution)/shard_map/ppermute | solution.py:17
  101.5 78.6 %collective-permute-start.8 = (bf16[512,1024]{1,0:T(8,128)(2,1)}, bf16[512,1024]{1,0:T(8,128)(2,1)}, u32[]{:S(2)}, u32[]{:S(2)}) collective-permute-start(bf16[512,1024]{1,0:T(8,128)(2,1)} %collective-permute-done.7), channel_id=1, source_target_pairs={{0,16},{16,0},{1,17},{17,1},{2,18},{18,2},{3,19},{19,3},{4,20},{20... | collective-permute-start | bytes 3145736 | tf_op jit(solution)/shard_map/ppermute | solution.py:17
  115.1 2.8 %copy-start.7 = (bf16[1024,1,1024]{2,1,0:T(2,128)(2,1)S(1)}, bf16[1024,1,1024]{2,1,0:T(2,128)(2,1)}, u32[]{:S(2)}) copy-start(bf16[1024,1,1024]{2,1,0:T(2,128)(2,1)} %copy-done.6) | copy-start | bytes 6291460
  126.0 12.3 %copy-start.11 = (f32[1024,1024]{0,1:T(8,128)}, f32[1024,1024]{0,1:T(8,128)S(1)}, u32[]{:S(2)}) copy-start(f32[1024,1024]{0,1:T(8,128)S(1)} %get-tuple-element.31) | copy-start | bytes 12582916
  126.0 4.5 %copy-start.15 = (f32[1024,8]{0,1:T(8,128)}, f32[1024,8]{0,1:T(8,128)S(1)}, u32[]{:S(2)}) copy-start(f32[1024,8]{0,1:T(8,128)S(1)} %add_rsqrt_fusion) | copy-start | bytes 98308
  126.0 4.5 %copy-start.5 = (bf16[1024,1,1024]{2,1,0:T(2,128)(2,1)S(1)}, bf16[1024,1,1024]{2,1,0:T(2,128)(2,1)}, u32[]{:S(2)}) copy-start(bf16[1024,1,1024]{2,1,0:T(2,128)(2,1)} %copy-done.4) | copy-start | bytes 6291460
  130.5 1.6 copy-start.13
  132.1 6.2 %slice-start = ((f32[1024,8]{0,1:T(8,128)}), f32[512,8]{0,1:T(8,128)S(1)}, s32[]{:S(2)}) async-start(f32[1024,8]{0,1:T(8,128)} %copy-done.15), calls=%async_computation.1 | async-start | bytes 32768 | tf_op jit(solution)/shard_map/slice | solution.py:144
  151.8 4.3 %copy-start.16 = (f32[1024,8]{0,1:T(8,128)S(1)}, f32[1024,8]{0,1:T(8,128)}, u32[]{:S(2)}) copy-start(f32[1024,8]{0,1:T(8,128)} %copy-done.15) | copy-start | bytes 98308
  156.1 12.2 %copy-start.2 = (bf16[512,1024]{1,0:T(8,128)(2,1)}, bf16[512,1024]{1,0:T(8,128)(2,1)S(1)}, u32[]{:S(2)}) copy-start(bf16[512,1024]{1,0:T(8,128)(2,1)S(1)} %copy.45.q_ref) | copy-start | bytes 3145732
  178.8 1.3 copy-start.3
  191.5 7.0 %copy-start.9 = (bf16[1,512,2048]{2,1,0:T(8,128)(2,1)S(1)}, bf16[1,512,2048]{2,1,0:T(8,128)(2,1)}, u32[]{:S(2)}) copy-start(bf16[1,512,2048]{2,1,0:T(8,128)(2,1)} %param.7) | copy-start | bytes 6291460
  195.5 3.0 %collective-permute-start.9 = (bf16[512,1024]{1,0:T(8,128)(2,1)}, bf16[512,1024]{1,0:T(8,128)(2,1)}, u32[]{:S(2)}, u32[]{:S(2)}) collective-permute-start(bf16[512,1024]{1,0:T(8,128)(2,1)} %fusion.31), channel_id=1, source_target_pairs={{0,1},{1,0},{2,3},{3,2},{4,5},{5,4},{6,7},{7,6},{8,9},{9,8},{10,11... | collective-permute-start | bytes 3145736 | tf_op jit(solution)/shard_map/ppermute | solution.py:17
  198.5 4.8 %copy-start.1 = (f32[1,8,512]{2,1,0:T(8,128)S(1)}, f32[1,8,512]{2,1,0:T(8,128)}, u32[]{:S(2)}) copy-start(f32[1,8,512]{2,1,0:T(8,128)} %param.12) | copy-start | bytes 49156
Sparse Core Ops, SparseCore 0:
  139.7 27.6 all-gather.4

commit v3 on v2

--- a/solution.py
+++ b/solution.py
@@ -26,14 +26,87 @@
     return values * lax.rsqrt(jnp.mean(values * values, axis=-1, keepdims=True) + eps)
 
 
-def other_half(block):
-    group = lax.axis_index("groups")
+def after(value, *earlier):
+    return lax.optimization_barrier((value, *earlier))[0]
+
+
+def rows_of_group(block):
     rows = block.shape[0] // 2
-    first = around(lax.dynamic_slice_in_dim(block, group * rows, rows, 0), "wloop")
-    second = around(first, "groups")
-    return jnp.concatenate(
-        [jnp.where(group == 0, first, second), jnp.where(group == 0, second, first)], axis=0
-    )
+    return lax.dynamic_slice_in_dim(block, lax.axis_index("groups") * rows, rows, 0)
+
+
+def projection_kernel(head_dim, place_ref, x_ref, own_ref, first_ref, second_ref, out_ref):
+    side, group = place_ref[0], place_ref[1]
+    deep, part = own_ref.shape[0], first_ref.shape[0]
+
+    def columns(start, size):
+        return x_ref[:, pl.ds(pl.multiple_of(start, 128), size)]
+
+    total = jnp.dot(columns(side * deep, deep), own_ref[...], preferred_element_type=F32)
+    base = (1 - side) * deep
+    total += jnp.dot(columns(base + group * part, part), first_ref[...], preferred_element_type=F32)
+    total += jnp.dot(
+        columns(base + (1 - group) * part, part), second_ref[...], preferred_element_type=F32
+    )
+    if not head_dim:
+        out_ref[...] = total.astype(BF16)
+        return
+    for start in range(0, total.shape[1], head_dim):
+        head = total[:, start : start + head_dim]
+        out_ref[:, start : start + head_dim] = rms_rows(head, 1e-06).astype(BF16)
+
+
+def projection(place, rows, own, first, second, head_dim):
+    count, width = rows.shape
+    inner = own.shape[1]
+    tile = 256
+    return pl.pallas_call(
+        functools.partial(projection_kernel, head_dim),
+        grid=(inner // tile,),
+        in_specs=[
+            pl.BlockSpec(memory_space=pltpu.SMEM),
+            pl.BlockSpec((count, width), lambda c: (0, 0)),
+            pl.BlockSpec((own.shape[0], tile), lambda c: (0, c)),
+            pl.BlockSpec((first.shape[0], tile), lambda c: (0, c)),
+            pl.BlockSpec((second.shape[0], tile), lambda c: (0, c)),
+        ],
+        out_specs=pl.BlockSpec((count, tile), lambda c: (0, c)),
+        out_shape=jax.ShapeDtypeStruct((count, inner), BF16),
+        compiler_params=pltpu.CompilerParams(vmem_limit_bytes=32 << 20),
+        cost_estimate=pl.CostEstimate(
+            flops=2 * count * width * inner,
+            bytes_accessed=2 * (count * width + width * inner + count * inner),
+            transcendentals=0,
+        ),
+    )(place, rows, own, first, second)
+
+
+def state_kernel(k_ref, v_ref, weight_ref, out_ref):
+    head = pl.program_id(0)
+    weight = weight_ref[...]
+    column = lax.broadcasted_iota(jnp.int32, weight.shape, 1)
+    mine = jnp.sum(jnp.where(column == head, weight, 0.0), axis=-1, keepdims=True)
+    faded = (k_ref[...].astype(F32) * mine).astype(BF16)
+    out_ref[0] = lax.dot_general(
+        faded, v_ref[...], (((0,), (0,)), ((), ())), preferred_element_type=F32
+    ).astype(BF16)
+
+
+def local_states(keys, values, weight, head_dim):
+    span, heads = weight.shape
+    block = pl.BlockSpec((span, head_dim), lambda h: (1, h))
+    return pl.pallas_call(
+        state_kernel,
+        grid=(heads,),
+        in_specs=[block, block, pl.BlockSpec((span, heads), lambda h: (0, 0))],
+        out_specs=pl.BlockSpec((1, head_dim, head_dim), lambda h: (h, 0, 0)),
+        out_shape=jax.ShapeDtypeStruct((heads, head_dim, head_dim), BF16),
+    )(keys, values, weight)
+
+
+def two_parts(value):
+    high = value.astype(BF16)
+    return high, (value - high.astype(F32)).astype(BF16)
 
 
 def window_kernel(scale, allow_ref, q_ref, k_ref, v_ref, out_ref):
@@ -114,25 +187,40 @@
     paired = lax.axis_size("wloop") == 2 and lax.axis_size("groups") == 2
     acts = activations.reshape(span, width)
 
-    def whole_rows(block):
-        if not paired:
-            return lax.all_gather(block, "wloop", axis=0, tiled=True)
-        other = other_half(block)
-        return jnp.concatenate(
-            [jnp.where(side == 0, block, other), jnp.where(side == 0, other, block)], axis=0
-        )
+    place = jnp.stack([side, lax.axis_index("groups")]).astype(jnp.int32)
+    w_pair = w_keyvalue.reshape(w_keyvalue.shape[0], 2 * inner_here)
+    own = [w_pair[:, :inner_here], w_pair[:, inner_here:], w_query, w_output]
+    if paired:
+        firsts, seconds = [], []
+        for block in own:
+            part = rows_of_group(block)
+            if firsts:
+                part = after(part, firsts[-1])
+            firsts.append(around(part, "wloop"))
+            part = firsts[-1]
+            if seconds:
+                part = after(part, seconds[-1])
+            seconds.append(around(part, "groups"))
+        blocks = list(zip(own, firsts, seconds))
+    else:
+        place = jnp.zeros((2,), jnp.int32)
+        blocks = []
+        for block in own[:3]:
+            full = lax.all_gather(block, "wloop", axis=0, tiled=True)
+            half = full.shape[0] // 2
+            blocks.append((full[:half], full[half : half + half // 2], full[half + half // 2 :]))
 
     normed = (rms_rows(acts.astype(F32), 1e-05) * norm_gain).astype(BF16)
-    both = jnp.concatenate([shifted(normed, "seq"), normed], axis=0)
-    w_key, w_value = w_keyvalue[:, 0, :], w_keyvalue[:, 1, :]
-    w_key, w_value, w_query = whole_rows(w_key), whole_rows(w_value), whole_rows(w_query)
-
-    def headed(raw):
-        return rms_rows(raw.reshape(-1, heads_here, head_dim), 1e-06).astype(BF16)
-
-    keys = headed(jnp.dot(both, w_key, preferred_element_type=F32)).reshape(2 * span, inner_here)
-    values = jnp.dot(both, w_value, preferred_element_type=F32).astype(BF16)
-    queries = headed(jnp.dot(normed, w_query, preferred_element_type=F32)).reshape(span, inner_here)
+    lane = width // 2
+    ours = shifted(lax.dynamic_slice_in_dim(normed, core * lane, lane, 1), "seq")
+    theirs = around(ours, "heads")
+    prior = jnp.concatenate(
+        [jnp.where(core == 0, ours, theirs), jnp.where(core == 0, theirs, ours)], axis=1
+    )
+    both = jnp.concatenate([prior, normed], axis=0)
+    keys = projection(place, both, *blocks[0], head_dim)
+    values = projection(place, both, *blocks[1], 0)
+    queries = projection(place, normed, *blocks[2], head_dim)
 
     keep = (1 - resets[0, 0]).astype(F32)
     upto = jnp.triu(jnp.ones((span, span), F32))
@@ -140,23 +228,18 @@
     whole = climb[:, -1]
     factor = jnp.exp(whole) * keep
     weight = jnp.exp(whole[:, None] - climb)
-    faded = (
-        keys[span:].reshape(span, heads_here, head_dim).astype(F32) * weight.T[:, :, None]
-    ).astype(BF16)
-    local_state = jnp.einsum(
-        "thd,the->hde",
-        faded,
-        values[span:].reshape(span, heads_here, head_dim),
-        preferred_element_type=F32,
-    )
-    local_mass = jnp.sum(weight * weight, axis=-1)
-    states = lax.all_gather(local_state.astype(BF16), "seq")
-    small = lax.all_gather(jnp.stack([factor, local_mass]), "seq")
-    state, mass = jnp.zeros_like(local_state), jnp.zeros_like(local_mass)
+    local_state = local_states(keys, values, weight.T, head_dim)
+    small = jnp.stack([*two_parts(factor), *two_parts(jnp.sum(weight * weight, axis=-1))], axis=1)
+    small = jnp.pad(small, ((0, 0), (0, 12)))
+    small = jnp.broadcast_to(small[:, :, None], (heads_here, 16, head_dim))
+    gathered = lax.all_gather(jnp.concatenate([local_state, small], axis=1), "seq")
+    state, mass = jnp.zeros(local_state.shape, F32), jnp.zeros(factor.shape, F32)
     for j in range(segments - 1):
-        fac, add_mass = small[j, 0], small[j, 1]
+        tail = gathered[j, :, head_dim : head_dim + 4, 0].astype(F32)
+        fac, add_mass = tail[:, 0] + tail[:, 1], tail[:, 2] + tail[:, 3]
         past = j < seg
-        state = jnp.where(past, fac[:, None, None] * state + states[j].astype(F32), state)
+        local = gathered[j, :, :head_dim].astype(F32)
+        state = jnp.where(past, fac[:, None, None] * state + local, state)
         mass = jnp.where(past, fac * fac * mass + add_mass, mass)
     entering = (state * keep).astype(BF16)
     decay = jnp.exp(climb) / jnp.sqrt(head_dim * (1.0 + mass * keep))[:, None]
@@ -165,7 +248,11 @@
     attended = add_read(queries, entering, decay.T, window)
 
     if paired:
-        other = other_half(w_output)
+        first, second = blocks[3][1:]
+        group = lax.axis_index("groups")
+        other = jnp.concatenate(
+            [jnp.where(group == 0, first, second), jnp.where(group == 0, second, first)], axis=0
+        )
         mine = jnp.where(side == core, w_output, other)
         theirs = jnp.where(side == core, other, w_output)
     else:

time: 211 us -> 179 us (0.85)
  blocking collectives: 40.7 us -> 0 us
  waiting for transfers between devices: 25.4 us -> 54.4 us
  matrix products: 30.3 us -> 4.59 us
  Pallas kernels: 17 us -> 42 us
  local copies, waits for them, and re-layouts: 41.5 us -> 23.9 us
  other arithmetic: 25.8 us -> 22.2 us
    all_gather x1 -> x0, blocking collectives: 40.7 us -> none  [shards(): small = lax.all_gather(jnp.stack([factor, local_mass]), 'seq')]
    pallas_call x0 -> x4, Pallas kernels: none -> 25 us  [the longest x3 18.2 us: projection(): pl.pallas_call(functools.partial(projection_kernel, head_dim), grid=(inne...]
    ppermute x9 -> x10, waiting for transfers between devices: 25.4 us -> 49.8 us  [around(): lax.ppermute(value, axis, [(i, (i + 1) % count) for i in range(count)])]
    dot_general x4 -> x0, matrix products: 20.6 us -> none  [the longest x1 6.79 us: shards(): jnp.dot(normed, w_query, preferred_element_type=F32)]
    dot_general x2 -> x1, local copies, waits for them, and re-layouts: 11.9 us -> 0.13 us  [shards(): climb = jnp.dot(log_retain[0], upto, precision=lax.Precision.HIGHEST)]
    concatenate x0 -> x2, other arithmetic: none -> 9.9 us  [the longest x1 8.19 us: shards(): both = jnp.concatenate([prior, normed], axis=0)]
    select_n x7 -> x2, other arithmetic: 11.9 us -> 3.51 us  [the longest x1 1.83 us: shards(): jnp.where(group == 0, first, second)]
    mul x2 -> x0, local copies, waits for them, and re-layouts: 8 us -> none  [rms_rows(): values * lax.rsqrt(jnp.mean(values * values, axis=-1, keepdims=True) + eps)]
  transfers between devices with their start and end apart: 11 -> 12, of which waited for: 3 -> 7; matrix products, arithmetic and copies ran while one was open for 38% -> 17% of each run, Pallas kernels for 5% -> 24%
where the time goes in v3:
time: 179 us; the launch traced here: 178 us
  waiting for transfers between devices  54.4 us (30%)
  Pallas kernels  42 us (23%)
  local copies, waits for them, and re-layouts  23.9 us (13%)
  other arithmetic  22.2 us (12%)
  starting transfers between devices  17 us (9%)
  between operations  14.3 us (8%)
  matrix products  4.59 us (3%)
    ppermute x10, waiting for transfers between devices, around(): lax.ppermute(value, axis, [(i, (i + 1) % count) for i in range(count)])  49.8 us
    pallas_call x3, Pallas kernels, projection(): pl.pallas_call(functools.partial(projection_kernel, head_dim), grid=(inne...  18.2 us
    ppermute x10, starting transfers between devices, around(): lax.ppermute(value, axis, [(i, (i + 1) % count) for i in range(count)])  12.5 us
    unnamed x36, local copies, waits for them, and re-layouts  12.3 us
    pallas_call x1, Pallas kernels, window_mix(): pl.pallas_call(functools.partial(window_kernel, scale), grid=(inner // he...  10.4 us
    concatenate x1, other arithmetic, shards(): both = jnp.concatenate([prior, normed], axis=0)  8.19 us
    dynamic_slice x4, local copies, waits for them, and re-layouts, rows_of_group(): lax.dynamic_slice_in_dim(block, lax.axis_index('groups') * rows, rows, 0)  8.13 us
    pallas_call x1, Pallas kernels, local_states(): pl.pallas_call(state_kernel, grid=(heads,), in_specs=[block, block, pl.Bl...  6.76 us
  transfers between devices with their start and end apart: 12, of which 7 were waited for; matrix products, arithmetic and copies ran while one was open for 17% of the time, Pallas kernels for 24%

profile of v3, /device:TPU:0, one launch (start us, length us, event | category | flops | bytes accessed | tf_op | source)
XLA Modules:
  0.0 178.4 jit_solution(14007188219613603175)
XLA Ops:
  6.5 3.6 %copy.74 = bf16[128,8,2,1024]{3,1,2,0:T(8,128)(2,1)S(1)} copy(bf16[128,8,2,1024]{3,2,1,0:T(2,128)(2,1)} %bitcast.61) | data formatting | bytes 8388608
  10.2 1.8 %fusion.40 = (bf16[1024,1024]{1,0:T(8,128)(2,1)S(1)}, bf16[1024,1024]{1,0:T(8,128)(2,1)}) fusion(bf16[1024,2048]{1,0:T(8,128)(2,1)S(1)} %bitcast.60), kind=kLoop, calls=%fused_computation.79 | loop fusion | bytes 8388608 | tf_op jit(solution)/shard_map/slice | solution.py:192
  12.0 1.2 constant_dynamic-slice_fusion.2
  13.2 2.9 %collective-permute-start = (bf16[512,1024]{1,0:T(8,128)(2,1)}, bf16[512,1024]{1,0:T(8,128)(2,1)S(1)}, u32[]{:S(2)}, u32[]{:S(2)}) collective-permute-start(bf16[512,1024]{1,0:T(8,128)(2,1)} %constant_dynamic-slice_fusion.2), channel_id=1, source_target_pairs={{0,2},{2,0},{1,3},{3,1},{4,6},{6,4},{5,7},{7,5},{8,10},{10,8},{9,1... | collective-permute-start | bytes 3145736 | tf_op jit(solution)/shard_map/ppermute | solution.py:17
  16.1 2.1 %fusion = f32[512]{0:T(512)S(1)} fusion(bf16[1,512,2048]{2,1,0:T(8,128)(2,1)} %param.7), kind=kLoop, calls=%fused_computation.2 | loop fusion | flops 3145216 | bytes 2099200 | tf_op jit(solution)/shard_map/reduce_sum | solution.py:26
  18.2 2.1 %fusion.2.x_ref = bf16[512,2048]{1,0:T(8,128)(2,1)S(1)} fusion(bf16[1,512,2048]{2,1,0:T(8,128)(2,1)} %param.7, f32[2048]{0:T(1024)S(1)} %copy-done.16, f32[512]{0:T(512)S(1)} %add_rsqrt_fusion), kind=kLoop, calls=%fused_computation.4 | loop fusion | flops 4194304 | bytes 4204544 | tf_op jit(solution)/shard_map/convert_element_type | solution.py:213
  20.3 1.1 constant_dynamic-slice_fusion.1
  21.4 4.4 %collective-permute-start.6 = (bf16[512,1024]{1,0:T(8,128)(2,1)}, bf16[512,1024]{1,0:T(8,128)(2,1)}, u32[]{:S(2)}, u32[]{:S(2)}) collective-permute-start(bf16[512,1024]{1,0:T(8,128)(2,1)} %constant_dynamic-slice_fusion.1), channel_id=1, source_target_pairs={{0,4},{4,8},{8,12},{1,5},{5,9},{9,13},{2,6},{6,10},{10,14},{3,7},{... | collective-permute-start | bytes 3145736 | tf_op jit(solution)/shard_map/ppermute | solution.py:22
  26.5 0.9 fusion.41
  27.5 0.1 copy.65
  27.6 0.1 multiply_reduce_fusion
  27.7 2.3 %constant_dynamic-slice_fusion.3 = bf16[512,1024]{1,0:T(8,128)(2,1)} fusion(bf16[1024,1024]{1,0:T(8,128)(2,1)} %get-tuple-element.18.own_ref, s32[]{:T(128)S(6)} %select_n.92), kind=kLoop, calls=%fused_computation.52 | loop fusion | bytes 2097156 | tf_op jit(solution)/shard_map/dynamic_slice | solution.py:35
  30.0 9.4 %collective-permute-done.first_ref = bf16[512,1024]{1,0:T(8,128)(2,1)S(1)} collective-permute-done((bf16[512,1024]{1,0:T(8,128)(2,1)}, bf16[512,1024]{1,0:T(8,128)(2,1)S(1)}, u32[]{:S(2)}, u32[]{:S(2)}) %collective-permute-start) | collective-permute-done | bytes 1048608 | tf_op jit(solution)/shard_map/ppermute | solution.py:17
  39.5 1.7 collective-permute-start.1
  41.2 1.5 collective-permute-start.3
  42.7 4.6 %collective-permute-done.6 = bf16[512,1024]{1,0:T(8,128)(2,1)} collective-permute-done((bf16[512,1024]{1,0:T(8,128)(2,1)}, bf16[512,1024]{1,0:T(8,128)(2,1)}, u32[]{:S(2)}, u32[]{:S(2)}) %collective-permute-start.6) | collective-permute-done | bytes 1048608 | tf_op jit(solution)/shard_map/ppermute | solution.py:22
  47.3 0.0 collective-permute-start.7
  47.4 0.1 copy.73
  47.5 0.1 pad_add_fusion.place_ref
  47.5 2.3 %constant_dynamic-slice_fusion.4 = bf16[512,1024]{1,0:T(8,128)(2,1)} fusion(bf16[1024,1024]{1,0:T(8,128)(2,1)} %own_ref.1, s32[]{:T(128)S(6)} %select_n.92), kind=kLoop, calls=%fused_computation.53 | loop fusion | bytes 2097156 | tf_op jit(solution)/shard_map/dynamic_slice | solution.py:35
  49.8 0.7 subtract_exponential_fusion.weight_ref
  50.5 13.6 %collective-permute-done.1.first_ref = bf16[512,1024]{1,0:T(8,128)(2,1)} collective-permute-done((bf16[512,1024]{1,0:T(8,128)(2,1)}, bf16[512,1024]{1,0:T(8,128)(2,1)}, u32[]{:S(2)}, u32[]{:S(2)}) %collective-permute-start.1) | collective-permute-done | bytes 1048608 | tf_op jit(solution)/shard_map/ppermute | solution.py:17
  64.1 1.4 collective-permute-start.2
  65.5 1.5 collective-permute-start.4
  67.1 0.0 collective-permute-done.7
  67.1 1.7 broadcast_select_fusion.3
  68.8 8.2 %pad_maximum_fusion.x_ref = bf16[1024,2048]{1,0:T(8,128)(2,1)S(1)} fusion(bf16[512,2048]{1,0:T(8,128)(2,1)S(1)} %fusion.2.x_ref, bf16[512,1024]{1,0:T(8,128)(2,1)S(1)} %get-tuple-element.22, bf16[512,1024]{1,0:T(8,128)(2,1)S(1)} %get-tuple-element.21), kind=kLoop, calls=%fused_computation.5 | loop fusion | flops 12582912 | bytes 8388608 | tf_op jit(solution)/shard_map/concatenate | solution.py:220
  77.0 7.1 %shard_map.74.k_ref = bf16[1024,1024]{1,0:T(8,128)(2,1)S(1)} custom-call(s32[2]{0:T(128)S(1)} %pad_add_fusion.place_ref, bf16[1024,2048]{1,0:T(8,128)(2,1)S(1)} %pad_maximum_fusion.x_ref, bf16[1024,1024]{1,0:T(8,128)(2,1)S(1)} %copy-done.3, bf16[512,1024]{1,0:T(8,128)(2,1)S(1)} %collective-permute-done.first_ref, ...), custom_call_target="tpu_custom_call" | custom-call | flops 4294967296 | bytes 10485760 | tf_op jit(solution)/shard_map/pallas_call | solution.py:63
  84.1 1.3 copy-done.4
  85.4 3.2 %collective-permute-done.4.second_ref = bf16[512,1024]{1,0:T(8,128)(2,1)S(1)} collective-permute-done((bf16[512,1024]{1,0:T(8,128)(2,1)}, bf16[512,1024]{1,0:T(8,128)(2,1)S(1)}, u32[]{:S(2)}, u32[]{:S(2)}) %collective-permute-start.4) | collective-permute-done | bytes 1048608 | tf_op jit(solution)/shard_map/ppermute | solution.py:17
  88.6 6.5 %shard_map.75.v_ref = bf16[1024,1024]{1,0:T(8,128)(2,1)S(1)} custom-call(s32[2]{0:T(128)S(1)} %pad_add_fusion.place_ref, bf16[1024,2048]{1,0:T(8,128)(2,1)S(1)} %pad_maximum_fusion.x_ref, bf16[1024,1024]{1,0:T(8,128)(2,1)S(1)} %copy-done.1, bf16[512,1024]{1,0:T(8,128)(2,1)} %collective-permute-done.1.first_ref, ...), custom_call_target="tpu_custom_call" | custom-call | flops 4294967296 | bytes 10485760 | tf_op jit(solution)/shard_map/pallas_call | solution.py:63
  95.1 1.3 copy-done.6
  96.5 6.8 %shard_map.76 = bf16[8,128,128]{2,1,0:T(8,128)(2,1)} custom-call(bf16[1024,1024]{1,0:T(8,128)(2,1)} %copy-done.4, bf16[1024,1024]{1,0:T(8,128)(2,1)} %copy-done.6, f32[512,8]{1,0:T(8,128)} %subtract_exponential_fusion.weight_ref), custom_call_target="tpu_custom_call" | custom-call | tf_op jit(solution)/shard_map/pallas_call | solution.py:98
  103.2 0.1 broadcast_in_dim.26
  103.3 1.7 pad_maximum_fusion.4
  105.0 0.0 all-gather.3.cloned.1.call-update
  105.0 2.4 %constant_dynamic-slice_fusion = bf16[512,1024]{1,0:T(8,128)(2,1)} fusion(bf16[1024,1024]{1,0:T(8,128)(2,1)} %param.11, s32[]{:T(128)S(6)} %select_n.92), kind=kLoop, calls=%fused_computation.49 | loop fusion | bytes 2097156 | tf_op jit(solution)/shard_map/dynamic_slice | solution.py:35
  107.4 0.9 collective-permute-start.8
  108.4 1.2 collective-permute-start.5
  109.6 0.1 copy.72
  109.7 20.0 %collective-permute-done.8 = bf16[512,1024]{1,0:T(8,128)(2,1)} collective-permute-done((bf16[512,1024]{1,0:T(8,128)(2,1)}, bf16[512,1024]{1,0:T(8,128)(2,1)}, u32[]{:S(2)}, u32[]{:S(2)}) %collective-permute-start.8) | collective-permute-done | bytes 1048608 | tf_op jit(solution)/shard_map/ppermute | solution.py:17
  129.8 0.9 collective-permute-done.5.second_ref
  130.6 1.0 copy-done.11
  131.6 1.2 collective-permute-start.9
  132.8 1.6 copy-done.10
  134.4 1.2 copy-done.12
  135.6 4.6 %shard_map.73.q_ref = bf16[512,1024]{1,0:T(8,128)(2,1)S(1)} custom-call(s32[2]{0:T(128)S(1)} %pad_add_fusion.place_ref, bf16[512,2048]{1,0:T(8,128)(2,1)S(1)} %fusion.2.x_ref, bf16[1024,1024]{1,0:T(8,128)(2,1)S(1)} %copy-done.10, bf16[512,1024]{1,0:T(8,128)(2,1)} %collective-permute-done.2.first_ref, bf16[512,1024]{1,0:T(8,128)(2,1)S(1)} %copy-done.12), custom_call_target="tpu_custom_call" | custom-call | flops 2147483648 | bytes 7340032 | tf_op jit(solution)/shard_map/pallas_call | solution.py:63
  140.2 0.0 copy-start.9
  140.3 10.4 %shard_map.77.window_ref = f32[512,1024]{1,0:T(8,128)S(1)} custom-call(f32[1,1]{1,0:T(1,128)} %bitcast.21.allow_ref, bf16[512,1024]{1,0:T(8,128)(2,1)S(1)} %shard_map.73.q_ref, bf16[1024,1024]{1,0:T(8,128)(2,1)S(1)} %copy-done.5, bf16[1024,1024]{1,0:T(8,128)(2,1)S(1)} %copy-done.7), custom_call_target="tpu_custom_call" | custom-call | flops 2147483648 | bytes 7340032 | tf_op jit(solution)/shard_map/pallas_call | solution.py:134
  150.7 1.3 copy-done.8
  152.1 0.8 slice_convert_fusion.2
  152.8 0.1 copy.69
  152.9 0.1 copy.71
  153.1 0.1 copy.70
  153.2 0.7 broadcast_divide_fusion.decay_ref
  153.9 2.1 %fusion.22.state_ref = bf16[8,128,128]{2,1,0:T(8,128)(2,1)} fusion(bf16[4,8,144,128]{3,2,1,0:T(8,128)(2,1)} %bitcast.64, f32[]{:T(128)} %bitcast.8, f32[8]{0:T(128)S(1)} %get-tuple-element.30, f32[8]{0:T(128)S(1)} %get-tuple-element.34, f32[8]{0:T(128)S(1)} %get-tuple-element.33, pred[]{:T(512)S(6)} %gt.15, pred[]{:T(512)S(6)} %gt.14, pred[]{:T(512)S(6)} %gt.13), kind=kLoop, calls=%fused_computation.27 | loop fusion | flops 1703936 | bytes 1048679 | tf_op jit(solution)/shard_map/convert_element_type | solution.py:244
  156.1 6.5 %shard_map.78 = bf16[512,1024]{1,0:T(8,128)(2,1)} custom-call(bf16[512,1024]{1,0:T(8,128)(2,1)} %copy-done.9, bf16[8,128,128]{2,1,0:T(8,128)(2,1)} %fusion.22.state_ref, f32[512,8]{1,0:T(8,128)} %broadcast_divide_fusion.decay_ref, f32[512,1024]{1,0:T(8,128)} %copy-done.8), custom_call_target="tpu_custom_call" | custom-call | tf_op jit(solution)/shard_map/pallas_call | solution.py:165
  162.6 1.8 %broadcast_select_fusion.1 = (bf16[512,1024]{1,0:T(8,128)(2,1)S(1)}, bf16[512,1024]{1,0:T(8,128)(2,1)S(1)}) fusion(bf16[512,1024]{1,0:T(8,128)(2,1)} %collective-permute-done.8, bf16[512,1024]{1,0:T(8,128)(2,1)} %collective-permute-done.9, pred[]{:T(512)S(6)} %eq.14), kind=kLoop, calls=%fused_computation.21 | loop fusion | flops 1048576 | bytes 4194305 | tf_op jit(solution)/shard_map/jit(_where)/select_n | solution.py:254
  164.5 0.0 copy-done.14
  164.5 0.7 copy-done.15
  165.2 1.3 fusion.10
  166.5 0.1 collective-permute-start.10
  166.6 2.6 %collective-permute-done.10 = bf16[512,1024]{1,0:T(8,128)(2,1)S(1)} collective-permute-done((bf16[512,1024]{1,0:T(8,128)(2,1)S(1)}, bf16[512,1024]{1,0:T(8,128)(2,1)S(1)}, u32[]{:S(2)}, u32[]{:S(2)}) %collective-permute-start.10) | collective-permute-done | bytes 1048608 | tf_op jit(solution)/shard_map/ppermute | solution.py:17
  169.2 2.4 %fusion.15 = bf16[1,512,1024]{2,1,0:T(8,128)(2,1)} fusion(bf16[512,1024]{1,0:T(8,128)(2,1)S(1)} %collective-permute-done.10, bf16[512,1024]{1,0:T(8,128)(2,1)S(1)} %copy-done.14, bf16[1024,1024]{1,0:T(8,128)(2,1)S(1)} %copy-done.15, pred[]{:T(512)S(6)} %eq.13, bf16[512,1024]{1,0:T(8,128)(2,1)S(1)} %get-tuple-element.20, ...), kind=kOutput, calls=%fused_computation.16 | convolution fusion | flops 1081606144 | bytes 8388613 | tf_op jit(solution)/shard_map/dot_general | solution.py:265
  (39 shorter events, 0.1 us)
Async XLA Ops:
  6.5 20.0 %copy-start = (f32[1,8,512]{2,1,0:T(8,128)S(1)}, f32[1,8,512]{2,1,0:T(8,128)}, u32[]{:S(2)}) copy-start(f32[1,8,512]{2,1,0:T(8,128)} %param.12) | copy-start | bytes 49156
  6.5 145.5 %all-gather.3.cloned.1.call-start = ((), (), s32[]{:S(2)}) async-start(), calls=%async_computation | async-start | bytes 1474560 | tf_op jit(solution)/shard_map/all_gather | solution.py:235
  12.0 6.2 %copy-start.2 = (bf16[1024,1024]{1,0:T(8,128)(2,1)}, bf16[1024,1024]{1,0:T(8,128)(2,1)S(1)}, u32[]{:S(2)}) copy-start(bf16[1024,1024]{1,0:T(8,128)(2,1)S(1)} %get-tuple-element.17.own_ref) | copy-start | bytes 6291460
  12.0 6.2 %copy-start.16 = (f32[2048]{0:T(1024)S(1)}, f32[2048]{0:T(1024)}, u32[]{:S(2)}) copy-start(f32[2048]{0:T(1024)} %param.8) | copy-start | bytes 24580
  13.2 26.3 %collective-permute-start = (bf16[512,1024]{1,0:T(8,128)(2,1)}, bf16[512,1024]{1,0:T(8,128)(2,1)S(1)}, u32[]{:S(2)}, u32[]{:S(2)}) collective-permute-start(bf16[512,1024]{1,0:T(8,128)(2,1)} %constant_dynamic-slice_fusion.2), channel_id=1, source_target_pairs={{0,2},{2,0},{1,3},{3,1},{4,6},{6,4},{5,7},{7,5},{8,10},{10,8},{9,1... | collective-permute-start | bytes 3145736 | tf_op jit(solution)/shard_map/ppermute | solution.py:17
  21.4 25.9 %collective-permute-start.6 = (bf16[512,1024]{1,0:T(8,128)(2,1)}, bf16[512,1024]{1,0:T(8,128)(2,1)}, u32[]{:S(2)}, u32[]{:S(2)}) collective-permute-start(bf16[512,1024]{1,0:T(8,128)(2,1)} %constant_dynamic-slice_fusion.1), channel_id=1, source_target_pairs={{0,4},{4,8},{8,12},{1,5},{5,9},{9,13},{2,6},{6,10},{10,14},{3,7},{... | collective-permute-start | bytes 3145736 | tf_op jit(solution)/shard_map/ppermute | solution.py:22
  39.5 24.7 %collective-permute-start.1 = (bf16[512,1024]{1,0:T(8,128)(2,1)}, bf16[512,1024]{1,0:T(8,128)(2,1)}, u32[]{:S(2)}, u32[]{:S(2)}) collective-permute-start(bf16[512,1024]{1,0:T(8,128)(2,1)} %constant_dynamic-slice_fusion.3), channel_id=1, source_target_pairs={{0,2},{2,0},{1,3},{3,1},{4,6},{6,4},{5,7},{7,5},{8,10},{10,8},{9,1... | collective-permute-start | bytes 3145736 | tf_op jit(solution)/shard_map/ppermute | solution.py:17
  41.2 24.3 %collective-permute-start.3 = (bf16[512,1024]{1,0:T(8,128)(2,1)S(1)}, bf16[512,1024]{1,0:T(8,128)(2,1)}, u32[]{:S(2)}, u32[]{:S(2)}) collective-permute-start(bf16[512,1024]{1,0:T(8,128)(2,1)S(1)} %collective-permute-done.first_ref), channel_id=1, source_target_pairs={{0,16},{16,0},{1,17},{17,1},{2,18},{18,2},{3,19},{19,3},{4,20},{20... | collective-permute-start | bytes 3145736 | tf_op jit(solution)/shard_map/ppermute | solution.py:17
  47.3 19.7 %collective-permute-start.7 = (bf16[512,1024]{1,0:T(8,128)(2,1)}, bf16[512,1024]{1,0:T(8,128)(2,1)}, u32[]{:S(2)}, u32[]{:S(2)}) collective-permute-start(bf16[512,1024]{1,0:T(8,128)(2,1)} %collective-permute-done.6), channel_id=1, source_target_pairs={{0,1},{1,0},{2,3},{3,2},{4,5},{5,4},{6,7},{7,6},{8,9},{9,8},{10,11... | collective-permute-start | bytes 3145736 | tf_op jit(solution)/shard_map/ppermute | solution.py:17
  64.1 43.3 %collective-permute-start.2 = (bf16[512,1024]{1,0:T(8,128)(2,1)}, bf16[512,1024]{1,0:T(8,128)(2,1)}, u32[]{:S(2)}, u32[]{:S(2)}) collective-permute-start(bf16[512,1024]{1,0:T(8,128)(2,1)} %constant_dynamic-slice_fusion.4), channel_id=1, source_target_pairs={{0,2},{2,0},{1,3},{3,1},{4,6},{6,4},{5,7},{7,5},{8,10},{10,8},{9,1... | collective-permute-start | bytes 3145736 | tf_op jit(solution)/shard_map/ppermute | solution.py:17
  65.5 23.0 %collective-permute-start.4 = (bf16[512,1024]{1,0:T(8,128)(2,1)}, bf16[512,1024]{1,0:T(8,128)(2,1)S(1)}, u32[]{:S(2)}, u32[]{:S(2)}) collective-permute-start(bf16[512,1024]{1,0:T(8,128)(2,1)} %collective-permute-done.1.first_ref), channel_id=1, source_target_pairs={{0,16},{16,0},{1,17},{17,1},{2,18},{18,2},{3,19},{19,3},{4,20},{20... | collective-permute-start | bytes 3145736 | tf_op jit(solution)/shard_map/ppermute | solution.py:17
  68.8 8.2 %copy-start.3 = (bf16[1024,1024]{1,0:T(8,128)(2,1)S(1)}, bf16[1024,1024]{1,0:T(8,128)(2,1)}, u32[]{:S(2)}) copy-start(bf16[1024,1024]{1,0:T(8,128)(2,1)} %copy-done.2) | copy-start | bytes 6291460
  77.0 11.6 %copy-start.1 = (bf16[1024,1024]{1,0:T(8,128)(2,1)S(1)}, bf16[1024,1024]{1,0:T(8,128)(2,1)}, u32[]{:S(2)}) copy-start(bf16[1024,1024]{1,0:T(8,128)(2,1)} %get-tuple-element.18.own_ref) | copy-start | bytes 6291460
  84.0 1.3 copy-start.4
  95.1 1.4 copy-start.6
  107.4 22.3 %collective-permute-start.8 = (bf16[512,1024]{1,0:T(8,128)(2,1)}, bf16[512,1024]{1,0:T(8,128)(2,1)}, u32[]{:S(2)}, u32[]{:S(2)}) collective-permute-start(bf16[512,1024]{1,0:T(8,128)(2,1)} %constant_dynamic-slice_fusion), channel_id=1, source_target_pairs={{0,2},{2,0},{1,3},{3,1},{4,6},{6,4},{5,7},{7,5},{8,10},{10,8},{9,1... | collective-permute-start | bytes 3145736 | tf_op jit(solution)/shard_map/ppermute | solution.py:17
  108.4 22.3 %collective-permute-start.5 = (bf16[512,1024]{1,0:T(8,128)(2,1)}, bf16[512,1024]{1,0:T(8,128)(2,1)S(1)}, u32[]{:S(2)}, u32[]{:S(2)}) collective-permute-start(bf16[512,1024]{1,0:T(8,128)(2,1)} %collective-permute-done.2.first_ref), channel_id=1, source_target_pairs={{0,16},{16,0},{1,17},{17,1},{2,18},{18,2},{3,19},{19,3},{4,20},{20... | collective-permute-start | bytes 3145736 | tf_op jit(solution)/shard_map/ppermute | solution.py:17
  109.7 30.5 %copy-start.5 = (bf16[1024,1024]{1,0:T(8,128)(2,1)S(1)}, bf16[1024,1024]{1,0:T(8,128)(2,1)}, u32[]{:S(2)}) copy-start(bf16[1024,1024]{1,0:T(8,128)(2,1)} %copy-done.4) | copy-start | bytes 6291460
  109.7 30.5 %copy-start.7 = (bf16[1024,1024]{1,0:T(8,128)(2,1)S(1)}, bf16[1024,1024]{1,0:T(8,128)(2,1)}, u32[]{:S(2)}) copy-start(bf16[1024,1024]{1,0:T(8,128)(2,1)} %copy-done.6) | copy-start | bytes 6291460
  130.6 1.0 copy-start.11
  131.6 31.0 %collective-permute-start.9 = (bf16[512,1024]{1,0:T(8,128)(2,1)}, bf16[512,1024]{1,0:T(8,128)(2,1)}, u32[]{:S(2)}, u32[]{:S(2)}) collective-permute-start(bf16[512,1024]{1,0:T(8,128)(2,1)} %collective-permute-done.8), channel_id=1, source_target_pairs={{0,16},{16,0},{1,17},{17,1},{2,18},{18,2},{3,19},{19,3},{4,20},{20... | collective-permute-start | bytes 3145736 | tf_op jit(solution)/shard_map/ppermute | solution.py:17
  132.8 1.6 copy-start.10
  134.3 1.2 copy-start.12
  140.2 10.5 %copy-start.9 = (bf16[512,1024]{1,0:T(8,128)(2,1)}, bf16[512,1024]{1,0:T(8,128)(2,1)S(1)}, u32[]{:S(2)}) copy-start(bf16[512,1024]{1,0:T(8,128)(2,1)S(1)} %shard_map.73.q_ref) | copy-start | bytes 3145732
  150.7 1.4 copy-start.8
  162.6 1.9 %copy-start.14 = (bf16[512,1024]{1,0:T(8,128)(2,1)S(1)}, bf16[512,1024]{1,0:T(8,128)(2,1)}, u32[]{:S(2)}) copy-start(bf16[512,1024]{1,0:T(8,128)(2,1)} %shard_map.78) | copy-start | bytes 3145732
  162.6 2.5 %copy-start.15 = (bf16[1024,1024]{1,0:T(8,128)(2,1)S(1)}, bf16[1024,1024]{1,0:T(8,128)(2,1)}, u32[]{:S(2)}) copy-start(bf16[1024,1024]{1,0:T(8,128)(2,1)} %param.11) | copy-start | bytes 6291460
  165.2 4.0 %copy-start.13 = (bf16[1,512,2048]{2,1,0:T(8,128)(2,1)S(1)}, bf16[1,512,2048]{2,1,0:T(8,128)(2,1)}, u32[]{:S(2)}) copy-start(bf16[1,512,2048]{2,1,0:T(8,128)(2,1)} %param.7) | copy-start | bytes 6291460
  166.5 2.7 %collective-permute-start.10 = (bf16[512,1024]{1,0:T(8,128)(2,1)S(1)}, bf16[512,1024]{1,0:T(8,128)(2,1)S(1)}, u32[]{:S(2)}, u32[]{:S(2)}) collective-permute-start(bf16[512,1024]{1,0:T(8,128)(2,1)S(1)} %fusion.10), channel_id=1, source_target_pairs={{0,1},{1,0},{2,3},{3,2},{4,5},{5,4},{6,7},{7,6},{8,9},{9,8},{10,11... | collective-permute-start | bytes 3145736 | tf_op jit(solution)/shard_map/ppermute | solution.py:17
Sparse Core Ops, SparseCore 0:
  105.2 31.0 all-gather.2

commit v4 on v3

--- a/solution.py
+++ b/solution.py
@@ -30,9 +30,20 @@
     return lax.optimization_barrier((value, *earlier))[0]
 
 
-def rows_of_group(block):
-    rows = block.shape[0] // 2
-    return lax.dynamic_slice_in_dim(block, lax.axis_index("groups") * rows, rows, 0)
+def part_of(block, index, count):
+    rows = block.shape[0] // count
+    return lax.dynamic_slice_in_dim(block, index * rows, rows, 0)
+
+
+def swapped(value, axis):
+    count = lax.axis_size(axis)
+    return lax.ppermute(value, axis, [(i, i + 1 - 2 * (i % 2)) for i in range(count)])
+
+
+def in_order(index, first, second):
+    return jnp.concatenate(
+        [jnp.where(index == 0, first, second), jnp.where(index == 0, second, first)], axis=0
+    )
 
 
 def projection_kernel(head_dim, place_ref, x_ref, own_ref, first_ref, second_ref, out_ref):
@@ -185,34 +196,41 @@
     side, core, seg = lax.axis_index("wloop"), lax.axis_index("heads"), lax.axis_index("seq")
     segments = lax.axis_size("seq")
     paired = lax.axis_size("wloop") == 2 and lax.axis_size("groups") == 2
+    paired = paired and segments % 2 == 0
     acts = activations.reshape(span, width)
 
-    place = jnp.stack([side, lax.axis_index("groups")]).astype(jnp.int32)
+    group, twin = lax.axis_index("groups"), seg % 2
+    place = jnp.stack([side, group]).astype(jnp.int32)
+    place_query = jnp.stack([side, twin]).astype(jnp.int32)
+    normed = (rms_rows(acts.astype(F32), 1e-05) * norm_gain).astype(BF16)
+    lane = width // 2
+    ours = shifted(lax.dynamic_slice_in_dim(normed, core * lane, lane, 1), "seq")
     w_pair = w_keyvalue.reshape(w_keyvalue.shape[0], 2 * inner_here)
     own = [w_pair[:, :inner_here], w_pair[:, inner_here:], w_query, w_output]
     if paired:
-        firsts, seconds = [], []
-        for block in own:
-            part = rows_of_group(block)
-            if firsts:
-                part = after(part, firsts[-1])
-            firsts.append(around(part, "wloop"))
-            part = firsts[-1]
-            if seconds:
-                part = after(part, seconds[-1])
-            seconds.append(around(part, "groups"))
-        blocks = list(zip(own, firsts, seconds))
+        key_x = swapped(part_of(own[0], group, 2), "wloop")
+        key_y = swapped(key_x, "groups")
+        value_x = swapped(after(part_of(own[1], 2 * group + twin, 4), key_x), "wloop")
+        query_x = swapped(after(part_of(own[2], twin, 2), value_x), "wloop")
+        value_z = swapped(after(value_x, ours), "seq")
+        value_half = in_order(twin, value_x, value_z)
+        value_y = swapped(after(value_half, key_y), "groups")
+        output_x = swapped(after(part_of(own[3], group, 2), query_x), "wloop")
+        query_z = swapped(after(query_x, value_z), "seq")
+        output_y = swapped(after(output_x, value_y), "groups")
+        blocks = [
+            (own[0], key_x, key_y),
+            (own[1], value_half, after(value_y, query_x)),
+            (own[2], query_x, after(query_z, output_x)),
+        ]
     else:
-        place = jnp.zeros((2,), jnp.int32)
+        place = place_query = jnp.zeros((2,), jnp.int32)
         blocks = []
         for block in own[:3]:
             full = lax.all_gather(block, "wloop", axis=0, tiled=True)
             half = full.shape[0] // 2
             blocks.append((full[:half], full[half : half + half // 2], full[half + half // 2 :]))
 
-    normed = (rms_rows(acts.astype(F32), 1e-05) * norm_gain).astype(BF16)
-    lane = width // 2
-    ours = shifted(lax.dynamic_slice_in_dim(normed, core * lane, lane, 1), "seq")
     theirs = around(ours, "heads")
     prior = jnp.concatenate(
         [jnp.where(core == 0, ours, theirs), jnp.where(core == 0, theirs, ours)], axis=1
@@ -220,7 +238,7 @@
     both = jnp.concatenate([prior, normed], axis=0)
     keys = projection(place, both, *blocks[0], head_dim)
     values = projection(place, both, *blocks[1], 0)
-    queries = projection(place, normed, *blocks[2], head_dim)
+    queries = projection(place_query, normed, *blocks[2], head_dim)
 
     keep = (1 - resets[0, 0]).astype(F32)
     upto = jnp.triu(jnp.ones((span, span), F32))
@@ -248,11 +266,7 @@
     attended = add_read(queries, entering, decay.T, window)
 
     if paired:
-        first, second = blocks[3][1:]
-        group = lax.axis_index("groups")
-        other = jnp.concatenate(
-            [jnp.where(group == 0, first, second), jnp.where(group == 0, second, first)], axis=0
-        )
+        other = in_order(group, output_x, output_y)
         mine = jnp.where(side == core, w_output, other)
         theirs = jnp.where(side == core, other, w_output)
     else:

time: 179 us -> 165 us (0.922)
  waiting for transfers between devices: 54.4 us -> 41.5 us
  local copies, waits for them, and re-layouts: 23.9 us -> 19.3 us
  starting transfers between devices: 17 us -> 18.8 us
    ppermute x10 -> x2, waiting for transfers between devices: 49.8 us -> 2.65 us  [around(): lax.ppermute(value, axis, [(i, (i + 1) % count) for i in range(count)])]
    ppermute x0 -> x9, waiting for transfers between devices: none -> 33.6 us  [swapped(): lax.ppermute(value, axis, [(i, i + 1 - 2 * (i % 2)) for i in range(count)])]
    ppermute x0 -> x9, starting transfers between devices: none -> 14.1 us  [swapped(): lax.ppermute(value, axis, [(i, i + 1 - 2 * (i % 2)) for i in range(count)])]
    ppermute x10 -> x2, starting transfers between devices: 12.5 us -> 0.07 us  [around(): lax.ppermute(value, axis, [(i, (i + 1) % count) for i in range(count)])]
    all_gather x1, waiting for transfers between devices: 0.01 us -> 3.4 us  [shards(): lax.all_gather(jnp.concatenate([local_state, small], axis=1), 'seq')]
    select_n x1 -> x2, other arithmetic: 1.83 us -> 4.72 us  [in_order(): jnp.where(index == 0, first, second)]
    ppermute x1, waiting for transfers between devices: 4.6 us -> 1.86 us  [shifted(): return lax.ppermute(value, axis, [(i, i + 1) for i in range(count - 1)])]
    dynamic_slice x4, local copies, waits for them, and re-layouts: 8.13 us -> 5.42 us  [part_of(): return lax.dynamic_slice_in_dim(block, index * rows, rows, 0)]
  transfers between devices with their start and end apart: 12 -> 13, of which waited for: 7 -> 8; matrix products, arithmetic and copies ran while one was open for 17% -> 15% of each run, Pallas kernels for 24% -> 21%
where the time goes in v4:
time: 165 us; the launch traced here: 164 us
  waiting for transfers between devices  41.5 us (25%)
  Pallas kernels  41.5 us (25%)
  other arithmetic  22.1 us (13%)
  local copies, waits for them, and re-layouts  19.3 us (12%)
  starting transfers between devices  18.8 us (11%)
  between operations  14.4 us (9%)
  matrix products  6.31 us (4%)
    ppermute x9, waiting for transfers between devices, swapped(): lax.ppermute(value, axis, [(i, i + 1 - 2 * (i % 2)) for i in range(count)])  33.6 us
    pallas_call x3, Pallas kernels, projection(): pl.pallas_call(functools.partial(projection_kernel, head_dim), grid=(inne...  17.8 us
    ppermute x9, starting transfers between devices, swapped(): lax.ppermute(value, axis, [(i, i + 1 - 2 * (i % 2)) for i in range(count)])  14.1 us
    pallas_call x1, Pallas kernels, window_mix(): pl.pallas_call(functools.partial(window_kernel, scale), grid=(inner // he...  10.4 us
    unnamed x42, local copies, waits for them, and re-layouts  10.4 us
    concatenate x1, other arithmetic, shards(): both = jnp.concatenate([prior, normed], axis=0)  8.19 us
    pallas_call x1, Pallas kernels, local_states(): pl.pallas_call(state_kernel, grid=(heads,), in_specs=[block, block, pl.Bl...  6.77 us
    pallas_call x1, Pallas kernels, add_read(): pl.pallas_call(read_kernel, grid=(heads,), in_specs=[block, pl.BlockSpec(...  6.5 us
  transfers between devices with their start and end apart: 13, of which 8 were waited for; matrix products, arithmetic and copies ran while one was open for 15% of the time, Pallas kernels for 21%

profile of v4, /device:TPU:0, one launch (start us, length us, event | category | flops | bytes accessed | tf_op | source)
XLA Modules:
  0.0 164.0 jit_solution(12710444585480931235)
XLA Ops:
  6.5 3.6 %copy.74 = bf16[128,8,2,1024]{3,1,2,0:T(8,128)(2,1)S(1)} copy(bf16[128,8,2,1024]{3,2,1,0:T(2,128)(2,1)} %bitcast.62) | data formatting | bytes 8388608
  10.2 1.8 %fusion.40 = (bf16[1024,1024]{1,0:T(8,128)(2,1)S(1)}, bf16[1024,1024]{1,0:T(8,128)(2,1)}) fusion(bf16[1024,2048]{1,0:T(8,128)(2,1)S(1)} %bitcast.61), kind=kLoop, calls=%fused_computation.83 | loop fusion | bytes 8388608 | tf_op jit(solution)/shard_map/slice | solution.py:209
  12.0 1.1 constant_dynamic-slice_fusion.2
  13.0 2.9 %collective-permute-start = (bf16[512,1024]{1,0:T(8,128)(2,1)}, bf16[512,1024]{1,0:T(8,128)(2,1)S(1)}, u32[]{:S(2)}, u32[]{:S(2)}) collective-permute-start(bf16[512,1024]{1,0:T(8,128)(2,1)} %constant_dynamic-slice_fusion.2), channel_id=1, source_target_pairs={{0,2},{2,0},{1,3},{3,1},{4,6},{6,4},{5,7},{7,5},{8,10},{10,8},{9,1... | collective-permute-start | bytes 3145736 | tf_op jit(solution)/shard_map/ppermute | solution.py:40
  16.0 0.5 fusion
  16.5 0.5 fusion.2.x_ref
  17.0 1.1 constant_dynamic-slice_fusion.1
  18.1 4.6 %collective-permute-start.3 = (bf16[512,1024]{1,0:T(8,128)(2,1)}, bf16[512,1024]{1,0:T(8,128)(2,1)}, u32[]{:S(2)}, u32[]{:S(2)}) collective-permute-start(bf16[512,1024]{1,0:T(8,128)(2,1)} %constant_dynamic-slice_fusion.1), channel_id=1, source_target_pairs={{0,4},{4,8},{8,12},{1,5},{5,9},{9,13},{2,6},{6,10},{10,14},{3,7},{... | collective-permute-start | bytes 3145736 | tf_op jit(solution)/shard_map/ppermute | solution.py:22
  23.4 0.9 fusion.41
  24.4 0.1 copy.65
  24.5 0.1 multiply_reduce_fusion
  24.6 1.9 %constant_dynamic-slice_fusion.3 = bf16[256,1024]{1,0:T(8,128)(2,1)} fusion(bf16[1024,1024]{1,0:T(8,128)(2,1)} %get-tuple-element.24.own_ref, s32[]{:T(128)S(6)} %select_n.117), kind=kLoop, calls=%fused_computation.55 | loop fusion | bytes 1048580 | tf_op jit(solution)/shard_map/dynamic_slice | solution.py:35
  26.5 12.8 %collective-permute-done.first_ref = bf16[512,1024]{1,0:T(8,128)(2,1)S(1)} collective-permute-done((bf16[512,1024]{1,0:T(8,128)(2,1)}, bf16[512,1024]{1,0:T(8,128)(2,1)S(1)}, u32[]{:S(2)}, u32[]{:S(2)}) %collective-permute-start) | collective-permute-done | bytes 1048608 | tf_op jit(solution)/shard_map/ppermute | solution.py:40
  39.3 1.7 %collective-permute-start.1 = (bf16[256,1024]{1,0:T(8,128)(2,1)}, bf16[256,1024]{1,0:T(8,128)(2,1)}, u32[]{:S(2)}, u32[]{:S(2)}) collective-permute-start(bf16[256,1024]{1,0:T(8,128)(2,1)} %constant_dynamic-slice_fusion.3), channel_id=1, source_target_pairs={{0,2},{2,0},{1,3},{3,1},{4,6},{6,4},{5,7},{7,5},{8,10},{10,8},{9,1... | collective-permute-start | bytes 1572872 | tf_op jit(solution)/shard_map/ppermute | solution.py:40
  41.1 1.5 collective-permute-start.8
  42.6 1.9 %collective-permute-done.3 = bf16[512,1024]{1,0:T(8,128)(2,1)} collective-permute-done((bf16[512,1024]{1,0:T(8,128)(2,1)}, bf16[512,1024]{1,0:T(8,128)(2,1)}, u32[]{:S(2)}, u32[]{:S(2)}) %collective-permute-start.3) | collective-permute-done | bytes 1048608 | tf_op jit(solution)/shard_map/ppermute | solution.py:22
  44.5 8.3 %collective-permute-done.1 = bf16[256,1024]{1,0:T(8,128)(2,1)} collective-permute-done((bf16[256,1024]{1,0:T(8,128)(2,1)}, bf16[256,1024]{1,0:T(8,128)(2,1)}, u32[]{:S(2)}, u32[]{:S(2)}) %collective-permute-start.1) | collective-permute-done | bytes 524320 | tf_op jit(solution)/shard_map/ppermute | solution.py:40
  52.8 1.6 collective-permute-start.4
  54.4 0.1 pad_add_fusion.1.place_ref
  54.5 0.1 copy.73
  54.6 2.4 %constant_dynamic-slice_fusion = bf16[512,1024]{1,0:T(8,128)(2,1)} fusion(bf16[1024,1024]{1,0:T(8,128)(2,1)} %param.11, s32[]{:T(128)S(6)} %select_n.118), kind=kLoop, calls=%fused_computation.52 | loop fusion | bytes 2097156 | tf_op jit(solution)/shard_map/dynamic_slice | solution.py:35
  57.0 0.1 constant_dynamic-slice_fusion.4
  57.1 0.8 subtract_exponential_fusion.weight_ref
  57.8 1.5 collective-permute-start.2
  59.3 6.0 %collective-permute-done.4 = bf16[256,1024]{1,0:T(8,128)(2,1)} collective-permute-done((bf16[256,1024]{1,0:T(8,128)(2,1)}, bf16[256,1024]{1,0:T(8,128)(2,1)}, u32[]{:S(2)}, u32[]{:S(2)}) %collective-permute-start.4) | collective-permute-done | bytes 524320 | tf_op jit(solution)/shard_map/ppermute | solution.py:40
  65.3 1.3 broadcast_select_fusion.5
  66.6 0.1 pad_maximum_fusion.4.first_ref
  66.6 1.2 collective-permute-start.9
  67.9 1.7 %broadcast_select_fusion.3 = (bf16[512,1024]{1,0:T(8,128)(2,1)S(1)}, bf16[512,1024]{1,0:T(8,128)(2,1)S(1)}) fusion(bf16[512,1024]{1,0:T(8,128)(2,1)} %collective-permute-done.3, bf16[512,1024]{1,0:T(8,128)(2,1)} %collective-permute-done.7, pred[]{:T(512)S(6)} %eq.18), kind=kLoop, calls=%fused_computation.24 | loop fusion | flops 1048576 | bytes 4194305 | tf_op jit(solution)/shard_map/jit(_where)/select_n | solution.py:236
  69.6 8.2 %pad_maximum_fusion.x_ref = bf16[1024,2048]{1,0:T(8,128)(2,1)S(1)} fusion(bf16[512,2048]{1,0:T(8,128)(2,1)S(1)} %fusion.2.x_ref, bf16[512,1024]{1,0:T(8,128)(2,1)S(1)} %get-tuple-element.28, bf16[512,1024]{1,0:T(8,128)(2,1)S(1)} %get-tuple-element.27), kind=kLoop, calls=%fused_computation.5 | loop fusion | flops 12582912 | bytes 8388608 | tf_op jit(solution)/shard_map/concatenate | solution.py:238
  77.8 3.1 %collective-permute-done.2.first_ref = bf16[512,1024]{1,0:T(8,128)(2,1)} collective-permute-done((bf16[512,1024]{1,0:T(8,128)(2,1)S(1)}, bf16[512,1024]{1,0:T(8,128)(2,1)}, u32[]{:S(2)}, u32[]{:S(2)}) %collective-permute-start.2) | collective-permute-done | bytes 1048608 | tf_op jit(solution)/shard_map/ppermute | solution.py:40
  80.9 1.5 collective-permute-start.6
  82.4 6.9 %shard_map.74.k_ref = bf16[1024,1024]{1,0:T(8,128)(2,1)S(1)} custom-call(s32[2]{0:T(128)S(1)} %pad_add_fusion.1.place_ref, bf16[1024,2048]{1,0:T(8,128)(2,1)S(1)} %pad_maximum_fusion.x_ref, bf16[1024,1024]{1,0:T(8,128)(2,1)S(1)} %copy-done.2, bf16[512,1024]{1,0:T(8,128)(2,1)S(1)} %collective-permute-done.first_ref, ...), custom_call_target="tpu_custom_call" | custom-call | flops 4294967296 | bytes 10485760 | tf_op jit(solution)/shard_map/pallas_call | solution.py:74
  89.4 1.3 copy-done.4
  90.7 0.3 collective-permute-start.5
  91.0 6.2 %shard_map.75.v_ref = bf16[1024,1024]{1,0:T(8,128)(2,1)S(1)} custom-call(s32[2]{0:T(128)S(1)} %pad_add_fusion.1.place_ref, bf16[1024,2048]{1,0:T(8,128)(2,1)S(1)} %pad_maximum_fusion.x_ref, bf16[1024,1024]{1,0:T(8,128)(2,1)S(1)} %copy-done.3, bf16[512,1024]{1,0:T(8,128)(2,1)S(1)} %pad_maximum_fusion.4.first_ref, ...), custom_call_target="tpu_custom_call" | custom-call | flops 4294967296 | bytes 10485760 | tf_op jit(solution)/shard_map/pallas_call | solution.py:74
  97.3 1.4 copy-done.6
  98.7 6.8 %shard_map.76 = bf16[8,128,128]{2,1,0:T(8,128)(2,1)} custom-call(bf16[1024,1024]{1,0:T(8,128)(2,1)} %copy-done.4, bf16[1024,1024]{1,0:T(8,128)(2,1)} %copy-done.6, f32[512,8]{1,0:T(8,128)} %subtract_exponential_fusion.weight_ref), custom_call_target="tpu_custom_call" | custom-call | tf_op jit(solution)/shard_map/pallas_call | solution.py:109
  105.5 0.1 broadcast_in_dim.26
  105.5 1.7 %pad_maximum_fusion.5 = bf16[8,144,128]{2,1,0:T(8,128)(2,1)} fusion(bf16[8,16,128]{2,1,0:T(8,128)(2,1)S(1)} %broadcast_in_dim.26, bf16[8,128,128]{2,1,0:T(8,128)(2,1)} %shard_map.76), kind=kLoop, calls=%fused_computation.39 | loop fusion | flops 589824 | bytes 589824 | tf_op jit(solution)/shard_map/concatenate | solution.py:253
  107.2 0.0 all-gather.3.cloned.1.call-update
  107.3 1.7 %collective-permute-start.10 = (bf16[512,1024]{1,0:T(8,128)(2,1)}, bf16[512,1024]{1,0:T(8,128)(2,1)}, u32[]{:S(2)}, u32[]{:S(2)}) collective-permute-start(bf16[512,1024]{1,0:T(8,128)(2,1)} %collective-permute-done.6), channel_id=1, source_target_pairs={{0,16},{16,0},{1,17},{17,1},{2,18},{18,2},{3,19},{19,3},{4,20},{20... | collective-permute-start | bytes 3145736 | tf_op jit(solution)/shard_map/ppermute | solution.py:40
  109.0 0.1 copy.72
  109.1 0.1 pad_add_fusion.place_ref
  109.2 3.3 %collective-permute-done.5.second_ref = bf16[512,1024]{1,0:T(8,128)(2,1)S(1)} collective-permute-done((bf16[512,1024]{1,0:T(8,128)(2,1)}, bf16[512,1024]{1,0:T(8,128)(2,1)S(1)}, u32[]{:S(2)}, u32[]{:S(2)}) %collective-permute-start.5) | collective-permute-done | bytes 1048608 | tf_op jit(solution)/shard_map/ppermute | solution.py:40
  112.5 1.0 copy-done.12
  113.5 1.7 %copy-done.11 = bf16[1024,1024]{1,0:T(8,128)(2,1)S(1)} copy-done((bf16[1024,1024]{1,0:T(8,128)(2,1)S(1)}, bf16[1024,1024]{1,0:T(8,128)(2,1)}, u32[]{:S(2)}) %copy-start.11) | copy-done | bytes 2097176
  115.2 1.2 copy-done.13
  116.4 4.6 %shard_map.73.q_ref = bf16[512,1024]{1,0:T(8,128)(2,1)S(1)} custom-call(s32[2]{0:T(128)S(1)} %pad_add_fusion.place_ref, bf16[512,2048]{1,0:T(8,128)(2,1)S(1)} %fusion.2.x_ref, bf16[1024,1024]{1,0:T(8,128)(2,1)S(1)} %copy-done.11, bf16[512,1024]{1,0:T(8,128)(2,1)} %collective-permute-done.2.first_ref, bf16[512,1024]{1,0:T(8,128)(2,1)S(1)} %copy-done.13), custom_call_target="tpu_custom_call" | custom-call | flops 2147483648 | bytes 7340032 | tf_op jit(solution)/shard_map/pallas_call | solution.py:74
  121.1 0.0 copy-start.9
  121.1 10.4 %shard_map.77.window_ref = f32[512,1024]{1,0:T(8,128)S(1)} custom-call(f32[1,1]{1,0:T(1,128)} %bitcast.22.allow_ref, bf16[512,1024]{1,0:T(8,128)(2,1)S(1)} %shard_map.73.q_ref, bf16[1024,1024]{1,0:T(8,128)(2,1)S(1)} %copy-done.5, bf16[1024,1024]{1,0:T(8,128)(2,1)S(1)} %copy-done.7), custom_call_target="tpu_custom_call" | custom-call | flops 2147483648 | bytes 7340032 | tf_op jit(solution)/shard_map/pallas_call | solution.py:145
  131.6 3.4 %broadcast_select_fusion.1 = (bf16[512,1024]{1,0:T(8,128)(2,1)S(1)}, bf16[512,1024]{1,0:T(8,128)(2,1)}) fusion(bf16[512,1024]{1,0:T(8,128)(2,1)} %collective-permute-done.6, bf16[512,1024]{1,0:T(8,128)(2,1)} %collective-permute-done.10, pred[]{:T(512)S(6)} %eq.21), kind=kLoop, calls=%fused_computation.22 | loop fusion | flops 1048576 | bytes 4194305 | tf_op jit(solution)/shard_map/jit(_where)/select_n | solution.py:45
  135.0 3.4 %all-gather.3.cloned.1.call-done = bf16[32,144,128]{2,1,0:T(8,128)(2,1)} async-done(((bf16[8,144,128]{2,1,0:T(8,128)(2,1)}), bf16[32,144,128]{2,1,0:T(8,128)(2,1)}) %all-gather.3.cloned.1.call-update) | async-done | bytes 1179664 | tf_op jit(solution)/shard_map/all_gather | solution.py:253
  138.4 0.8 slice_convert_fusion.2
  139.2 0.1 copy.69
  139.3 0.1 copy.70
  139.4 0.1 copy.71
  139.5 0.8 broadcast_divide_fusion.decay_ref
  140.3 2.2 %fusion.22.state_ref = bf16[8,128,128]{2,1,0:T(8,128)(2,1)} fusion(bf16[4,8,144,128]{3,2,1,0:T(8,128)(2,1)} %bitcast.65, f32[]{:T(128)} %bitcast.9, f32[8]{0:T(128)S(1)} %get-tuple-element.38, f32[8]{0:T(128)S(1)} %get-tuple-element.42, f32[8]{0:T(128)S(1)} %get-tuple-element.41, pred[]{:T(512)S(6)} %gt.15, pred[]{:T(512)S(6)} %gt.14, pred[]{:T(512)S(6)} %gt.13), kind=kLoop, calls=%fused_computation.28 | loop fusion | flops 1703936 | bytes 1048679 | tf_op jit(solution)/shard_map/convert_element_type | solution.py:262
  142.5 6.5 %shard_map.78 = bf16[512,1024]{1,0:T(8,128)(2,1)} custom-call(bf16[512,1024]{1,0:T(8,128)(2,1)} %copy-done.9, bf16[8,128,128]{2,1,0:T(8,128)(2,1)} %fusion.22.state_ref, f32[512,8]{1,0:T(8,128)} %broadcast_divide_fusion.decay_ref, f32[512,1024]{1,0:T(8,128)} %copy-done.8), custom_call_target="tpu_custom_call" | custom-call | tf_op jit(solution)/shard_map/pallas_call | solution.py:176
  149.0 3.0 %fusion.10 = bf16[512,1024]{1,0:T(8,128)(2,1)S(1)} fusion(bf16[512,1024]{1,0:T(8,128)(2,1)} %shard_map.78, bf16[1024,1024]{1,0:T(8,128)(2,1)} %param.11, pred[]{:T(512)S(6)} %eq.20, bf16[512,1024]{1,0:T(8,128)(2,1)} %get-tuple-element.26, bf16[512,1024]{1,0:T(8,128)(2,1)S(1)} %get-tuple-element.25), kind=kOutput, calls=%fused_computation.15 | convolution fusion | flops 1079508992 | bytes 6291457 | tf_op jit(solution)/shard_map/dot_general | solution.py:277
  152.0 0.1 collective-permute-start.11
  152.1 2.6 %collective-permute-done.11 = bf16[512,1024]{1,0:T(8,128)(2,1)S(1)} collective-permute-done((bf16[512,1024]{1,0:T(8,128)(2,1)S(1)}, bf16[512,1024]{1,0:T(8,128)(2,1)S(1)}, u32[]{:S(2)}, u32[]{:S(2)}) %collective-permute-start.11) | collective-permute-done | bytes 1048608 | tf_op jit(solution)/shard_map/ppermute | solution.py:17
  154.7 2.4 %fusion.15 = bf16[1,512,1024]{2,1,0:T(8,128)(2,1)} fusion(bf16[512,1024]{1,0:T(8,128)(2,1)S(1)} %collective-permute-done.11, bf16[512,1024]{1,0:T(8,128)(2,1)S(1)} %copy-done.17, bf16[1024,1024]{1,0:T(8,128)(2,1)S(1)} %copy-done.18, pred[]{:T(512)S(6)} %eq.20, bf16[512,1024]{1,0:T(8,128)(2,1)S(1)} %copy-done.16, ...), kind=kOutput, calls=%fused_computation.16 | convolution fusion | flops 1081606144 | bytes 8388613 | tf_op jit(solution)/shard_map/dot_general | solution.py:279
  (50 shorter events, 0.2 us)
Async XLA Ops:
  6.5 16.9 %copy-start = (f32[1,8,512]{2,1,0:T(8,128)S(1)}, f32[1,8,512]{2,1,0:T(8,128)}, u32[]{:S(2)}) copy-start(f32[1,8,512]{2,1,0:T(8,128)} %param.12) | copy-start | bytes 49156
  6.5 131.9 %all-gather.3.cloned.1.call-start = ((), (), s32[]{:S(2)}) async-start(), calls=%async_computation | async-start | bytes 1474560 | tf_op jit(solution)/shard_map/all_gather | solution.py:253
  12.0 4.5 %copy-start.1 = (bf16[1024,1024]{1,0:T(8,128)(2,1)}, bf16[1024,1024]{1,0:T(8,128)(2,1)S(1)}, u32[]{:S(2)}) copy-start(bf16[1024,1024]{1,0:T(8,128)(2,1)S(1)} %get-tuple-element.23.own_ref) | copy-start | bytes 6291460
  12.0 4.0 %copy-start.14 = (bf16[1,512,2048]{2,1,0:T(8,128)(2,1)S(1)}, bf16[1,512,2048]{2,1,0:T(8,128)(2,1)}, u32[]{:S(2)}) copy-start(bf16[1,512,2048]{2,1,0:T(8,128)(2,1)} %param.7) | copy-start | bytes 6291460
  12.0 4.5 %copy-start.19 = (f32[2048]{0:T(1024)S(1)}, f32[2048]{0:T(1024)}, u32[]{:S(2)}) copy-start(f32[2048]{0:T(1024)} %param.8) | copy-start | bytes 24580
  13.0 26.3 %collective-permute-start = (bf16[512,1024]{1,0:T(8,128)(2,1)}, bf16[512,1024]{1,0:T(8,128)(2,1)S(1)}, u32[]{:S(2)}, u32[]{:S(2)}) collective-permute-start(bf16[512,1024]{1,0:T(8,128)(2,1)} %constant_dynamic-slice_fusion.2), channel_id=1, source_target_pairs={{0,2},{2,0},{1,3},{3,1},{4,6},{6,4},{5,7},{7,5},{8,10},{10,8},{9,1... | collective-permute-start | bytes 3145736 | tf_op jit(solution)/shard_map/ppermute | solution.py:40
  18.1 26.4 %collective-permute-start.3 = (bf16[512,1024]{1,0:T(8,128)(2,1)}, bf16[512,1024]{1,0:T(8,128)(2,1)}, u32[]{:S(2)}, u32[]{:S(2)}) collective-permute-start(bf16[512,1024]{1,0:T(8,128)(2,1)} %constant_dynamic-slice_fusion.1), channel_id=1, source_target_pairs={{0,4},{4,8},{8,12},{1,5},{5,9},{9,13},{2,6},{6,10},{10,14},{3,7},{... | collective-permute-start | bytes 3145736 | tf_op jit(solution)/shard_map/ppermute | solution.py:22
  39.3 13.4 %collective-permute-start.1 = (bf16[256,1024]{1,0:T(8,128)(2,1)}, bf16[256,1024]{1,0:T(8,128)(2,1)}, u32[]{:S(2)}, u32[]{:S(2)}) collective-permute-start(bf16[256,1024]{1,0:T(8,128)(2,1)} %constant_dynamic-slice_fusion.3), channel_id=1, source_target_pairs={{0,2},{2,0},{1,3},{3,1},{4,6},{6,4},{5,7},{7,5},{8,10},{10,8},{9,1... | collective-permute-start | bytes 1572872 | tf_op jit(solution)/shard_map/ppermute | solution.py:40
  41.1 25.5 %collective-permute-start.8 = (bf16[512,1024]{1,0:T(8,128)(2,1)S(1)}, bf16[512,1024]{1,0:T(8,128)(2,1)}, u32[]{:S(2)}, u32[]{:S(2)}) collective-permute-start(bf16[512,1024]{1,0:T(8,128)(2,1)S(1)} %collective-permute-done.first_ref), channel_id=1, source_target_pairs={{0,16},{16,0},{1,17},{17,1},{2,18},{18,2},{3,19},{19,3},{4,20},{20... | collective-permute-start | bytes 3145736 | tf_op jit(solution)/shard_map/ppermute | solution.py:40
  44.5 23.4 %collective-permute-start.7 = (bf16[512,1024]{1,0:T(8,128)(2,1)}, bf16[512,1024]{1,0:T(8,128)(2,1)}, u32[]{:S(2)}, u32[]{:S(2)}) collective-permute-start(bf16[512,1024]{1,0:T(8,128)(2,1)} %collective-permute-done.3), channel_id=1, source_target_pairs={{0,1},{1,0},{2,3},{3,2},{4,5},{5,4},{6,7},{7,6},{8,9},{9,8},{10,11... | collective-permute-start | bytes 3145736 | tf_op jit(solution)/shard_map/ppermute | solution.py:17
  52.8 12.5 %collective-permute-start.4 = (bf16[256,1024]{1,0:T(8,128)(2,1)}, bf16[256,1024]{1,0:T(8,128)(2,1)}, u32[]{:S(2)}, u32[]{:S(2)}) collective-permute-start(bf16[256,1024]{1,0:T(8,128)(2,1)} %collective-permute-done.1), channel_id=1, source_target_pairs={{0,4},{4,0},{8,12},{12,8},{1,5},{5,1},{9,13},{13,9},{2,6},{6,2},{1... | collective-permute-start | bytes 1572872 | tf_op jit(solution)/shard_map/ppermute | solution.py:40
  54.6 2.4 %copy-start.10 = (bf16[1024,1024]{1,0:T(8,128)(2,1)S(1)}, bf16[1024,1024]{1,0:T(8,128)(2,1)}, u32[]{:S(2)}) copy-start(bf16[1024,1024]{1,0:T(8,128)(2,1)} %own_ref.1) | copy-start | bytes 6291460
  57.8 23.1 %collective-permute-start.2 = (bf16[512,1024]{1,0:T(8,128)(2,1)S(1)}, bf16[512,1024]{1,0:T(8,128)(2,1)}, u32[]{:S(2)}, u32[]{:S(2)}) collective-permute-start(bf16[512,1024]{1,0:T(8,128)(2,1)S(1)} %constant_dynamic-slice_fusion.4), channel_id=1, source_target_pairs={{0,2},{2,0},{1,3},{3,1},{4,6},{6,4},{5,7},{7,5},{8,10},{10,8},{9,1... | collective-permute-start | bytes 3145736 | tf_op jit(solution)/shard_map/ppermute | solution.py:40
  66.6 24.4 %collective-permute-start.9 = (bf16[512,1024]{1,0:T(8,128)(2,1)S(1)}, bf16[512,1024]{1,0:T(8,128)(2,1)S(1)}, u32[]{:S(2)}, u32[]{:S(2)}) collective-permute-start(bf16[512,1024]{1,0:T(8,128)(2,1)S(1)} %pad_maximum_fusion.4.first_ref), channel_id=1, source_target_pairs={{0,16},{16,0},{1,17},{17,1},{2,18},{18,2},{3,19},{19,3},{4,20},{20... | collective-permute-start | bytes 3145736 | tf_op jit(solution)/shard_map/ppermute | solution.py:40
  69.6 12.9 %copy-start.2 = (bf16[1024,1024]{1,0:T(8,128)(2,1)S(1)}, bf16[1024,1024]{1,0:T(8,128)(2,1)}, u32[]{:S(2)}) copy-start(bf16[1024,1024]{1,0:T(8,128)(2,1)} %copy-done.1) | copy-start | bytes 6291460
  77.8 13.3 %copy-start.3 = (bf16[1024,1024]{1,0:T(8,128)(2,1)S(1)}, bf16[1024,1024]{1,0:T(8,128)(2,1)}, u32[]{:S(2)}) copy-start(bf16[1024,1024]{1,0:T(8,128)(2,1)} %get-tuple-element.24.own_ref) | copy-start | bytes 6291460
  80.9 26.3 %collective-permute-start.6 = (bf16[512,1024]{1,0:T(8,128)(2,1)}, bf16[512,1024]{1,0:T(8,128)(2,1)}, u32[]{:S(2)}, u32[]{:S(2)}) collective-permute-start(bf16[512,1024]{1,0:T(8,128)(2,1)} %constant_dynamic-slice_fusion), channel_id=1, source_target_pairs={{0,2},{2,0},{1,3},{3,1},{4,6},{6,4},{5,7},{7,5},{8,10},{10,8},{9,1... | collective-permute-start | bytes 3145736 | tf_op jit(solution)/shard_map/ppermute | solution.py:40
  89.3 1.3 copy-start.4
  90.7 21.9 %collective-permute-start.5 = (bf16[512,1024]{1,0:T(8,128)(2,1)}, bf16[512,1024]{1,0:T(8,128)(2,1)S(1)}, u32[]{:S(2)}, u32[]{:S(2)}) collective-permute-start(bf16[512,1024]{1,0:T(8,128)(2,1)} %collective-permute-done.2.first_ref), channel_id=1, source_target_pairs={{0,4},{4,0},{8,12},{12,8},{1,5},{5,1},{9,13},{13,9},{2,6},{6,2},{1... | collective-permute-start | bytes 3145736 | tf_op jit(solution)/shard_map/ppermute | solution.py:40
  97.3 1.4 copy-start.6
  107.3 24.3 %collective-permute-start.10 = (bf16[512,1024]{1,0:T(8,128)(2,1)}, bf16[512,1024]{1,0:T(8,128)(2,1)}, u32[]{:S(2)}, u32[]{:S(2)}) collective-permute-start(bf16[512,1024]{1,0:T(8,128)(2,1)} %collective-permute-done.6), channel_id=1, source_target_pairs={{0,16},{16,0},{1,17},{17,1},{2,18},{18,2},{3,19},{19,3},{4,20},{20... | collective-permute-start | bytes 3145736 | tf_op jit(solution)/shard_map/ppermute | solution.py:40
  109.2 11.9 %copy-start.5 = (bf16[1024,1024]{1,0:T(8,128)(2,1)S(1)}, bf16[1024,1024]{1,0:T(8,128)(2,1)}, u32[]{:S(2)}) copy-start(bf16[1024,1024]{1,0:T(8,128)(2,1)} %copy-done.4) | copy-start | bytes 6291460
  109.2 11.9 %copy-start.7 = (bf16[1024,1024]{1,0:T(8,128)(2,1)S(1)}, bf16[1024,1024]{1,0:T(8,128)(2,1)}, u32[]{:S(2)}) copy-start(bf16[1024,1024]{1,0:T(8,128)(2,1)} %copy-done.6) | copy-start | bytes 6291460
  112.5 1.0 copy-start.12
  113.5 1.7 %copy-start.11 = (bf16[1024,1024]{1,0:T(8,128)(2,1)S(1)}, bf16[1024,1024]{1,0:T(8,128)(2,1)}, u32[]{:S(2)}) copy-start(bf16[1024,1024]{1,0:T(8,128)(2,1)} %own_ref.1) | copy-start | bytes 6291460
  115.2 1.2 copy-start.13
  121.1 10.5 %copy-start.9 = (bf16[512,1024]{1,0:T(8,128)(2,1)}, bf16[512,1024]{1,0:T(8,128)(2,1)S(1)}, u32[]{:S(2)}) copy-start(bf16[512,1024]{1,0:T(8,128)(2,1)S(1)} %shard_map.73.q_ref) | copy-start | bytes 3145732
  131.6 3.5 %copy-start.8 = (f32[512,1024]{1,0:T(8,128)}, f32[512,1024]{1,0:T(8,128)S(1)}, u32[]{:S(2)}) copy-start(f32[512,1024]{1,0:T(8,128)S(1)} %shard_map.77.window_ref) | copy-start | bytes 6291460
  149.0 5.7 %copy-start.15 = (bf16[1,512,2048]{2,1,0:T(8,128)(2,1)S(1)}, bf16[1,512,2048]{2,1,0:T(8,128)(2,1)}, u32[]{:S(2)}) copy-start(bf16[1,512,2048]{2,1,0:T(8,128)(2,1)} %param.7) | copy-start | bytes 6291460
  149.0 5.7 %copy-start.16 = (bf16[512,1024]{1,0:T(8,128)(2,1)S(1)}, bf16[512,1024]{1,0:T(8,128)(2,1)}, u32[]{:S(2)}) copy-start(bf16[512,1024]{1,0:T(8,128)(2,1)} %get-tuple-element.26) | copy-start | bytes 3145732
  149.0 5.7 %copy-start.17 = (bf16[512,1024]{1,0:T(8,128)(2,1)S(1)}, bf16[512,1024]{1,0:T(8,128)(2,1)}, u32[]{:S(2)}) copy-start(bf16[512,1024]{1,0:T(8,128)(2,1)} %shard_map.78) | copy-start | bytes 3145732
  149.0 5.7 %copy-start.18 = (bf16[1024,1024]{1,0:T(8,128)(2,1)S(1)}, bf16[1024,1024]{1,0:T(8,128)(2,1)}, u32[]{:S(2)}) copy-start(bf16[1024,1024]{1,0:T(8,128)(2,1)} %param.11) | copy-start | bytes 6291460
  152.0 2.7 %collective-permute-start.11 = (bf16[512,1024]{1,0:T(8,128)(2,1)S(1)}, bf16[512,1024]{1,0:T(8,128)(2,1)S(1)}, u32[]{:S(2)}, u32[]{:S(2)}) collective-permute-start(bf16[512,1024]{1,0:T(8,128)(2,1)S(1)} %fusion.10), channel_id=1, source_target_pairs={{0,1},{1,0},{2,3},{3,2},{4,5},{5,4},{6,7},{7,6},{8,9},{9,8},{10,11... | collective-permute-start | bytes 3145736 | tf_op jit(solution)/shard_map/ppermute | solution.py:17
Sparse Core Ops, SparseCore 0:
  107.4 31.0 all-gather.2

commit v5 on v4

--- a/solution.py
+++ b/solution.py
@@ -46,29 +46,34 @@
     )
 
 
-def projection_kernel(head_dim, place_ref, x_ref, own_ref, first_ref, second_ref, out_ref):
+def projection_kernel(head_dim, place_ref, own_ref, first_ref, second_ref, *refs):
+    out_ref = refs[-1]
     side, group = place_ref[0], place_ref[1]
     deep, part = own_ref.shape[0], first_ref.shape[0]
-
-    def columns(start, size):
-        return x_ref[:, pl.ds(pl.multiple_of(start, 128), size)]
-
-    total = jnp.dot(columns(side * deep, deep), own_ref[...], preferred_element_type=F32)
     base = (1 - side) * deep
-    total += jnp.dot(columns(base + group * part, part), first_ref[...], preferred_element_type=F32)
-    total += jnp.dot(
-        columns(base + (1 - group) * part, part), second_ref[...], preferred_element_type=F32
-    )
-    if not head_dim:
-        out_ref[...] = total.astype(BF16)
-        return
-    for start in range(0, total.shape[1], head_dim):
-        head = total[:, start : start + head_dim]
-        out_ref[:, start : start + head_dim] = rms_rows(head, 1e-06).astype(BF16)
+    row = 0
+    for x_ref in refs[:-1]:
+
+        def product(start, w_ref):
+            columns = x_ref[:, pl.ds(pl.multiple_of(start, 128), w_ref.shape[0])]
+            return jnp.dot(columns, w_ref[...], preferred_element_type=F32)
+
+        total = product(side * deep, own_ref)
+        total += product(base + group * part, first_ref)
+        total += product(base + (1 - group) * part, second_ref)
+        there = slice(row, row + x_ref.shape[0])
+        row += x_ref.shape[0]
+        if not head_dim:
+            out_ref[there, :] = total.astype(BF16)
+            continue
+        for start in range(0, total.shape[1], head_dim):
+            head = total[:, start : start + head_dim]
+            out_ref[there, start : start + head_dim] = rms_rows(head, 1e-06).astype(BF16)
 
 
 def projection(place, rows, own, first, second, head_dim):
-    count, width = rows.shape
+    width = rows[0].shape[1]
+    count = sum(block.shape[0] for block in rows)
     inner = own.shape[1]
     tile = 256
     return pl.pallas_call(
@@ -76,11 +81,11 @@
         grid=(inner // tile,),
         in_specs=[
             pl.BlockSpec(memory_space=pltpu.SMEM),
-            pl.BlockSpec((count, width), lambda c: (0, 0)),
             pl.BlockSpec((own.shape[0], tile), lambda c: (0, c)),
             pl.BlockSpec((first.shape[0], tile), lambda c: (0, c)),
             pl.BlockSpec((second.shape[0], tile), lambda c: (0, c)),
-        ],
+        ]
+        + [pl.BlockSpec(block.shape, lambda c: (0, 0)) for block in rows],
         out_specs=pl.BlockSpec((count, tile), lambda c: (0, c)),
         out_shape=jax.ShapeDtypeStruct((count, inner), BF16),
         compiler_params=pltpu.CompilerParams(vmem_limit_bytes=32 << 20),
@@ -89,28 +94,35 @@
             bytes_accessed=2 * (count * width + width * inner + count * inner),
             transcendentals=0,
         ),
-    )(place, rows, own, first, second)
+    )(place, own, first, second, *rows)
+
+
+def head_column(values, head):
+    column = lax.broadcasted_iota(jnp.int32, values.shape, 1)
+    return jnp.sum(jnp.where(column == head, values, 0.0), axis=-1, keepdims=True)
 
 
 def state_kernel(k_ref, v_ref, weight_ref, out_ref):
-    head = pl.program_id(0)
+    count, head_dim = out_ref.shape[:2]
     weight = weight_ref[...]
-    column = lax.broadcasted_iota(jnp.int32, weight.shape, 1)
-    mine = jnp.sum(jnp.where(column == head, weight, 0.0), axis=-1, keepdims=True)
-    faded = (k_ref[...].astype(F32) * mine).astype(BF16)
-    out_ref[0] = lax.dot_general(
-        faded, v_ref[...], (((0,), (0,)), ((), ())), preferred_element_type=F32
-    ).astype(BF16)
+    for h in range(count):
+        mine = head_column(weight, pl.program_id(0) * count + h)
+        here = slice(h * head_dim, (h + 1) * head_dim)
+        faded = (k_ref[:, here].astype(F32) * mine).astype(BF16)
+        out_ref[h] = lax.dot_general(
+            faded, v_ref[:, here], (((0,), (0,)), ((), ())), preferred_element_type=F32
+        ).astype(BF16)
 
 
 def local_states(keys, values, weight, head_dim):
     span, heads = weight.shape
-    block = pl.BlockSpec((span, head_dim), lambda h: (1, h))
+    step = math.gcd(heads, 4)
+    block = pl.BlockSpec((span, step * head_dim), lambda h: (1, h))
     return pl.pallas_call(
         state_kernel,
-        grid=(heads,),
+        grid=(heads // step,),
         in_specs=[block, block, pl.BlockSpec((span, heads), lambda h: (0, 0))],
-        out_specs=pl.BlockSpec((1, head_dim, head_dim), lambda h: (h, 0, 0)),
+        out_specs=pl.BlockSpec((step, head_dim, head_dim), lambda h: (h, 0, 0)),
         out_shape=jax.ShapeDtypeStruct((heads, head_dim, head_dim), BF16),
     )(keys, values, weight)
 
@@ -161,24 +173,26 @@
 
 
 def read_kernel(q_ref, state_ref, decay_ref, window_ref, out_ref):
-    head = pl.program_id(0)
+    count, head_dim = state_ref.shape[:2]
     decay = decay_ref[...]
-    column = lax.broadcasted_iota(jnp.int32, decay.shape, 1)
-    mine = jnp.sum(jnp.where(column == head, decay, 0.0), axis=-1, keepdims=True)
-    read = jnp.dot(q_ref[...], state_ref[0], preferred_element_type=F32)
-    out_ref[...] = (window_ref[...] + mine * read).astype(BF16)
+    for h in range(count):
+        mine = head_column(decay, pl.program_id(0) * count + h)
+        here = slice(h * head_dim, (h + 1) * head_dim)
+        read = jnp.dot(q_ref[:, here], state_ref[h], preferred_element_type=F32)
+        out_ref[:, here] = (window_ref[:, here] + mine * read).astype(BF16)
 
 
 def add_read(queries, states, decay, window):
     span, inner = queries.shape
     heads, head_dim = states.shape[:2]
-    block = pl.BlockSpec((span, head_dim), lambda h: (0, h))
+    step = math.gcd(heads, 4)
+    block = pl.BlockSpec((span, step * head_dim), lambda h: (0, h))
     return pl.pallas_call(
         read_kernel,
-        grid=(heads,),
+        grid=(heads // step,),
         in_specs=[
             block,
-            pl.BlockSpec((1, head_dim, head_dim), lambda h: (h, 0, 0)),
+            pl.BlockSpec((step, head_dim, head_dim), lambda h: (h, 0, 0)),
             pl.BlockSpec((span, heads), lambda h: (0, 0)),
             block,
         ],
@@ -235,10 +249,10 @@
     prior = jnp.concatenate(
         [jnp.where(core == 0, ours, theirs), jnp.where(core == 0, theirs, ours)], axis=1
     )
-    both = jnp.concatenate([prior, normed], axis=0)
+    both = (prior, normed)
     keys = projection(place, both, *blocks[0], head_dim)
     values = projection(place, both, *blocks[1], 0)
-    queries = projection(place_query, normed, *blocks[2], head_dim)
+    queries = projection(place_query, (normed,), *blocks[2], head_dim)
 
     keep = (1 - resets[0, 0]).astype(F32)
     upto = jnp.triu(jnp.ones((span, span), F32))

time: 165 us -> 158 us (0.958)
  waiting for transfers between devices: 41.5 us -> 52.3 us
  other arithmetic: 22.1 us -> 12.9 us
  Pallas kernels: 41.5 us -> 36 us
  local copies, waits for them, and re-layouts: 19.3 us -> 16.1 us
    ppermute x9, waiting for transfers between devices: 33.6 us -> 45.1 us  [swapped(): lax.ppermute(value, axis, [(i, i + 1 - 2 * (i % 2)) for i in range(count)])]
    concatenate x1, other arithmetic: 8.19 us -> 0.18 us  [shards(): jnp.concatenate([jnp.where(core == 0, ours, theirs), jnp.where(core == 0,...]
    pallas_call x2, Pallas kernels: 13.3 us -> 6.71 us  [the longest x1 3.43 us: local_states(): pl.pallas_call(state_kernel, grid=(heads // step,), in_specs=[block, bloc...]
    unnamed x42 -> x38, local copies, waits for them, and re-layouts: 10.4 us -> 8 us
  transfers between devices with their start and end apart: 13 -> 13, of which waited for: 8 -> 9; matrix products, arithmetic and copies ran while one was open for 15% -> 10% of each run, Pallas kernels for 21% -> 21%
where the time goes in v5:
time: 158 us
  waiting for transfers between devices  52.3 us (33%)
  Pallas kernels  36 us (23%)
  starting transfers between devices  19.6 us (12%)
  local copies, waits for them, and re-layouts  16.1 us (10%)
  between operations  14.4 us (9%)
  other arithmetic  12.9 us (8%)
  matrix products  6.31 us (4%)
    ppermute x9, waiting for transfers between devices, swapped(): lax.ppermute(value, axis, [(i, i + 1 - 2 * (i % 2)) for i in range(count)])  45.1 us
    pallas_call x3, Pallas kernels, projection(): pl.pallas_call(functools.partial(projection_kernel, head_dim), grid=(inne...  18.8 us
    ppermute x9, starting transfers between devices, swapped(): lax.ppermute(value, axis, [(i, i + 1 - 2 * (i % 2)) for i in range(count)])  14.3 us
    pallas_call x1, Pallas kernels, window_mix(): pl.pallas_call(functools.partial(window_kernel, scale), grid=(inner // he...  10.4 us
    unnamed x38, local copies, waits for them, and re-layouts  8 us
    ppermute x1, starting transfers between devices, shifted(): return lax.ppermute(value, axis, [(i, i + 1) for i in range(count - 1)])  5.17 us
    dynamic_slice x4, local copies, waits for them, and re-layouts, part_of(): return lax.dynamic_slice_in_dim(block, index * rows, rows, 0)  4.65 us
    select_n x2, other arithmetic, in_order(): jnp.where(index == 0, first, second)  3.48 us
  transfers between devices with their start and end apart: 13, of which 9 were waited for; matrix products, arithmetic and copies ran while one was open for 10% of the time, Pallas kernels for 21%

profile of v5, /device:TPU:0, one launch (start us, length us, event | category | flops | bytes accessed | tf_op | source)
XLA Modules:
  0.0 157.5 jit_solution(17323077206015582389)
XLA Ops:
  6.5 3.6 %copy.74 = bf16[128,8,2,1024]{3,1,2,0:T(8,128)(2,1)S(1)} copy(bf16[128,8,2,1024]{3,2,1,0:T(2,128)(2,1)} %bitcast.62) | data formatting | bytes 8388608
  10.2 1.7 %fusion.40 = (bf16[1024,1024]{1,0:T(8,128)(2,1)S(1)}, bf16[1024,1024]{1,0:T(8,128)(2,1)}) fusion(bf16[1024,2048]{1,0:T(8,128)(2,1)S(1)} %bitcast.61), kind=kLoop, calls=%fused_computation.83 | loop fusion | bytes 8388608 | tf_op jit(solution)/shard_map/slice | solution.py:223
  11.9 0.1 constant_dynamic-slice_fusion.2
  12.0 3.0 %collective-permute-start = (bf16[512,1024]{1,0:T(8,128)(2,1)S(1)}, bf16[512,1024]{1,0:T(8,128)(2,1)}, u32[]{:S(2)}, u32[]{:S(2)}) collective-permute-start(bf16[512,1024]{1,0:T(8,128)(2,1)S(1)} %constant_dynamic-slice_fusion.2), channel_id=1, source_target_pairs={{0,2},{2,0},{1,3},{3,1},{4,6},{6,4},{5,7},{7,5},{8,10},{10,8},{9,1... | collective-permute-start | bytes 3145736 | tf_op jit(solution)/shard_map/ppermute | solution.py:40
  15.0 0.5 fusion
  15.5 0.5 fusion.2.refs_0_.refs_1_
  16.1 1.1 constant_dynamic-slice_fusion.1
  17.1 5.2 %collective-permute-start.3 = (bf16[512,1024]{1,0:T(8,128)(2,1)}, bf16[512,1024]{1,0:T(8,128)(2,1)}, u32[]{:S(2)}, u32[]{:S(2)}) collective-permute-start(bf16[512,1024]{1,0:T(8,128)(2,1)} %constant_dynamic-slice_fusion.1), channel_id=1, source_target_pairs={{0,4},{4,8},{8,12},{1,5},{5,9},{9,13},{2,6},{6,10},{10,14},{3,7},{... | collective-permute-start | bytes 3145736 | tf_op jit(solution)/shard_map/ppermute | solution.py:22
  23.0 0.9 fusion.41
  23.9 0.1 copy.65
  24.1 1.1 constant_dynamic-slice_fusion.3
  25.2 13.1 %collective-permute-done.first_ref = bf16[512,1024]{1,0:T(8,128)(2,1)} collective-permute-done((bf16[512,1024]{1,0:T(8,128)(2,1)S(1)}, bf16[512,1024]{1,0:T(8,128)(2,1)}, u32[]{:S(2)}, u32[]{:S(2)}) %collective-permute-start) | collective-permute-done | bytes 1048608 | tf_op jit(solution)/shard_map/ppermute | solution.py:40
  38.3 1.7 %collective-permute-start.1 = (bf16[256,1024]{1,0:T(8,128)(2,1)S(1)}, bf16[256,1024]{1,0:T(8,128)(2,1)S(1)}, u32[]{:S(2)}, u32[]{:S(2)}) collective-permute-start(bf16[256,1024]{1,0:T(8,128)(2,1)S(1)} %constant_dynamic-slice_fusion.3), channel_id=1, source_target_pairs={{0,2},{2,0},{1,3},{3,1},{4,6},{6,4},{5,7},{7,5},{8,10},{10,8},{9,1... | collective-permute-start | bytes 1572872 | tf_op jit(solution)/shard_map/ppermute | solution.py:40
  40.0 0.1 multiply_reduce_fusion
  40.1 1.6 %collective-permute-start.7 = (bf16[512,1024]{1,0:T(8,128)(2,1)}, bf16[512,1024]{1,0:T(8,128)(2,1)}, u32[]{:S(2)}, u32[]{:S(2)}) collective-permute-start(bf16[512,1024]{1,0:T(8,128)(2,1)} %collective-permute-done.first_ref), channel_id=1, source_target_pairs={{0,16},{16,0},{1,17},{17,1},{2,18},{18,2},{3,19},{19,3},{4,20},{20... | collective-permute-start | bytes 3145736 | tf_op jit(solution)/shard_map/ppermute | solution.py:40
  41.7 2.4 %collective-permute-done.3 = bf16[512,1024]{1,0:T(8,128)(2,1)} collective-permute-done((bf16[512,1024]{1,0:T(8,128)(2,1)}, bf16[512,1024]{1,0:T(8,128)(2,1)}, u32[]{:S(2)}, u32[]{:S(2)}) %collective-permute-start.3) | collective-permute-done | bytes 1048608 | tf_op jit(solution)/shard_map/ppermute | solution.py:22
  44.0 7.3 %collective-permute-done.1 = bf16[256,1024]{1,0:T(8,128)(2,1)S(1)} collective-permute-done((bf16[256,1024]{1,0:T(8,128)(2,1)S(1)}, bf16[256,1024]{1,0:T(8,128)(2,1)S(1)}, u32[]{:S(2)}, u32[]{:S(2)}) %collective-permute-start.1) | collective-permute-done | bytes 524320 | tf_op jit(solution)/shard_map/ppermute | solution.py:40
  51.4 1.5 collective-permute-start.4
  52.9 0.0 copy-start.10
  52.9 2.5 %constant_dynamic-slice_fusion = bf16[512,1024]{1,0:T(8,128)(2,1)} fusion(bf16[1024,1024]{1,0:T(8,128)(2,1)} %param.11, s32[]{:T(128)S(6)} %select_n.118), kind=kLoop, calls=%fused_computation.52 | loop fusion | bytes 2097156 | tf_op jit(solution)/shard_map/dynamic_slice | solution.py:35
  55.4 1.0 constant_dynamic-slice_fusion.4
  56.4 0.8 subtract_exponential_fusion.weight_ref
  57.2 1.5 collective-permute-start.2
  58.7 5.0 %collective-permute-done.4 = bf16[256,1024]{1,0:T(8,128)(2,1)S(1)} collective-permute-done((bf16[256,1024]{1,0:T(8,128)(2,1)S(1)}, bf16[256,1024]{1,0:T(8,128)(2,1)S(1)}, u32[]{:S(2)}, u32[]{:S(2)}) %collective-permute-start.4) | collective-permute-done | bytes 524320 | tf_op jit(solution)/shard_map/ppermute | solution.py:40
  63.7 0.1 broadcast_select_fusion.5
  63.7 0.1 pad_maximum_fusion.4.first_ref
  63.8 0.4 collective-permute-done.7.second_ref
  64.2 1.5 collective-permute-start.9
  65.7 0.1 pad_add_fusion.1.place_ref
  65.8 0.1 copy.73
  65.9 1.7 %broadcast_select_fusion.3 = (bf16[512,1024]{1,0:T(8,128)(2,1)S(1)}, bf16[512,1024]{1,0:T(8,128)(2,1)S(1)}) fusion(bf16[512,1024]{1,0:T(8,128)(2,1)} %collective-permute-done.3, bf16[512,1024]{1,0:T(8,128)(2,1)} %collective-permute-done.8, pred[]{:T(512)S(6)} %eq.18), kind=kLoop, calls=%fused_computation.24 | loop fusion | flops 1048576 | bytes 4194305 | tf_op jit(solution)/shard_map/jit(_where)/select_n | solution.py:250
  67.6 0.2 pad_maximum_fusion.refs_0_
  67.8 12.7 %collective-permute-done.2.first_ref = bf16[512,1024]{1,0:T(8,128)(2,1)} collective-permute-done((bf16[512,1024]{1,0:T(8,128)(2,1)}, bf16[512,1024]{1,0:T(8,128)(2,1)}, u32[]{:S(2)}, u32[]{:S(2)}) %collective-permute-start.2) | collective-permute-done | bytes 1048608 | tf_op jit(solution)/shard_map/ppermute | solution.py:40
  80.5 1.5 collective-permute-start.6
  82.0 7.4 %shard_map.74.k_ref = bf16[1024,1024]{1,0:T(8,128)(2,1)S(1)} custom-call(s32[2]{0:T(128)S(1)} %pad_add_fusion.1.place_ref, bf16[1024,1024]{1,0:T(8,128)(2,1)S(1)} %copy-done.2, bf16[512,1024]{1,0:T(8,128)(2,1)} %collective-permute-done.first_ref, bf16[512,1024]{1,0:T(8,128)(2,1)} %collective-permute-done.7.second_ref, ...), custom_call_target="tpu_custom_call" | custom-call | flops 4294967296 | bytes 10485760 | tf_op jit(solution)/shard_map/pallas_call | solution.py:79
  89.5 1.3 copy-done.4
  90.8 0.4 collective-permute-start.5
  91.2 6.5 %shard_map.75.v_ref = bf16[1024,1024]{1,0:T(8,128)(2,1)S(1)} custom-call(s32[2]{0:T(128)S(1)} %pad_add_fusion.1.place_ref, bf16[1024,1024]{1,0:T(8,128)(2,1)S(1)} %copy-done.3, bf16[512,1024]{1,0:T(8,128)(2,1)S(1)} %pad_maximum_fusion.4.first_ref, bf16[512,1024]{1,0:T(8,128)(2,1)} %collective-permute-done.9.second_ref, ...), custom_call_target="tpu_custom_call" | custom-call | flops 4294967296 | bytes 10485760 | tf_op jit(solution)/shard_map/pallas_call | solution.py:79
  97.8 1.3 copy-done.6
  99.1 3.4 %shard_map.76 = bf16[8,128,128]{2,1,0:T(8,128)(2,1)} custom-call(bf16[1024,1024]{1,0:T(8,128)(2,1)} %copy-done.4, bf16[1024,1024]{1,0:T(8,128)(2,1)} %copy-done.6, f32[512,8]{1,0:T(8,128)} %subtract_exponential_fusion.weight_ref), custom_call_target="tpu_custom_call" | custom-call | tf_op jit(solution)/shard_map/pallas_call | solution.py:121
  102.5 0.1 broadcast_in_dim.26
  102.6 1.7 %pad_maximum_fusion.5 = bf16[8,144,128]{2,1,0:T(8,128)(2,1)} fusion(bf16[8,16,128]{2,1,0:T(8,128)(2,1)S(1)} %broadcast_in_dim.26, bf16[8,128,128]{2,1,0:T(8,128)(2,1)} %shard_map.76), kind=kLoop, calls=%fused_computation.39 | loop fusion | flops 589824 | bytes 589824 | tf_op jit(solution)/shard_map/concatenate | solution.py:267
  104.3 0.0 all-gather.3.cloned.1.call-update
  104.4 1.6 collective-permute-start.10
  105.9 0.1 copy.72
  106.1 0.1 pad_add_fusion.place_ref
  106.2 6.6 %collective-permute-done.5.second_ref = bf16[512,1024]{1,0:T(8,128)(2,1)} collective-permute-done((bf16[512,1024]{1,0:T(8,128)(2,1)}, bf16[512,1024]{1,0:T(8,128)(2,1)}, u32[]{:S(2)}, u32[]{:S(2)}) %collective-permute-start.5) | collective-permute-done | bytes 1048608 | tf_op jit(solution)/shard_map/ppermute | solution.py:40
  112.7 1.6 %copy-done.11 = bf16[1024,1024]{1,0:T(8,128)(2,1)S(1)} copy-done((bf16[1024,1024]{1,0:T(8,128)(2,1)S(1)}, bf16[1024,1024]{1,0:T(8,128)(2,1)}, u32[]{:S(2)}) %copy-start.11) | copy-done | bytes 2097176
  114.3 4.8 %shard_map.73.q_ref = bf16[512,1024]{1,0:T(8,128)(2,1)S(1)} custom-call(s32[2]{0:T(128)S(1)} %pad_add_fusion.place_ref, bf16[1024,1024]{1,0:T(8,128)(2,1)S(1)} %copy-done.11, bf16[512,1024]{1,0:T(8,128)(2,1)} %collective-permute-done.2.first_ref, bf16[512,1024]{1,0:T(8,128)(2,1)} %collective-permute-done.5.second_ref, ...), custom_call_target="tpu_custom_call" | custom-call | flops 2147483648 | bytes 7340032 | tf_op jit(solution)/shard_map/pallas_call | solution.py:79
  119.2 0.0 copy-start.9
  119.2 10.4 %shard_map.77.window_ref = f32[512,1024]{1,0:T(8,128)S(1)} custom-call(f32[1,1]{1,0:T(1,128)} %bitcast.22.allow_ref, bf16[512,1024]{1,0:T(8,128)(2,1)S(1)} %shard_map.73.q_ref, bf16[1024,1024]{1,0:T(8,128)(2,1)S(1)} %copy-done.5, bf16[1024,1024]{1,0:T(8,128)(2,1)S(1)} %copy-done.7), custom_call_target="tpu_custom_call" | custom-call | flops 2147483648 | bytes 7340032 | tf_op jit(solution)/shard_map/pallas_call | solution.py:157
  129.7 3.4 %broadcast_select_fusion.1 = (bf16[512,1024]{1,0:T(8,128)(2,1)S(1)}, bf16[512,1024]{1,0:T(8,128)(2,1)}) fusion(bf16[512,1024]{1,0:T(8,128)(2,1)} %collective-permute-done.6, bf16[512,1024]{1,0:T(8,128)(2,1)} %collective-permute-done.10, pred[]{:T(512)S(6)} %eq.21), kind=kLoop, calls=%fused_computation.22 | loop fusion | flops 1048576 | bytes 4194305 | tf_op jit(solution)/shard_map/jit(_where)/select_n | solution.py:45
  133.1 2.2 %all-gather.3.cloned.1.call-done = bf16[32,144,128]{2,1,0:T(8,128)(2,1)} async-done(((bf16[8,144,128]{2,1,0:T(8,128)(2,1)}), bf16[32,144,128]{2,1,0:T(8,128)(2,1)}) %all-gather.3.cloned.1.call-update) | async-done | bytes 1179664 | tf_op jit(solution)/shard_map/all_gather | solution.py:267
  135.3 0.8 slice_convert_fusion.2
  136.0 0.1 copy.69
  136.1 0.1 copy.70
  136.2 0.1 copy.71
  136.4 0.7 broadcast_divide_fusion.decay_ref
  137.1 2.2 %fusion.22.state_ref = bf16[8,128,128]{2,1,0:T(8,128)(2,1)} fusion(bf16[4,8,144,128]{3,2,1,0:T(8,128)(2,1)} %bitcast.65, f32[]{:T(128)} %bitcast.9, f32[8]{0:T(128)S(1)} %get-tuple-element.38, f32[8]{0:T(128)S(1)} %get-tuple-element.42, f32[8]{0:T(128)S(1)} %get-tuple-element.41, pred[]{:T(512)S(6)} %gt.15, pred[]{:T(512)S(6)} %gt.14, pred[]{:T(512)S(6)} %gt.13), kind=kLoop, calls=%fused_computation.28 | loop fusion | flops 1703936 | bytes 1048679 | tf_op jit(solution)/shard_map/convert_element_type | solution.py:276
  139.3 3.3 %shard_map.78 = bf16[512,1024]{1,0:T(8,128)(2,1)} custom-call(bf16[512,1024]{1,0:T(8,128)(2,1)} %copy-done.9, bf16[8,128,128]{2,1,0:T(8,128)(2,1)} %fusion.22.state_ref, f32[512,8]{1,0:T(8,128)} %broadcast_divide_fusion.decay_ref, f32[512,1024]{1,0:T(8,128)} %copy-done.8), custom_call_target="tpu_custom_call" | custom-call | tf_op jit(solution)/shard_map/pallas_call | solution.py:190
  142.6 3.0 %fusion.10 = bf16[512,1024]{1,0:T(8,128)(2,1)S(1)} fusion(bf16[512,1024]{1,0:T(8,128)(2,1)} %shard_map.78, bf16[1024,1024]{1,0:T(8,128)(2,1)} %param.11, pred[]{:T(512)S(6)} %eq.20, bf16[512,1024]{1,0:T(8,128)(2,1)} %get-tuple-element.26, bf16[512,1024]{1,0:T(8,128)(2,1)S(1)} %get-tuple-element.25), kind=kOutput, calls=%fused_computation.15 | convolution fusion | flops 1079508992 | bytes 6291457 | tf_op jit(solution)/shard_map/dot_general | solution.py:291
  145.5 0.1 collective-permute-start.11
  145.6 2.6 %collective-permute-done.11 = bf16[512,1024]{1,0:T(8,128)(2,1)S(1)} collective-permute-done((bf16[512,1024]{1,0:T(8,128)(2,1)S(1)}, bf16[512,1024]{1,0:T(8,128)(2,1)S(1)}, u32[]{:S(2)}, u32[]{:S(2)}) %collective-permute-start.11) | collective-permute-done | bytes 1048608 | tf_op jit(solution)/shard_map/ppermute | solution.py:17
  148.3 2.4 %fusion.15 = bf16[1,512,1024]{2,1,0:T(8,128)(2,1)} fusion(bf16[512,1024]{1,0:T(8,128)(2,1)S(1)} %collective-permute-done.11, bf16[512,1024]{1,0:T(8,128)(2,1)S(1)} %copy-done.15, bf16[1024,1024]{1,0:T(8,128)(2,1)S(1)} %copy-done.16, pred[]{:T(512)S(6)} %eq.20, bf16[512,1024]{1,0:T(8,128)(2,1)S(1)} %copy-done.14, ...), kind=kOutput, calls=%fused_computation.16 | convolution fusion | flops 1081606144 | bytes 8388613 | tf_op jit(solution)/shard_map/dot_general | solution.py:293
  (46 shorter events, 0.2 us)
Async XLA Ops:
  6.5 16.4 %copy-start = (f32[1,8,512]{2,1,0:T(8,128)S(1)}, f32[1,8,512]{2,1,0:T(8,128)}, u32[]{:S(2)}) copy-start(f32[1,8,512]{2,1,0:T(8,128)} %param.12) | copy-start | bytes 49156
  6.5 128.7 %all-gather.3.cloned.1.call-start = ((), (), s32[]{:S(2)}) async-start(), calls=%async_computation | async-start | bytes 1474560 | tf_op jit(solution)/shard_map/all_gather | solution.py:267
  11.9 3.6 %copy-start.1 = (bf16[1024,1024]{1,0:T(8,128)(2,1)}, bf16[1024,1024]{1,0:T(8,128)(2,1)S(1)}, u32[]{:S(2)}) copy-start(bf16[1024,1024]{1,0:T(8,128)(2,1)S(1)} %get-tuple-element.23.own_ref) | copy-start | bytes 6291460
  11.9 3.1 %copy-start.12 = (bf16[1,512,2048]{2,1,0:T(8,128)(2,1)S(1)}, bf16[1,512,2048]{2,1,0:T(8,128)(2,1)}, u32[]{:S(2)}) copy-start(bf16[1,512,2048]{2,1,0:T(8,128)(2,1)} %param.7) | copy-start | bytes 6291460
  11.9 3.6 %copy-start.17 = (f32[2048]{0:T(1024)S(1)}, f32[2048]{0:T(1024)}, u32[]{:S(2)}) copy-start(f32[2048]{0:T(1024)} %param.8) | copy-start | bytes 24580
  12.0 26.3 %collective-permute-start = (bf16[512,1024]{1,0:T(8,128)(2,1)S(1)}, bf16[512,1024]{1,0:T(8,128)(2,1)}, u32[]{:S(2)}, u32[]{:S(2)}) collective-permute-start(bf16[512,1024]{1,0:T(8,128)(2,1)S(1)} %constant_dynamic-slice_fusion.2), channel_id=1, source_target_pairs={{0,2},{2,0},{1,3},{3,1},{4,6},{6,4},{5,7},{7,5},{8,10},{10,8},{9,1... | collective-permute-start | bytes 3145736 | tf_op jit(solution)/shard_map/ppermute | solution.py:40
  17.1 26.9 %collective-permute-start.3 = (bf16[512,1024]{1,0:T(8,128)(2,1)}, bf16[512,1024]{1,0:T(8,128)(2,1)}, u32[]{:S(2)}, u32[]{:S(2)}) collective-permute-start(bf16[512,1024]{1,0:T(8,128)(2,1)} %constant_dynamic-slice_fusion.1), channel_id=1, source_target_pairs={{0,4},{4,8},{8,12},{1,5},{5,9},{9,13},{2,6},{6,10},{10,14},{3,7},{... | collective-permute-start | bytes 3145736 | tf_op jit(solution)/shard_map/ppermute | solution.py:22
  38.3 13.1 %collective-permute-start.1 = (bf16[256,1024]{1,0:T(8,128)(2,1)S(1)}, bf16[256,1024]{1,0:T(8,128)(2,1)S(1)}, u32[]{:S(2)}, u32[]{:S(2)}) collective-permute-start(bf16[256,1024]{1,0:T(8,128)(2,1)S(1)} %constant_dynamic-slice_fusion.3), channel_id=1, source_target_pairs={{0,2},{2,0},{1,3},{3,1},{4,6},{6,4},{5,7},{7,5},{8,10},{10,8},{9,1... | collective-permute-start | bytes 1572872 | tf_op jit(solution)/shard_map/ppermute | solution.py:40
  40.1 24.1 %collective-permute-start.7 = (bf16[512,1024]{1,0:T(8,128)(2,1)}, bf16[512,1024]{1,0:T(8,128)(2,1)}, u32[]{:S(2)}, u32[]{:S(2)}) collective-permute-start(bf16[512,1024]{1,0:T(8,128)(2,1)} %collective-permute-done.first_ref), channel_id=1, source_target_pairs={{0,16},{16,0},{1,17},{17,1},{2,18},{18,2},{3,19},{19,3},{4,20},{20... | collective-permute-start | bytes 3145736 | tf_op jit(solution)/shard_map/ppermute | solution.py:40
  44.0 21.9 %collective-permute-start.8 = (bf16[512,1024]{1,0:T(8,128)(2,1)}, bf16[512,1024]{1,0:T(8,128)(2,1)}, u32[]{:S(2)}, u32[]{:S(2)}) collective-permute-start(bf16[512,1024]{1,0:T(8,128)(2,1)} %collective-permute-done.3), channel_id=1, source_target_pairs={{0,1},{1,0},{2,3},{3,2},{4,5},{5,4},{6,7},{7,6},{8,9},{9,8},{10,11... | collective-permute-start | bytes 3145736 | tf_op jit(solution)/shard_map/ppermute | solution.py:17
  51.4 12.3 %collective-permute-start.4 = (bf16[256,1024]{1,0:T(8,128)(2,1)S(1)}, bf16[256,1024]{1,0:T(8,128)(2,1)S(1)}, u32[]{:S(2)}, u32[]{:S(2)}) collective-permute-start(bf16[256,1024]{1,0:T(8,128)(2,1)S(1)} %collective-permute-done.1), channel_id=1, source_target_pairs={{0,4},{4,0},{8,12},{12,8},{1,5},{5,1},{9,13},{13,9},{2,6},{6,2},{1... | collective-permute-start | bytes 1572872 | tf_op jit(solution)/shard_map/ppermute | solution.py:40
  52.9 2.5 %copy-start.10 = (bf16[1024,1024]{1,0:T(8,128)(2,1)S(1)}, bf16[1024,1024]{1,0:T(8,128)(2,1)}, u32[]{:S(2)}) copy-start(bf16[1024,1024]{1,0:T(8,128)(2,1)} %own_ref.1) | copy-start | bytes 6291460
  57.2 23.3 %collective-permute-start.2 = (bf16[512,1024]{1,0:T(8,128)(2,1)}, bf16[512,1024]{1,0:T(8,128)(2,1)}, u32[]{:S(2)}, u32[]{:S(2)}) collective-permute-start(bf16[512,1024]{1,0:T(8,128)(2,1)} %constant_dynamic-slice_fusion.4), channel_id=1, source_target_pairs={{0,2},{2,0},{1,3},{3,1},{4,6},{6,4},{5,7},{7,5},{8,10},{10,8},{9,1... | collective-permute-start | bytes 3145736 | tf_op jit(solution)/shard_map/ppermute | solution.py:40
  64.2 27.0 %collective-permute-start.9 = (bf16[512,1024]{1,0:T(8,128)(2,1)S(1)}, bf16[512,1024]{1,0:T(8,128)(2,1)}, u32[]{:S(2)}, u32[]{:S(2)}) collective-permute-start(bf16[512,1024]{1,0:T(8,128)(2,1)S(1)} %pad_maximum_fusion.4.first_ref), channel_id=1, source_target_pairs={{0,16},{16,0},{1,17},{17,1},{2,18},{18,2},{3,19},{19,3},{4,20},{20... | collective-permute-start | bytes 3145736 | tf_op jit(solution)/shard_map/ppermute | solution.py:40
  67.6 14.4 %copy-start.2 = (bf16[1024,1024]{1,0:T(8,128)(2,1)S(1)}, bf16[1024,1024]{1,0:T(8,128)(2,1)}, u32[]{:S(2)}) copy-start(bf16[1024,1024]{1,0:T(8,128)(2,1)} %copy-done.1) | copy-start | bytes 6291460
  67.8 23.4 %copy-start.3 = (bf16[1024,1024]{1,0:T(8,128)(2,1)S(1)}, bf16[1024,1024]{1,0:T(8,128)(2,1)}, u32[]{:S(2)}) copy-start(bf16[1024,1024]{1,0:T(8,128)(2,1)} %get-tuple-element.24.own_ref) | copy-start | bytes 6291460
  80.5 23.8 %collective-permute-start.6 = (bf16[512,1024]{1,0:T(8,128)(2,1)}, bf16[512,1024]{1,0:T(8,128)(2,1)}, u32[]{:S(2)}, u32[]{:S(2)}) collective-permute-start(bf16[512,1024]{1,0:T(8,128)(2,1)} %constant_dynamic-slice_fusion), channel_id=1, source_target_pairs={{0,2},{2,0},{1,3},{3,1},{4,6},{6,4},{5,7},{7,5},{8,10},{10,8},{9,1... | collective-permute-start | bytes 3145736 | tf_op jit(solution)/shard_map/ppermute | solution.py:40
  89.5 1.3 copy-start.4
  90.8 22.0 %collective-permute-start.5 = (bf16[512,1024]{1,0:T(8,128)(2,1)}, bf16[512,1024]{1,0:T(8,128)(2,1)}, u32[]{:S(2)}, u32[]{:S(2)}) collective-permute-start(bf16[512,1024]{1,0:T(8,128)(2,1)} %collective-permute-done.2.first_ref), channel_id=1, source_target_pairs={{0,4},{4,0},{8,12},{12,8},{1,5},{5,1},{9,13},{13,9},{2,6},{6,2},{1... | collective-permute-start | bytes 3145736 | tf_op jit(solution)/shard_map/ppermute | solution.py:40
  97.8 1.3 copy-start.6
  104.4 25.3 %collective-permute-start.10 = (bf16[512,1024]{1,0:T(8,128)(2,1)}, bf16[512,1024]{1,0:T(8,128)(2,1)}, u32[]{:S(2)}, u32[]{:S(2)}) collective-permute-start(bf16[512,1024]{1,0:T(8,128)(2,1)} %collective-permute-done.6), channel_id=1, source_target_pairs={{0,16},{16,0},{1,17},{17,1},{2,18},{18,2},{3,19},{19,3},{4,20},{20... | collective-permute-start | bytes 3145736 | tf_op jit(solution)/shard_map/ppermute | solution.py:40
  106.1 13.0 %copy-start.5 = (bf16[1024,1024]{1,0:T(8,128)(2,1)S(1)}, bf16[1024,1024]{1,0:T(8,128)(2,1)}, u32[]{:S(2)}) copy-start(bf16[1024,1024]{1,0:T(8,128)(2,1)} %copy-done.4) | copy-start | bytes 6291460
  106.1 13.1 %copy-start.7 = (bf16[1024,1024]{1,0:T(8,128)(2,1)S(1)}, bf16[1024,1024]{1,0:T(8,128)(2,1)}, u32[]{:S(2)}) copy-start(bf16[1024,1024]{1,0:T(8,128)(2,1)} %copy-done.6) | copy-start | bytes 6291460
  112.7 1.6 %copy-start.11 = (bf16[1024,1024]{1,0:T(8,128)(2,1)S(1)}, bf16[1024,1024]{1,0:T(8,128)(2,1)}, u32[]{:S(2)}) copy-start(bf16[1024,1024]{1,0:T(8,128)(2,1)} %own_ref.1) | copy-start | bytes 6291460
  119.2 10.5 %copy-start.9 = (bf16[512,1024]{1,0:T(8,128)(2,1)}, bf16[512,1024]{1,0:T(8,128)(2,1)S(1)}, u32[]{:S(2)}) copy-start(bf16[512,1024]{1,0:T(8,128)(2,1)S(1)} %shard_map.73.q_ref) | copy-start | bytes 3145732
  129.7 3.4 %copy-start.8 = (f32[512,1024]{1,0:T(8,128)}, f32[512,1024]{1,0:T(8,128)S(1)}, u32[]{:S(2)}) copy-start(f32[512,1024]{1,0:T(8,128)S(1)} %shard_map.77.window_ref) | copy-start | bytes 6291460
  142.5 5.7 %copy-start.13 = (bf16[1,512,2048]{2,1,0:T(8,128)(2,1)S(1)}, bf16[1,512,2048]{2,1,0:T(8,128)(2,1)}, u32[]{:S(2)}) copy-start(bf16[1,512,2048]{2,1,0:T(8,128)(2,1)} %param.7) | copy-start | bytes 6291460
  142.5 5.7 %copy-start.14 = (bf16[512,1024]{1,0:T(8,128)(2,1)S(1)}, bf16[512,1024]{1,0:T(8,128)(2,1)}, u32[]{:S(2)}) copy-start(bf16[512,1024]{1,0:T(8,128)(2,1)} %get-tuple-element.26) | copy-start | bytes 3145732
  142.5 5.7 %copy-start.15 = (bf16[512,1024]{1,0:T(8,128)(2,1)S(1)}, bf16[512,1024]{1,0:T(8,128)(2,1)}, u32[]{:S(2)}) copy-start(bf16[512,1024]{1,0:T(8,128)(2,1)} %shard_map.78) | copy-start | bytes 3145732
  142.5 5.7 %copy-start.16 = (bf16[1024,1024]{1,0:T(8,128)(2,1)S(1)}, bf16[1024,1024]{1,0:T(8,128)(2,1)}, u32[]{:S(2)}) copy-start(bf16[1024,1024]{1,0:T(8,128)(2,1)} %param.11) | copy-start | bytes 6291460
  145.5 2.7 %collective-permute-start.11 = (bf16[512,1024]{1,0:T(8,128)(2,1)S(1)}, bf16[512,1024]{1,0:T(8,128)(2,1)S(1)}, u32[]{:S(2)}, u32[]{:S(2)}) collective-permute-start(bf16[512,1024]{1,0:T(8,128)(2,1)S(1)} %fusion.10), channel_id=1, source_target_pairs={{0,1},{1,0},{2,3},{3,2},{4,5},{5,4},{6,7},{7,6},{8,9},{9,8},{10,11... | collective-permute-start | bytes 3145736 | tf_op jit(solution)/shard_map/ppermute | solution.py:17
Sparse Core Ops, SparseCore 0:
  104.5 30.7 all-gather.2

commit v6 on v5

--- a/solution.py
+++ b/solution.py
@@ -219,21 +219,27 @@
     normed = (rms_rows(acts.astype(F32), 1e-05) * norm_gain).astype(BF16)
     lane = width // 2
     ours = shifted(lax.dynamic_slice_in_dim(normed, core * lane, lane, 1), "seq")
+    theirs = around(ours, "heads")
+    prior = jnp.concatenate(
+        [jnp.where(core == 0, ours, theirs), jnp.where(core == 0, theirs, ours)], axis=1
+    )
+    both = (prior, normed)
     w_pair = w_keyvalue.reshape(w_keyvalue.shape[0], 2 * inner_here)
     own = [w_pair[:, :inner_here], w_pair[:, inner_here:], w_query, w_output]
     if paired:
-        key_x = swapped(part_of(own[0], group, 2), "wloop")
+        key_x = swapped(part_of(w_keyvalue, group, 2)[:, 0, :], "wloop")
         key_y = swapped(key_x, "groups")
-        value_x = swapped(after(part_of(own[1], 2 * group + twin, 4), key_x), "wloop")
+        value_x = swapped(after(part_of(w_keyvalue, 2 * group + twin, 4)[:, 1, :], key_x), "wloop")
         query_x = swapped(after(part_of(own[2], twin, 2), value_x), "wloop")
         value_z = swapped(after(value_x, ours), "seq")
         value_half = in_order(twin, value_x, value_z)
         value_y = swapped(after(value_half, key_y), "groups")
+        keys = projection(place, both, own[0], key_x, key_y, head_dim)
+        query_x = after(query_x, keys)
         output_x = swapped(after(part_of(own[3], group, 2), query_x), "wloop")
         query_z = swapped(after(query_x, value_z), "seq")
         output_y = swapped(after(output_x, value_y), "groups")
         blocks = [
-            (own[0], key_x, key_y),
             (own[1], value_half, after(value_y, query_x)),
             (own[2], query_x, after(query_z, output_x)),
         ]
@@ -245,14 +251,10 @@
             half = full.shape[0] // 2
             blocks.append((full[:half], full[half : half + half // 2], full[half + half // 2 :]))
 
-    theirs = around(ours, "heads")
-    prior = jnp.concatenate(
-        [jnp.where(core == 0, ours, theirs), jnp.where(core == 0, theirs, ours)], axis=1
-    )
-    both = (prior, normed)
-    keys = projection(place, both, *blocks[0], head_dim)
-    values = projection(place, both, *blocks[1], 0)
-    queries = projection(place_query, (normed,), *blocks[2], head_dim)
+        keys = projection(place, both, *blocks[0], head_dim)
+        blocks = blocks[1:]
+    values = projection(place, both, *blocks[0], 0)
+    queries = projection(place_query, (normed,), *blocks[1], head_dim)
 
     keep = (1 - resets[0, 0]).astype(F32)
     upto = jnp.triu(jnp.ones((span, span), F32))

time: 158 us -> 155 us (0.981)
  waiting for transfers between devices: 52.3 us -> 39.6 us
  local copies, waits for them, and re-layouts: 16.1 us -> 27.1 us
    ppermute x9, waiting for transfers between devices: 45.1 us -> 35.8 us  [swapped(): lax.ppermute(value, axis, [(i, i + 1 - 2 * (i % 2)) for i in range(count)])]
    unnamed x38 -> x30, local copies, waits for them, and re-layouts: 8 us -> 13.8 us
    slice x0 -> x2, local copies, waits for them, and re-layouts: none -> 5.35 us  [the longest x1 3.04 us: shards(): key_x = swapped(part_of(w_keyvalue, group, 2)[:, 0, :], 'wloop')]
    ppermute x1, waiting for transfers between devices: 2.36 us -> 0.01 us  [shifted(): return lax.ppermute(value, axis, [(i, i + 1) for i in range(count - 1)])]
    dynamic_slice x4 -> x2, local copies, waits for them, and re-layouts: 4.65 us -> 3.56 us  [part_of(): return lax.dynamic_slice_in_dim(block, index * rows, rows, 0)]
  transfers between devices with their start and end apart: 13 -> 13, of which waited for: 9 -> 9; matrix products, arithmetic and copies ran while one was open for 10% -> 17% of each run, Pallas kernels for 21% -> 21%
where the time goes in v6:
time: 155 us; the launch traced here: 154 us
  waiting for transfers between devices  39.6 us (26%)
  Pallas kernels  35.8 us (23%)
  local copies, waits for them, and re-layouts  27.1 us (17%)
  starting transfers between devices  18.8 us (12%)
  between operations  14.3 us (9%)
  other arithmetic  12.3 us (8%)
  matrix products  6.03 us (4%)
    ppermute x9, waiting for transfers between devices, swapped(): lax.ppermute(value, axis, [(i, i + 1 - 2 * (i % 2)) for i in range(count)])  35.8 us
    pallas_call x3, Pallas kernels, projection(): pl.pallas_call(functools.partial(projection_kernel, head_dim), grid=(inne...  18.6 us
    ppermute x9, starting transfers between devices, swapped(): lax.ppermute(value, axis, [(i, i + 1 - 2 * (i % 2)) for i in range(count)])  14.2 us
    unnamed x30, local copies, waits for them, and re-layouts  13.8 us
    pallas_call x1, Pallas kernels, window_mix(): pl.pallas_call(functools.partial(window_kernel, scale), grid=(inner // he...  10.4 us
    ppermute x1, starting transfers between devices, shifted(): return lax.ppermute(value, axis, [(i, i + 1) for i in range(count - 1)])  4.44 us
    dynamic_slice x2, local copies, waits for them, and re-layouts, part_of(): return lax.dynamic_slice_in_dim(block, index * rows, rows, 0)  3.56 us
    pallas_call x1, Pallas kernels, local_states(): pl.pallas_call(state_kernel, grid=(heads // step,), in_specs=[block, bloc...  3.43 us
  transfers between devices with their start and end apart: 13, of which 9 were waited for; matrix products, arithmetic and copies ran while one was open for 17% of the time, Pallas kernels for 21%

profile of v6, /device:TPU:0, one launch (start us, length us, event | category | flops | bytes accessed | tf_op | source)
XLA Modules:
  0.0 153.9 jit_solution(3797900802123989245)
XLA Ops:
  6.5 3.0 %constant_dynamic-slice_fusion.2 = bf16[512,1,1024]{2,1,0:T(2,128)(2,1)S(1)} fusion(bf16[1024,2,1024]{2,1,0:T(2,128)(2,1)} %param.10, s32[]{:T(128)S(6)} %select_n.118), kind=kLoop, calls=%fused_computation.56 | loop fusion | bytes 2097156 | tf_op jit(solution)/shard_map/slice | solution.py:230
  9.6 1.3 copy.89
  11.0 2.9 %collective-permute-start = (bf16[512,1024]{1,0:T(8,128)(2,1)}, bf16[512,1024]{1,0:T(8,128)(2,1)S(1)}, u32[]{:S(2)}, u32[]{:S(2)}) collective-permute-start(bf16[512,1024]{1,0:T(8,128)(2,1)} %bitcast.65), channel_id=1, source_target_pairs={{0,2},{2,0},{1,3},{3,1},{4,6},{6,4},{5,7},{7,5},{8,10},{10,8},{9,1... | collective-permute-start | bytes 3145736 | tf_op jit(solution)/shard_map/ppermute | solution.py:40
  13.9 0.5 fusion
  14.4 0.5 fusion.2.refs_1_.refs_0_
  15.0 1.1 constant_dynamic-slice_fusion.1
  16.0 4.4 %collective-permute-start.4 = (bf16[512,1024]{1,0:T(8,128)(2,1)}, bf16[512,1024]{1,0:T(8,128)(2,1)}, u32[]{:S(2)}, u32[]{:S(2)}) collective-permute-start(bf16[512,1024]{1,0:T(8,128)(2,1)} %constant_dynamic-slice_fusion.1), channel_id=1, source_target_pairs={{0,4},{4,8},{8,12},{1,5},{5,9},{9,13},{2,6},{6,10},{10,14},{3,7},{... | collective-permute-start | bytes 3145736 | tf_op jit(solution)/shard_map/ppermute | solution.py:22
  20.5 2.3 %constant_dynamic-slice_fusion.3 = bf16[256,1,1024]{2,1,0:T(2,128)(2,1)S(1)} fusion(bf16[1024,2,1024]{2,1,0:T(2,128)(2,1)} %param.10, s32[]{:T(128)S(6)} %select_n.117, s32[]{:T(128)S(6)} %add.146), kind=kLoop, calls=%fused_computation.57 | loop fusion | bytes 1048584 | tf_op jit(solution)/shard_map/slice | solution.py:232
  22.8 1.0 copy.90
  24.5 0.9 fusion.41
  25.4 0.1 copy.73
  25.5 0.1 multiply_reduce_fusion
  25.6 11.6 %collective-permute-done.first_ref = bf16[512,1024]{1,0:T(8,128)(2,1)S(1)} collective-permute-done((bf16[512,1024]{1,0:T(8,128)(2,1)}, bf16[512,1024]{1,0:T(8,128)(2,1)S(1)}, u32[]{:S(2)}, u32[]{:S(2)}) %collective-permute-start) | collective-permute-done | bytes 1048608 | tf_op jit(solution)/shard_map/ppermute | solution.py:40
  37.3 1.7 %collective-permute-start.1 = (bf16[256,1024]{1,0:T(8,128)(2,1)}, bf16[256,1024]{1,0:T(8,128)(2,1)}, u32[]{:S(2)}, u32[]{:S(2)}) collective-permute-start(bf16[256,1024]{1,0:T(8,128)(2,1)} %bitcast.72), channel_id=1, source_target_pairs={{0,2},{2,0},{1,3},{3,1},{4,6},{6,4},{5,7},{7,5},{8,10},{10,8},{9,1... | collective-permute-start | bytes 1572872 | tf_op jit(solution)/shard_map/ppermute | solution.py:40
  39.0 2.3 %constant_dynamic-slice_fusion = bf16[512,1024]{1,0:T(8,128)(2,1)} fusion(bf16[1024,1024]{1,0:T(8,128)(2,1)} %param.11, s32[]{:T(128)S(6)} %select_n.118), kind=kLoop, calls=%fused_computation.54 | loop fusion | bytes 2097156 | tf_op jit(solution)/shard_map/dynamic_slice | solution.py:35
  41.3 1.5 collective-permute-start.3
  42.8 7.9 %collective-permute-done.1 = bf16[256,1024]{1,0:T(8,128)(2,1)} collective-permute-done((bf16[256,1024]{1,0:T(8,128)(2,1)}, bf16[256,1024]{1,0:T(8,128)(2,1)}, u32[]{:S(2)}, u32[]{:S(2)}) %collective-permute-start.1) | collective-permute-done | bytes 524320 | tf_op jit(solution)/shard_map/ppermute | solution.py:40
  50.7 1.6 %collective-permute-start.6 = (bf16[256,1024]{1,0:T(8,128)(2,1)}, bf16[256,1024]{1,0:T(8,128)(2,1)}, u32[]{:S(2)}, u32[]{:S(2)}) collective-permute-start(bf16[256,1024]{1,0:T(8,128)(2,1)} %collective-permute-done.1), channel_id=1, source_target_pairs={{0,4},{4,0},{8,12},{12,8},{1,5},{5,1},{9,13},{13,9},{2,6},{6,2},{1... | collective-permute-start | bytes 1572872 | tf_op jit(solution)/shard_map/ppermute | solution.py:40
  52.3 0.1 pad_add_fusion.1.place_ref
  52.4 5.7 %copy.86 = bf16[128,8,2,1024]{3,1,2,0:T(8,128)(2,1)} copy(bf16[128,8,2,1024]{3,2,1,0:T(2,128)(2,1)} %bitcast.68) | data formatting | bytes 8388608
  58.0 0.1 copy.85
  58.1 1.3 constant_dynamic-slice_fusion.4
  59.4 2.7 %fusion.40 = (bf16[1024,1024]{1,0:T(8,128)(2,1)S(1)}, bf16[1024,1024]{1,0:T(8,128)(2,1)S(1)}) fusion(bf16[1024,2048]{1,0:T(8,128)(2,1)} %bitcast.67), kind=kLoop, calls=%fused_computation.85 | loop fusion | bytes 8388608 | tf_op jit(solution)/shard_map/slice | solution.py:228
  62.1 1.6 %collective-permute-start.2 = (bf16[512,1024]{1,0:T(8,128)(2,1)S(1)}, bf16[512,1024]{1,0:T(8,128)(2,1)}, u32[]{:S(2)}, u32[]{:S(2)}) collective-permute-start(bf16[512,1024]{1,0:T(8,128)(2,1)S(1)} %constant_dynamic-slice_fusion.4), channel_id=1, source_target_pairs={{0,2},{2,0},{1,3},{3,1},{4,6},{6,4},{5,7},{7,5},{8,10},{10,8},{9,1... | collective-permute-start | bytes 3145736 | tf_op jit(solution)/shard_map/ppermute | solution.py:40
  63.7 1.3 broadcast_select_fusion.5
  64.9 0.1 pad_maximum_fusion.4.first_ref
  65.0 0.1 collective-permute-done.3.second_ref
  65.1 1.5 collective-permute-start.9
  66.7 1.7 %broadcast_select_fusion.3 = (bf16[512,1024]{1,0:T(8,128)(2,1)S(1)}, bf16[512,1024]{1,0:T(8,128)(2,1)S(1)}) fusion(bf16[512,1024]{1,0:T(8,128)(2,1)} %collective-permute-done.4, bf16[512,1024]{1,0:T(8,128)(2,1)} %collective-permute-done.5, pred[]{:T(512)S(6)} %eq.18), kind=kLoop, calls=%fused_computation.25 | loop fusion | flops 1048576 | bytes 4194305 | tf_op jit(solution)/shard_map/jit(_where)/select_n | solution.py:224
  68.4 0.2 pad_maximum_fusion.refs_0_
  68.5 7.6 %shard_map.73.k_ref = bf16[1024,1024]{1,0:T(8,128)(2,1)S(1)} custom-call(s32[2]{0:T(128)S(1)} %pad_add_fusion.1.place_ref, bf16[1024,1024]{1,0:T(8,128)(2,1)S(1)} %get-tuple-element.26.own_ref, bf16[512,1024]{1,0:T(8,128)(2,1)S(1)} %collective-permute-done.first_ref, bf16[512,1024]{1,0:T(8,128)(2,1)} %collective-permute-done.3.second_ref, ...), custom_call_target="tpu_custom_call" | custom-call | flops 4294967296 | bytes 10485760 | tf_op jit(solution)/shard_map/pallas_call | solution.py:79
  76.2 1.3 copy-done.1
  77.5 7.8 %collective-permute-done.2.first_ref = bf16[512,1024]{1,0:T(8,128)(2,1)} collective-permute-done((bf16[512,1024]{1,0:T(8,128)(2,1)S(1)}, bf16[512,1024]{1,0:T(8,128)(2,1)}, u32[]{:S(2)}, u32[]{:S(2)}) %collective-permute-start.2) | collective-permute-done | bytes 1048608 | tf_op jit(solution)/shard_map/ppermute | solution.py:40
  85.3 1.5 collective-permute-start.8
  86.8 0.8 subtract_exponential_fusion.weight_ref
  87.5 0.3 collective-permute-start.7
  87.9 0.1 collective-permute-done.9.second_ref
  88.0 6.2 %shard_map.75.v_ref = bf16[1024,1024]{1,0:T(8,128)(2,1)S(1)} custom-call(s32[2]{0:T(128)S(1)} %pad_add_fusion.1.place_ref, bf16[1024,1024]{1,0:T(8,128)(2,1)S(1)} %get-tuple-element.25.own_ref, bf16[512,1024]{1,0:T(8,128)(2,1)S(1)} %pad_maximum_fusion.4.first_ref, bf16[512,1024]{1,0:T(8,128)(2,1)S(1)} %collective-permute-done.9.second_ref, ...), custom_call_target="tpu_custom_call" | custom-call | flops 4294967296 | bytes 10485760 | tf_op jit(solution)/shard_map/pallas_call | solution.py:79
  94.2 1.3 copy-done.3
  95.5 3.4 %shard_map.76 = bf16[8,128,128]{2,1,0:T(8,128)(2,1)} custom-call(bf16[1024,1024]{1,0:T(8,128)(2,1)} %copy-done.1, bf16[1024,1024]{1,0:T(8,128)(2,1)} %copy-done.3, f32[512,8]{1,0:T(8,128)} %subtract_exponential_fusion.weight_ref), custom_call_target="tpu_custom_call" | custom-call | tf_op jit(solution)/shard_map/pallas_call | solution.py:121
  99.0 0.1 broadcast_in_dim.26
  99.1 1.7 %pad_maximum_fusion.5 = bf16[8,144,128]{2,1,0:T(8,128)(2,1)} fusion(bf16[8,16,128]{2,1,0:T(8,128)(2,1)S(1)} %broadcast_in_dim.26, bf16[8,128,128]{2,1,0:T(8,128)(2,1)} %shard_map.76), kind=kLoop, calls=%fused_computation.41 | loop fusion | flops 589824 | bytes 589824 | tf_op jit(solution)/shard_map/concatenate | solution.py:269
  100.8 6.9 %collective-permute-done.8 = bf16[512,1024]{1,0:T(8,128)(2,1)} collective-permute-done((bf16[512,1024]{1,0:T(8,128)(2,1)}, bf16[512,1024]{1,0:T(8,128)(2,1)}, u32[]{:S(2)}, u32[]{:S(2)}) %collective-permute-start.8) | collective-permute-done | bytes 1048608 | tf_op jit(solution)/shard_map/ppermute | solution.py:40
  107.7 1.5 collective-permute-start.10
  109.2 0.1 copy.80
  109.3 0.1 pad_add_fusion.place_ref
  109.4 1.7 %copy-done.7 = bf16[1024,1024]{1,0:T(8,128)(2,1)S(1)} copy-done((bf16[1024,1024]{1,0:T(8,128)(2,1)S(1)}, bf16[1024,1024]{1,0:T(8,128)(2,1)}, u32[]{:S(2)}) %copy-start.7) | copy-done | bytes 2097176
  111.2 4.7 %shard_map.74.q_ref = bf16[512,1024]{1,0:T(8,128)(2,1)S(1)} custom-call(s32[2]{0:T(128)S(1)} %pad_add_fusion.place_ref, bf16[1024,1024]{1,0:T(8,128)(2,1)S(1)} %copy-done.7, bf16[512,1024]{1,0:T(8,128)(2,1)} %collective-permute-done.2.first_ref, bf16[512,1024]{1,0:T(8,128)(2,1)S(1)} %collective-permute-done.7.second_ref, ...), custom_call_target="tpu_custom_call" | custom-call | flops 2147483648 | bytes 7340032 | tf_op jit(solution)/shard_map/pallas_call | solution.py:79
  115.9 10.4 %shard_map.77.window_ref = f32[512,1024]{1,0:T(8,128)S(1)} custom-call(f32[1,1]{1,0:T(1,128)} %bitcast.24.allow_ref, bf16[512,1024]{1,0:T(8,128)(2,1)S(1)} %shard_map.74.q_ref, bf16[1024,1024]{1,0:T(8,128)(2,1)S(1)} %copy-done.2, bf16[1024,1024]{1,0:T(8,128)(2,1)S(1)} %copy-done.4), custom_call_target="tpu_custom_call" | custom-call | flops 2147483648 | bytes 7340032 | tf_op jit(solution)/shard_map/pallas_call | solution.py:157
  126.4 1.3 copy-done.5
  127.7 1.4 collective-permute-done.10
  129.1 1.7 %broadcast_select_fusion.1 = (bf16[512,1024]{1,0:T(8,128)(2,1)S(1)}, bf16[512,1024]{1,0:T(8,128)(2,1)S(1)}) fusion(bf16[512,1024]{1,0:T(8,128)(2,1)} %collective-permute-done.8, bf16[512,1024]{1,0:T(8,128)(2,1)} %collective-permute-done.10, pred[]{:T(512)S(6)} %eq.21), kind=kLoop, calls=%fused_computation.23 | loop fusion | flops 1048576 | bytes 4194305 | tf_op jit(solution)/shard_map/jit(_where)/select_n | solution.py:45
  130.8 1.1 all-gather.3.cloned.1.call-done
  131.9 0.8 slice_convert_fusion.2
  132.7 0.1 copy.77
  132.8 0.1 copy.78
  132.9 0.1 copy.79
  133.0 0.7 broadcast_divide_fusion.decay_ref
  133.8 2.2 %fusion.22.state_ref = bf16[8,128,128]{2,1,0:T(8,128)(2,1)} fusion(bf16[4,8,144,128]{3,2,1,0:T(8,128)(2,1)} %bitcast.71, f32[]{:T(128)} %bitcast.11, f32[8]{0:T(128)S(1)} %get-tuple-element.40, f32[8]{0:T(128)S(1)} %get-tuple-element.44, f32[8]{0:T(128)S(1)} %get-tuple-element.43, pred[]{:T(512)S(6)} %gt.15, pred[]{:T(512)S(6)} %gt.14, pred[]{:T(512)S(6)} %gt.13), kind=kLoop, calls=%fused_computation.30 | loop fusion | flops 1703936 | bytes 1048679 | tf_op jit(solution)/shard_map/convert_element_type | solution.py:278
  135.9 3.3 %shard_map.78 = bf16[512,1024]{1,0:T(8,128)(2,1)} custom-call(bf16[512,1024]{1,0:T(8,128)(2,1)} %copy-done.6, bf16[8,128,128]{2,1,0:T(8,128)(2,1)} %fusion.22.state_ref, f32[512,8]{1,0:T(8,128)} %broadcast_divide_fusion.decay_ref, f32[512,1024]{1,0:T(8,128)} %copy-done.5), custom_call_target="tpu_custom_call" | custom-call | tf_op jit(solution)/shard_map/pallas_call | solution.py:190
  139.2 2.7 %fusion.10 = bf16[512,1024]{1,0:T(8,128)(2,1)S(1)} fusion(bf16[512,1024]{1,0:T(8,128)(2,1)} %shard_map.78, bf16[1024,1024]{1,0:T(8,128)(2,1)} %param.11, pred[]{:T(512)S(6)} %eq.20, bf16[512,1024]{1,0:T(8,128)(2,1)S(1)} %get-tuple-element.28, bf16[512,1024]{1,0:T(8,128)(2,1)S(1)} %get-tuple-element.27), kind=kOutput, calls=%fused_computation.15 | convolution fusion | flops 1079508992 | bytes 6291457 | tf_op jit(solution)/shard_map/dot_general | solution.py:293
  141.9 0.1 collective-permute-start.11
  142.0 2.6 %collective-permute-done.11 = bf16[512,1024]{1,0:T(8,128)(2,1)S(1)} collective-permute-done((bf16[512,1024]{1,0:T(8,128)(2,1)S(1)}, bf16[512,1024]{1,0:T(8,128)(2,1)S(1)}, u32[]{:S(2)}, u32[]{:S(2)}) %collective-permute-start.11) | collective-permute-done | bytes 1048608 | tf_op jit(solution)/shard_map/ppermute | solution.py:17
  144.6 2.4 %fusion.15 = bf16[1,512,1024]{2,1,0:T(8,128)(2,1)} fusion(bf16[512,1024]{1,0:T(8,128)(2,1)S(1)} %collective-permute-done.11, bf16[512,1024]{1,0:T(8,128)(2,1)S(1)} %copy-done.10, bf16[1024,1024]{1,0:T(8,128)(2,1)S(1)} %copy-done.11, pred[]{:T(512)S(6)} %eq.20, bf16[512,1024]{1,0:T(8,128)(2,1)S(1)} %get-tuple-element.28, ...), kind=kOutput, calls=%fused_computation.16 | convolution fusion | flops 1081606144 | bytes 8388613 | tf_op jit(solution)/shard_map/dot_general | solution.py:295
  (38 shorter events, 0.2 us)
Async XLA Ops:
  6.5 17.9 %copy-start = (f32[1,8,512]{2,1,0:T(8,128)S(1)}, f32[1,8,512]{2,1,0:T(8,128)}, u32[]{:S(2)}) copy-start(f32[1,8,512]{2,1,0:T(8,128)} %param.12) | copy-start | bytes 49156
  6.5 125.4 %all-gather.3.cloned.1.call-start = ((), (), s32[]{:S(2)}) async-start(), calls=%async_computation | async-start | bytes 1474560 | tf_op jit(solution)/shard_map/all_gather | solution.py:269
  9.6 4.3 %copy-start.8 = (bf16[1,512,2048]{2,1,0:T(8,128)(2,1)S(1)}, bf16[1,512,2048]{2,1,0:T(8,128)(2,1)}, u32[]{:S(2)}) copy-start(bf16[1,512,2048]{2,1,0:T(8,128)(2,1)} %param.7) | copy-start | bytes 6291460
  9.6 4.8 %copy-start.12 = (f32[2048]{0:T(1024)S(1)}, f32[2048]{0:T(1024)}, u32[]{:S(2)}) copy-start(f32[2048]{0:T(1024)} %param.8) | copy-start | bytes 24580
  11.0 26.3 %collective-permute-start = (bf16[512,1024]{1,0:T(8,128)(2,1)}, bf16[512,1024]{1,0:T(8,128)(2,1)S(1)}, u32[]{:S(2)}, u32[]{:S(2)}) collective-permute-start(bf16[512,1024]{1,0:T(8,128)(2,1)} %bitcast.65), channel_id=1, source_target_pairs={{0,2},{2,0},{1,3},{3,1},{4,6},{6,4},{5,7},{7,5},{8,10},{10,8},{9,1... | collective-permute-start | bytes 3145736 | tf_op jit(solution)/shard_map/ppermute | solution.py:40
  16.0 26.8 %collective-permute-start.4 = (bf16[512,1024]{1,0:T(8,128)(2,1)}, bf16[512,1024]{1,0:T(8,128)(2,1)}, u32[]{:S(2)}, u32[]{:S(2)}) collective-permute-start(bf16[512,1024]{1,0:T(8,128)(2,1)} %constant_dynamic-slice_fusion.1), channel_id=1, source_target_pairs={{0,4},{4,8},{8,12},{1,5},{5,9},{9,13},{2,6},{6,10},{10,14},{3,7},{... | collective-permute-start | bytes 3145736 | tf_op jit(solution)/shard_map/ppermute | solution.py:22
  37.3 13.4 %collective-permute-start.1 = (bf16[256,1024]{1,0:T(8,128)(2,1)}, bf16[256,1024]{1,0:T(8,128)(2,1)}, u32[]{:S(2)}, u32[]{:S(2)}) collective-permute-start(bf16[256,1024]{1,0:T(8,128)(2,1)} %bitcast.72), channel_id=1, source_target_pairs={{0,2},{2,0},{1,3},{3,1},{4,6},{6,4},{5,7},{7,5},{8,10},{10,8},{9,1... | collective-permute-start | bytes 1572872 | tf_op jit(solution)/shard_map/ppermute | solution.py:40
  41.3 23.9 %collective-permute-start.3 = (bf16[512,1024]{1,0:T(8,128)(2,1)S(1)}, bf16[512,1024]{1,0:T(8,128)(2,1)}, u32[]{:S(2)}, u32[]{:S(2)}) collective-permute-start(bf16[512,1024]{1,0:T(8,128)(2,1)S(1)} %collective-permute-done.first_ref), channel_id=1, source_target_pairs={{0,16},{16,0},{1,17},{17,1},{2,18},{18,2},{3,19},{19,3},{4,20},{20... | collective-permute-start | bytes 3145736 | tf_op jit(solution)/shard_map/ppermute | solution.py:40
  42.8 23.9 %collective-permute-start.5 = (bf16[512,1024]{1,0:T(8,128)(2,1)}, bf16[512,1024]{1,0:T(8,128)(2,1)}, u32[]{:S(2)}, u32[]{:S(2)}) collective-permute-start(bf16[512,1024]{1,0:T(8,128)(2,1)} %collective-permute-done.4), channel_id=1, source_target_pairs={{0,1},{1,0},{2,3},{3,2},{4,5},{5,4},{6,7},{7,6},{8,9},{9,8},{10,11... | collective-permute-start | bytes 3145736 | tf_op jit(solution)/shard_map/ppermute | solution.py:17
  50.7 13.0 %collective-permute-start.6 = (bf16[256,1024]{1,0:T(8,128)(2,1)}, bf16[256,1024]{1,0:T(8,128)(2,1)}, u32[]{:S(2)}, u32[]{:S(2)}) collective-permute-start(bf16[256,1024]{1,0:T(8,128)(2,1)} %collective-permute-done.1), channel_id=1, source_target_pairs={{0,4},{4,0},{8,12},{12,8},{1,5},{5,1},{9,13},{13,9},{2,6},{6,2},{1... | collective-permute-start | bytes 1572872 | tf_op jit(solution)/shard_map/ppermute | solution.py:40
  62.1 23.2 %collective-permute-start.2 = (bf16[512,1024]{1,0:T(8,128)(2,1)S(1)}, bf16[512,1024]{1,0:T(8,128)(2,1)}, u32[]{:S(2)}, u32[]{:S(2)}) collective-permute-start(bf16[512,1024]{1,0:T(8,128)(2,1)S(1)} %constant_dynamic-slice_fusion.4), channel_id=1, source_target_pairs={{0,2},{2,0},{1,3},{3,1},{4,6},{6,4},{5,7},{7,5},{8,10},{10,8},{9,1... | collective-permute-start | bytes 3145736 | tf_op jit(solution)/shard_map/ppermute | solution.py:40
  65.1 22.8 %collective-permute-start.9 = (bf16[512,1024]{1,0:T(8,128)(2,1)S(1)}, bf16[512,1024]{1,0:T(8,128)(2,1)S(1)}, u32[]{:S(2)}, u32[]{:S(2)}) collective-permute-start(bf16[512,1024]{1,0:T(8,128)(2,1)S(1)} %pad_maximum_fusion.4.first_ref), channel_id=1, source_target_pairs={{0,16},{16,0},{1,17},{17,1},{2,18},{18,2},{3,19},{19,3},{4,20},{20... | collective-permute-start | bytes 3145736 | tf_op jit(solution)/shard_map/ppermute | solution.py:40
  76.2 1.3 copy-start.1
  85.3 22.4 %collective-permute-start.8 = (bf16[512,1024]{1,0:T(8,128)(2,1)}, bf16[512,1024]{1,0:T(8,128)(2,1)}, u32[]{:S(2)}, u32[]{:S(2)}) collective-permute-start(bf16[512,1024]{1,0:T(8,128)(2,1)} %constant_dynamic-slice_fusion), channel_id=1, source_target_pairs={{0,2},{2,0},{1,3},{3,1},{4,6},{6,4},{5,7},{7,5},{8,10},{10,8},{9,1... | collective-permute-start | bytes 3145736 | tf_op jit(solution)/shard_map/ppermute | solution.py:40
  87.5 21.9 %collective-permute-start.7 = (bf16[512,1024]{1,0:T(8,128)(2,1)}, bf16[512,1024]{1,0:T(8,128)(2,1)S(1)}, u32[]{:S(2)}, u32[]{:S(2)}) collective-permute-start(bf16[512,1024]{1,0:T(8,128)(2,1)} %collective-permute-done.2.first_ref), channel_id=1, source_target_pairs={{0,4},{4,0},{8,12},{12,8},{1,5},{5,1},{9,13},{13,9},{2,6},{6,2},{1... | collective-permute-start | bytes 3145736 | tf_op jit(solution)/shard_map/ppermute | solution.py:40
  94.2 1.3 copy-start.3
  107.7 21.5 %collective-permute-start.10 = (bf16[512,1024]{1,0:T(8,128)(2,1)}, bf16[512,1024]{1,0:T(8,128)(2,1)}, u32[]{:S(2)}, u32[]{:S(2)}) collective-permute-start(bf16[512,1024]{1,0:T(8,128)(2,1)} %collective-permute-done.8), channel_id=1, source_target_pairs={{0,16},{16,0},{1,17},{17,1},{2,18},{18,2},{3,19},{19,3},{4,20},{20... | collective-permute-start | bytes 3145736 | tf_op jit(solution)/shard_map/ppermute | solution.py:40
  109.4 6.5 %copy-start.2 = (bf16[1024,1024]{1,0:T(8,128)(2,1)S(1)}, bf16[1024,1024]{1,0:T(8,128)(2,1)}, u32[]{:S(2)}) copy-start(bf16[1024,1024]{1,0:T(8,128)(2,1)} %copy-done.1) | copy-start | bytes 6291460
  109.4 6.5 %copy-start.4 = (bf16[1024,1024]{1,0:T(8,128)(2,1)S(1)}, bf16[1024,1024]{1,0:T(8,128)(2,1)}, u32[]{:S(2)}) copy-start(bf16[1024,1024]{1,0:T(8,128)(2,1)} %copy-done.3) | copy-start | bytes 6291460
  109.4 1.7 %copy-start.7 = (bf16[1024,1024]{1,0:T(8,128)(2,1)S(1)}, bf16[1024,1024]{1,0:T(8,128)(2,1)}, u32[]{:S(2)}) copy-start(bf16[1024,1024]{1,0:T(8,128)(2,1)} %own_ref.1) | copy-start | bytes 6291460
  115.9 10.5 %copy-start.6 = (bf16[512,1024]{1,0:T(8,128)(2,1)}, bf16[512,1024]{1,0:T(8,128)(2,1)S(1)}, u32[]{:S(2)}) copy-start(bf16[512,1024]{1,0:T(8,128)(2,1)S(1)} %shard_map.74.q_ref) | copy-start | bytes 3145732
  126.4 1.3 copy-start.5
  139.2 5.4 %copy-start.9 = (bf16[1,512,2048]{2,1,0:T(8,128)(2,1)S(1)}, bf16[1,512,2048]{2,1,0:T(8,128)(2,1)}, u32[]{:S(2)}) copy-start(bf16[1,512,2048]{2,1,0:T(8,128)(2,1)} %param.7) | copy-start | bytes 6291460
  139.2 5.4 %copy-start.10 = (bf16[512,1024]{1,0:T(8,128)(2,1)S(1)}, bf16[512,1024]{1,0:T(8,128)(2,1)}, u32[]{:S(2)}) copy-start(bf16[512,1024]{1,0:T(8,128)(2,1)} %shard_map.78) | copy-start | bytes 3145732
  139.2 5.4 %copy-start.11 = (bf16[1024,1024]{1,0:T(8,128)(2,1)S(1)}, bf16[1024,1024]{1,0:T(8,128)(2,1)}, u32[]{:S(2)}) copy-start(bf16[1024,1024]{1,0:T(8,128)(2,1)} %param.11) | copy-start | bytes 6291460
  141.9 2.7 %collective-permute-start.11 = (bf16[512,1024]{1,0:T(8,128)(2,1)S(1)}, bf16[512,1024]{1,0:T(8,128)(2,1)S(1)}, u32[]{:S(2)}, u32[]{:S(2)}) collective-permute-start(bf16[512,1024]{1,0:T(8,128)(2,1)S(1)} %fusion.10), channel_id=1, source_target_pairs={{0,1},{1,0},{2,3},{3,2},{4,5},{5,4},{6,7},{7,6},{8,9},{9,8},{10,11... | collective-permute-start | bytes 3145736 | tf_op jit(solution)/shard_map/ppermute | solution.py:17
Sparse Core Ops, SparseCore 0:
  100.9 30.9 all-gather.2

commit v7 on v6

--- a/solution.py
+++ b/solution.py
@@ -228,15 +228,20 @@
     own = [w_pair[:, :inner_here], w_pair[:, inner_here:], w_query, w_output]
     if paired:
         key_x = swapped(part_of(w_keyvalue, group, 2)[:, 0, :], "wloop")
+        value_part = part_of(w_keyvalue, 2 * group + twin, 4)[:, 1, :]
+        query_part, output_part = part_of(w_query, twin, 2), part_of(w_output, group, 2)
+        key_x, own[0], own[1], value_part, query_part, output_part = lax.optimization_barrier(
+            (key_x, own[0], own[1], value_part, query_part, output_part)
+        )
         key_y = swapped(key_x, "groups")
-        value_x = swapped(after(part_of(w_keyvalue, 2 * group + twin, 4)[:, 1, :], key_x), "wloop")
-        query_x = swapped(after(part_of(own[2], twin, 2), value_x), "wloop")
+        value_x = swapped(value_part, "wloop")
+        query_x = swapped(after(query_part, value_x), "wloop")
         value_z = swapped(after(value_x, ours), "seq")
         value_half = in_order(twin, value_x, value_z)
         value_y = swapped(after(value_half, key_y), "groups")
         keys = projection(place, both, own[0], key_x, key_y, head_dim)
         query_x = after(query_x, keys)
-        output_x = swapped(after(part_of(own[3], group, 2), query_x), "wloop")
+        output_x = swapped(after(output_part, query_x), "wloop")
         query_z = swapped(after(query_x, value_z), "seq")
         output_y = swapped(after(output_x, value_y), "groups")
         blocks = [

time: 155 us -> 154 us (level)
  waiting for transfers between devices: 39.6 us -> 37.9 us
    ppermute x9, waiting for transfers between devices: 35.8 us -> 27.8 us  [swapped(): lax.ppermute(value, axis, [(i, i + 1 - 2 * (i % 2)) for i in range(count)])]
    all_gather x1, waiting for transfers between devices: 1.1 us -> 7.25 us  [shards(): lax.all_gather(jnp.concatenate([local_state, small], axis=1), 'seq')]
    unnamed x30 -> x36, local copies, waits for them, and re-layouts: 13.8 us -> 15.4 us
    dynamic_slice x2 -> x1, local copies, waits for them, and re-layouts: 3.56 us -> 3.26 us  [part_of(): return lax.dynamic_slice_in_dim(block, index * rows, rows, 0)]
  transfers between devices with their start and end apart: 13 -> 13, of which waited for: 9 -> 10; matrix products, arithmetic and copies ran while one was open for 17% -> 17% of each run, Pallas kernels for 21% -> 21%
where the time goes in v7:
time: 154 us
  waiting for transfers between devices  37.9 us (25%)
  Pallas kernels  35.6 us (23%)
  local copies, waits for them, and re-layouts  28.2 us (18%)
  starting transfers between devices  19.1 us (12%)
  between operations  14.3 us (9%)
  other arithmetic  12.4 us (8%)
  matrix products  6.03 us (4%)
    ppermute x9, waiting for transfers between devices, swapped(): lax.ppermute(value, axis, [(i, i + 1 - 2 * (i % 2)) for i in range(count)])  27.8 us
    pallas_call x3, Pallas kernels, projection(): pl.pallas_call(functools.partial(projection_kernel, head_dim), grid=(inne...  18.5 us
    unnamed x36, local copies, waits for them, and re-layouts  15.4 us
    ppermute x9, starting transfers between devices, swapped(): lax.ppermute(value, axis, [(i, i + 1 - 2 * (i % 2)) for i in range(count)])  14.5 us
    pallas_call x1, Pallas kernels, window_mix(): pl.pallas_call(functools.partial(window_kernel, scale), grid=(inner // he...  10.4 us
    all_gather x1, waiting for transfers between devices, shards(): lax.all_gather(jnp.concatenate([local_state, small], axis=1), 'seq')  7.25 us
    ppermute x1, starting transfers between devices, shifted(): return lax.ppermute(value, axis, [(i, i + 1) for i in range(count - 1)])  4.46 us
    pallas_call x1, Pallas kernels, local_states(): pl.pallas_call(state_kernel, grid=(heads // step,), in_specs=[block, bloc...  3.43 us
  transfers between devices with their start and end apart: 13, of which 10 were waited for; matrix products, arithmetic and copies ran while one was open for 17% of the time, Pallas kernels for 21%

profile of v7, /device:TPU:0, one launch (start us, length us, event | category | flops | bytes accessed | tf_op | source)
XLA Modules:
  0.0 153.5 jit_solution(14656791831183489887)
XLA Ops:
  6.5 3.0 %constant_dynamic-slice_fusion.4 = bf16[512,1,1024]{2,1,0:T(2,128)(2,1)S(1)} fusion(bf16[1024,2,1024]{2,1,0:T(2,128)(2,1)} %param.10, s32[]{:T(128)S(6)} %select_n.116), kind=kLoop, calls=%fused_computation.58 | loop fusion | bytes 2097156 | tf_op jit(solution)/shard_map/slice | solution.py:230
  9.6 1.5 copy.89
  11.1 2.9 %collective-permute-start = (bf16[512,1024]{1,0:T(8,128)(2,1)}, bf16[512,1024]{1,0:T(8,128)(2,1)S(1)}, u32[]{:S(2)}, u32[]{:S(2)}) collective-permute-start(bf16[512,1024]{1,0:T(8,128)(2,1)} %bitcast.65), channel_id=1, source_target_pairs={{0,2},{2,0},{1,3},{3,1},{4,6},{6,4},{5,7},{7,5},{8,10},{10,8},{9,1... | collective-permute-start | bytes 3145736 | tf_op jit(solution)/shard_map/ppermute | solution.py:40
  14.0 0.5 fusion
  14.5 0.5 fusion.2.refs_1_.refs_0_
  15.1 1.1 constant_dynamic-slice_fusion
  16.2 4.5 %collective-permute-start.4 = (bf16[512,1024]{1,0:T(8,128)(2,1)}, bf16[512,1024]{1,0:T(8,128)(2,1)}, u32[]{:S(2)}, u32[]{:S(2)}) collective-permute-start(bf16[512,1024]{1,0:T(8,128)(2,1)} %constant_dynamic-slice_fusion), channel_id=1, source_target_pairs={{0,4},{4,8},{8,12},{1,5},{5,9},{9,13},{2,6},{6,10},{10,14},{3,7},{... | collective-permute-start | bytes 3145736 | tf_op jit(solution)/shard_map/ppermute | solution.py:22
  20.6 5.6 %copy.86 = bf16[128,8,2,1024]{3,1,2,0:T(8,128)(2,1)} copy(bf16[128,8,2,1024]{3,2,1,0:T(2,128)(2,1)} %bitcast.68) | data formatting | bytes 8388608
  26.2 2.3 %constant_dynamic-slice_fusion.3 = bf16[256,1,1024]{2,1,0:T(2,128)(2,1)S(1)} fusion(bf16[1024,2,1024]{2,1,0:T(2,128)(2,1)} %param.10, s32[]{:T(128)S(6)} %select_n.117, s32[]{:T(128)S(6)} %add.146), kind=kLoop, calls=%fused_computation.57 | loop fusion | bytes 1048584 | tf_op jit(solution)/shard_map/slice | solution.py:231
  28.5 1.0 copy.90
  30.1 3.3 %constant_dynamic-slice_fusion.1 = (bf16[512,1024]{1,0:T(8,128)(2,1)}, bf16[512,1024]{1,0:T(8,128)(2,1)}) fusion(bf16[1024,1024]{1,0:T(8,128)(2,1)} %param.11, s32[]{:T(128)S(6)} %select_n.116, bf16[1024,1024]{1,0:T(8,128)(2,1)} %own_ref.1, s32[]{:T(128)S(6)} %select_n.118), kind=kLoop, calls=%fused_computation.55 | loop fusion | bytes 4194312 | tf_op jit(solution)/shard_map/dynamic_slice | solution.py:35
  33.4 2.4 %fusion.40 = (bf16[1024,1024]{1,0:T(8,128)(2,1)}, bf16[1024,1024]{1,0:T(8,128)(2,1)}) fusion(bf16[1024,2048]{1,0:T(8,128)(2,1)S(1)} %bitcast.67), kind=kLoop, calls=%fused_computation.85 | loop fusion | bytes 8388608 | tf_op jit(solution)/shard_map/slice | solution.py:228
  35.8 1.5 %collective-permute-done.first_ref = bf16[512,1024]{1,0:T(8,128)(2,1)S(1)} collective-permute-done((bf16[512,1024]{1,0:T(8,128)(2,1)}, bf16[512,1024]{1,0:T(8,128)(2,1)S(1)}, u32[]{:S(2)}, u32[]{:S(2)}) %collective-permute-start) | collective-permute-done | bytes 1048608 | tf_op jit(solution)/shard_map/ppermute | solution.py:40
  37.4 1.7 %collective-permute-start.1 = (bf16[256,1024]{1,0:T(8,128)(2,1)}, bf16[256,1024]{1,0:T(8,128)(2,1)}, u32[]{:S(2)}, u32[]{:S(2)}) collective-permute-start(bf16[256,1024]{1,0:T(8,128)(2,1)} %bitcast.66), channel_id=1, source_target_pairs={{0,2},{2,0},{1,3},{3,1},{4,6},{6,4},{5,7},{7,5},{8,10},{10,8},{9,1... | collective-permute-start | bytes 1572872 | tf_op jit(solution)/shard_map/ppermute | solution.py:40
  39.1 0.9 fusion.41
  40.1 0.1 copy.73
  40.2 0.1 multiply_reduce_fusion
  40.3 1.6 %collective-permute-start.3 = (bf16[512,1024]{1,0:T(8,128)(2,1)S(1)}, bf16[512,1024]{1,0:T(8,128)(2,1)}, u32[]{:S(2)}, u32[]{:S(2)}) collective-permute-start(bf16[512,1024]{1,0:T(8,128)(2,1)S(1)} %collective-permute-done.first_ref), channel_id=1, source_target_pairs={{0,16},{16,0},{1,17},{17,1},{2,18},{18,2},{3,19},{19,3},{4,20},{20... | collective-permute-start | bytes 3145736 | tf_op jit(solution)/shard_map/ppermute | solution.py:40
  41.9 0.2 collective-permute-done.4
  42.1 8.7 %collective-permute-done.1 = bf16[256,1024]{1,0:T(8,128)(2,1)} collective-permute-done((bf16[256,1024]{1,0:T(8,128)(2,1)}, bf16[256,1024]{1,0:T(8,128)(2,1)}, u32[]{:S(2)}, u32[]{:S(2)}) %collective-permute-start.1) | collective-permute-done | bytes 524320 | tf_op jit(solution)/shard_map/ppermute | solution.py:40
  50.8 1.6 %collective-permute-start.6 = (bf16[256,1024]{1,0:T(8,128)(2,1)}, bf16[256,1024]{1,0:T(8,128)(2,1)}, u32[]{:S(2)}, u32[]{:S(2)}) collective-permute-start(bf16[256,1024]{1,0:T(8,128)(2,1)} %collective-permute-done.1), channel_id=1, source_target_pairs={{0,4},{4,0},{8,12},{12,8},{1,5},{5,1},{9,13},{13,9},{2,6},{6,2},{1... | collective-permute-start | bytes 1572872 | tf_op jit(solution)/shard_map/ppermute | solution.py:40
  52.4 0.1 copy.85
  52.5 0.1 pad_add_fusion.1.place_ref
  52.6 1.5 collective-permute-start.2
  54.1 9.2 %collective-permute-done.6 = bf16[256,1024]{1,0:T(8,128)(2,1)} collective-permute-done((bf16[256,1024]{1,0:T(8,128)(2,1)}, bf16[256,1024]{1,0:T(8,128)(2,1)}, u32[]{:S(2)}, u32[]{:S(2)}) %collective-permute-start.6) | collective-permute-done | bytes 524320 | tf_op jit(solution)/shard_map/ppermute | solution.py:40
  63.3 1.3 broadcast_select_fusion.5
  64.7 1.2 collective-permute-start.9
  65.9 1.7 %broadcast_select_fusion.3 = (bf16[512,1024]{1,0:T(8,128)(2,1)S(1)}, bf16[512,1024]{1,0:T(8,128)(2,1)S(1)}) fusion(bf16[512,1024]{1,0:T(8,128)(2,1)} %collective-permute-done.4, bf16[512,1024]{1,0:T(8,128)(2,1)} %collective-permute-done.5, pred[]{:T(512)S(6)} %eq.18), kind=kLoop, calls=%fused_computation.25 | loop fusion | flops 1048576 | bytes 4194305 | tf_op jit(solution)/shard_map/jit(_where)/select_n | solution.py:224
  67.6 0.2 pad_maximum_fusion.refs_0_
  67.8 1.4 copy-done.7
  69.2 7.6 %shard_map.73.k_ref = bf16[1024,1024]{1,0:T(8,128)(2,1)S(1)} custom-call(s32[2]{0:T(128)S(1)} %pad_add_fusion.1.place_ref, bf16[1024,1024]{1,0:T(8,128)(2,1)S(1)} %copy-done.7, bf16[512,1024]{1,0:T(8,128)(2,1)S(1)} %collective-permute-done.first_ref, bf16[512,1024]{1,0:T(8,128)(2,1)} %collective-permute-done.3.second_ref, ...), custom_call_target="tpu_custom_call" | custom-call | flops 4294967296 | bytes 10485760 | tf_op jit(solution)/shard_map/pallas_call | solution.py:79
  76.8 1.3 copy-done.1
  78.1 1.5 collective-permute-start.8
  79.6 0.7 subtract_exponential_fusion.weight_ref
  80.3 1.7 %collective-permute-start.7 = (bf16[512,1024]{1,0:T(8,128)(2,1)}, bf16[512,1024]{1,0:T(8,128)(2,1)S(1)}, u32[]{:S(2)}, u32[]{:S(2)}) collective-permute-start(bf16[512,1024]{1,0:T(8,128)(2,1)} %collective-permute-done.2.first_ref), channel_id=1, source_target_pairs={{0,4},{4,0},{8,12},{12,8},{1,5},{5,1},{9,13},{13,9},{2,6},{6,2},{1... | collective-permute-start | bytes 3145736 | tf_op jit(solution)/shard_map/ppermute | solution.py:40
  82.1 5.2 %collective-permute-done.9.second_ref = bf16[512,1024]{1,0:T(8,128)(2,1)S(1)} collective-permute-done((bf16[512,1024]{1,0:T(8,128)(2,1)S(1)}, bf16[512,1024]{1,0:T(8,128)(2,1)S(1)}, u32[]{:S(2)}, u32[]{:S(2)}) %collective-permute-start.9) | collective-permute-done | bytes 1048608 | tf_op jit(solution)/shard_map/ppermute | solution.py:40
  87.2 6.2 %shard_map.75.v_ref = bf16[1024,1024]{1,0:T(8,128)(2,1)S(1)} custom-call(s32[2]{0:T(128)S(1)} %pad_add_fusion.1.place_ref, bf16[1024,1024]{1,0:T(8,128)(2,1)S(1)} %copy-done.6, bf16[512,1024]{1,0:T(8,128)(2,1)S(1)} %pad_maximum_fusion.4.first_ref, bf16[512,1024]{1,0:T(8,128)(2,1)S(1)} %collective-permute-done.9.second_ref, ...), custom_call_target="tpu_custom_call" | custom-call | flops 4294967296 | bytes 10485760 | tf_op jit(solution)/shard_map/pallas_call | solution.py:79
  93.5 1.3 copy-done.3
  94.8 3.4 %shard_map.76 = bf16[8,128,128]{2,1,0:T(8,128)(2,1)} custom-call(bf16[1024,1024]{1,0:T(8,128)(2,1)} %copy-done.1, bf16[1024,1024]{1,0:T(8,128)(2,1)} %copy-done.3, f32[512,8]{1,0:T(8,128)} %subtract_exponential_fusion.weight_ref), custom_call_target="tpu_custom_call" | custom-call | tf_op jit(solution)/shard_map/pallas_call | solution.py:121
  98.3 0.1 broadcast_in_dim.26
  98.3 1.7 %pad_maximum_fusion.5 = bf16[8,144,128]{2,1,0:T(8,128)(2,1)} fusion(bf16[8,16,128]{2,1,0:T(8,128)(2,1)S(1)} %broadcast_in_dim.26, bf16[8,128,128]{2,1,0:T(8,128)(2,1)} %shard_map.76), kind=kLoop, calls=%fused_computation.41 | loop fusion | flops 589824 | bytes 589824 | tf_op jit(solution)/shard_map/concatenate | solution.py:274
  100.1 0.7 collective-permute-done.8
  100.8 0.7 collective-permute-start.10
  101.5 0.1 copy.80
  101.6 0.1 pad_add_fusion.place_ref
  101.7 0.6 collective-permute-done.7.second_ref
  102.3 1.9 %copy-done.9 = bf16[1024,1024]{1,0:T(8,128)(2,1)S(1)} copy-done((bf16[1024,1024]{1,0:T(8,128)(2,1)S(1)}, bf16[1024,1024]{1,0:T(8,128)(2,1)}, u32[]{:S(2)}) %copy-start.9) | copy-done | bytes 2097176
  104.2 4.7 %shard_map.74.q_ref = bf16[512,1024]{1,0:T(8,128)(2,1)S(1)} custom-call(s32[2]{0:T(128)S(1)} %pad_add_fusion.place_ref, bf16[1024,1024]{1,0:T(8,128)(2,1)S(1)} %copy-done.9, bf16[512,1024]{1,0:T(8,128)(2,1)} %collective-permute-done.2.first_ref, bf16[512,1024]{1,0:T(8,128)(2,1)S(1)} %collective-permute-done.7.second_ref, ...), custom_call_target="tpu_custom_call" | custom-call | flops 2147483648 | bytes 7340032 | tf_op jit(solution)/shard_map/pallas_call | solution.py:79
  108.9 10.4 %shard_map.77.window_ref = f32[512,1024]{1,0:T(8,128)S(1)} custom-call(f32[1,1]{1,0:T(1,128)} %bitcast.24.allow_ref, bf16[512,1024]{1,0:T(8,128)(2,1)S(1)} %shard_map.74.q_ref, bf16[1024,1024]{1,0:T(8,128)(2,1)S(1)} %copy-done.2, bf16[1024,1024]{1,0:T(8,128)(2,1)S(1)} %copy-done.4), custom_call_target="tpu_custom_call" | custom-call | flops 2147483648 | bytes 7340032 | tf_op jit(solution)/shard_map/pallas_call | solution.py:157
  119.3 1.3 copy-done.5
  120.7 1.9 %collective-permute-done.10 = bf16[512,1024]{1,0:T(8,128)(2,1)} collective-permute-done((bf16[512,1024]{1,0:T(8,128)(2,1)}, bf16[512,1024]{1,0:T(8,128)(2,1)}, u32[]{:S(2)}, u32[]{:S(2)}) %collective-permute-start.10) | collective-permute-done | bytes 1048608 | tf_op jit(solution)/shard_map/ppermute | solution.py:40
  122.6 1.7 %broadcast_select_fusion.1 = (bf16[512,1024]{1,0:T(8,128)(2,1)S(1)}, bf16[512,1024]{1,0:T(8,128)(2,1)S(1)}) fusion(bf16[512,1024]{1,0:T(8,128)(2,1)} %collective-permute-done.8, bf16[512,1024]{1,0:T(8,128)(2,1)} %collective-permute-done.10, pred[]{:T(512)S(6)} %eq.21), kind=kLoop, calls=%fused_computation.23 | loop fusion | flops 1048576 | bytes 4194305 | tf_op jit(solution)/shard_map/jit(_where)/select_n | solution.py:45
  124.3 7.3 %all-gather.3.cloned.1.call-done = bf16[32,144,128]{2,1,0:T(8,128)(2,1)} async-done(((bf16[8,144,128]{2,1,0:T(8,128)(2,1)}), bf16[32,144,128]{2,1,0:T(8,128)(2,1)}) %all-gather.3.cloned.1.call-update) | async-done | bytes 1179664 | tf_op jit(solution)/shard_map/all_gather | solution.py:274
  131.5 0.8 slice_convert_fusion.2
  132.3 0.1 copy.77
  132.4 0.1 copy.78
  132.5 0.1 copy.79
  132.6 0.7 broadcast_divide_fusion.decay_ref
  133.4 2.2 %fusion.22.state_ref = bf16[8,128,128]{2,1,0:T(8,128)(2,1)} fusion(bf16[4,8,144,128]{3,2,1,0:T(8,128)(2,1)} %bitcast.71, f32[]{:T(128)} %bitcast.11, f32[8]{0:T(128)S(1)} %get-tuple-element.50, f32[8]{0:T(128)S(1)} %fusion.39, f32[8]{0:T(128)S(1)} %fusion.38, pred[]{:T(512)S(6)} %gt.15, pred[]{:T(512)S(6)} %gt.14, pred[]{:T(512)S(6)} %gt.13), kind=kLoop, calls=%fused_computation.30 | loop fusion | flops 1703936 | bytes 1048679 | tf_op jit(solution)/shard_map/convert_element_type | solution.py:283
  135.5 3.3 %shard_map.78 = bf16[512,1024]{1,0:T(8,128)(2,1)} custom-call(bf16[512,1024]{1,0:T(8,128)(2,1)} %copy-done.8, bf16[8,128,128]{2,1,0:T(8,128)(2,1)} %fusion.22.state_ref, f32[512,8]{1,0:T(8,128)} %broadcast_divide_fusion.decay_ref, f32[512,1024]{1,0:T(8,128)} %copy-done.5), custom_call_target="tpu_custom_call" | custom-call | tf_op jit(solution)/shard_map/pallas_call | solution.py:190
  138.8 2.7 %fusion.10 = bf16[512,1024]{1,0:T(8,128)(2,1)S(1)} fusion(bf16[512,1024]{1,0:T(8,128)(2,1)} %shard_map.78, bf16[1024,1024]{1,0:T(8,128)(2,1)} %param.11, pred[]{:T(512)S(6)} %eq.20, bf16[512,1024]{1,0:T(8,128)(2,1)S(1)} %get-tuple-element.38, bf16[512,1024]{1,0:T(8,128)(2,1)S(1)} %get-tuple-element.37), kind=kOutput, calls=%fused_computation.15 | convolution fusion | flops 1079508992 | bytes 6291457 | tf_op jit(solution)/shard_map/dot_general | solution.py:298
  141.5 0.1 collective-permute-start.11
  141.6 2.6 %collective-permute-done.11 = bf16[512,1024]{1,0:T(8,128)(2,1)S(1)} collective-permute-done((bf16[512,1024]{1,0:T(8,128)(2,1)S(1)}, bf16[512,1024]{1,0:T(8,128)(2,1)S(1)}, u32[]{:S(2)}, u32[]{:S(2)}) %collective-permute-start.11) | collective-permute-done | bytes 1048608 | tf_op jit(solution)/shard_map/ppermute | solution.py:17
  144.2 2.4 %fusion.15 = bf16[1,512,1024]{2,1,0:T(8,128)(2,1)} fusion(bf16[512,1024]{1,0:T(8,128)(2,1)S(1)} %collective-permute-done.11, bf16[512,1024]{1,0:T(8,128)(2,1)S(1)} %copy-done.13, bf16[1024,1024]{1,0:T(8,128)(2,1)S(1)} %copy-done.14, pred[]{:T(512)S(6)} %eq.20, bf16[512,1024]{1,0:T(8,128)(2,1)S(1)} %get-tuple-element.38, ...), kind=kOutput, calls=%fused_computation.16 | convolution fusion | flops 1081606144 | bytes 8388613 | tf_op jit(solution)/shard_map/dot_general | solution.py:300
  (44 shorter events, 0.2 us)
Async XLA Ops:
  6.5 32.6 %copy-start = (f32[1,8,512]{2,1,0:T(8,128)S(1)}, f32[1,8,512]{2,1,0:T(8,128)}, u32[]{:S(2)}) copy-start(f32[1,8,512]{2,1,0:T(8,128)} %param.12) | copy-start | bytes 49156
  6.5 125.0 %all-gather.3.cloned.1.call-start = ((), (), s32[]{:S(2)}) async-start(), calls=%async_computation | async-start | bytes 1474560 | tf_op jit(solution)/shard_map/all_gather | solution.py:274
  9.6 4.4 %copy-start.11 = (bf16[1,512,2048]{2,1,0:T(8,128)(2,1)S(1)}, bf16[1,512,2048]{2,1,0:T(8,128)(2,1)}, u32[]{:S(2)}) copy-start(bf16[1,512,2048]{2,1,0:T(8,128)(2,1)} %param.7) | copy-start | bytes 6291460
  9.6 4.9 %copy-start.15 = (f32[2048]{0:T(1024)S(1)}, f32[2048]{0:T(1024)}, u32[]{:S(2)}) copy-start(f32[2048]{0:T(1024)} %param.8) | copy-start | bytes 24580
  11.1 26.3 %collective-permute-start = (bf16[512,1024]{1,0:T(8,128)(2,1)}, bf16[512,1024]{1,0:T(8,128)(2,1)S(1)}, u32[]{:S(2)}, u32[]{:S(2)}) collective-permute-start(bf16[512,1024]{1,0:T(8,128)(2,1)} %bitcast.65), channel_id=1, source_target_pairs={{0,2},{2,0},{1,3},{3,1},{4,6},{6,4},{5,7},{7,5},{8,10},{10,8},{9,1... | collective-permute-start | bytes 3145736 | tf_op jit(solution)/shard_map/ppermute | solution.py:40
  16.2 25.9 %collective-permute-start.4 = (bf16[512,1024]{1,0:T(8,128)(2,1)}, bf16[512,1024]{1,0:T(8,128)(2,1)}, u32[]{:S(2)}, u32[]{:S(2)}) collective-permute-start(bf16[512,1024]{1,0:T(8,128)(2,1)} %constant_dynamic-slice_fusion), channel_id=1, source_target_pairs={{0,4},{4,8},{8,12},{1,5},{5,9},{9,13},{2,6},{6,10},{10,14},{3,7},{... | collective-permute-start | bytes 3145736 | tf_op jit(solution)/shard_map/ppermute | solution.py:22
  30.1 3.3 %copy-start.10 = (bf16[128,8,2,1024]{3,1,2,0:T(8,128)(2,1)S(1)}, bf16[128,8,2,1024]{3,1,2,0:T(8,128)(2,1)}, u32[]{:S(2)}) copy-start(bf16[128,8,2,1024]{3,1,2,0:T(8,128)(2,1)} %copy.86) | copy-start | bytes 12582916
  37.4 13.4 %collective-permute-start.1 = (bf16[256,1024]{1,0:T(8,128)(2,1)}, bf16[256,1024]{1,0:T(8,128)(2,1)}, u32[]{:S(2)}, u32[]{:S(2)}) collective-permute-start(bf16[256,1024]{1,0:T(8,128)(2,1)} %bitcast.66), channel_id=1, source_target_pairs={{0,2},{2,0},{1,3},{3,1},{4,6},{6,4},{5,7},{7,5},{8,10},{10,8},{9,1... | collective-permute-start | bytes 1572872 | tf_op jit(solution)/shard_map/ppermute | solution.py:40
  40.3 24.4 %collective-permute-start.3 = (bf16[512,1024]{1,0:T(8,128)(2,1)S(1)}, bf16[512,1024]{1,0:T(8,128)(2,1)}, u32[]{:S(2)}, u32[]{:S(2)}) collective-permute-start(bf16[512,1024]{1,0:T(8,128)(2,1)S(1)} %collective-permute-done.first_ref), channel_id=1, source_target_pairs={{0,16},{16,0},{1,17},{17,1},{2,18},{18,2},{3,19},{19,3},{4,20},{20... | collective-permute-start | bytes 3145736 | tf_op jit(solution)/shard_map/ppermute | solution.py:40
  42.1 23.8 %collective-permute-start.5 = (bf16[512,1024]{1,0:T(8,128)(2,1)}, bf16[512,1024]{1,0:T(8,128)(2,1)}, u32[]{:S(2)}, u32[]{:S(2)}) collective-permute-start(bf16[512,1024]{1,0:T(8,128)(2,1)} %collective-permute-done.4), channel_id=1, source_target_pairs={{0,1},{1,0},{2,3},{3,2},{4,5},{5,4},{6,7},{7,6},{8,9},{9,8},{10,11... | collective-permute-start | bytes 3145736 | tf_op jit(solution)/shard_map/ppermute | solution.py:17
  50.8 12.5 %collective-permute-start.6 = (bf16[256,1024]{1,0:T(8,128)(2,1)}, bf16[256,1024]{1,0:T(8,128)(2,1)}, u32[]{:S(2)}, u32[]{:S(2)}) collective-permute-start(bf16[256,1024]{1,0:T(8,128)(2,1)} %collective-permute-done.1), channel_id=1, source_target_pairs={{0,4},{4,0},{8,12},{12,8},{1,5},{5,1},{9,13},{13,9},{2,6},{6,2},{1... | collective-permute-start | bytes 1572872 | tf_op jit(solution)/shard_map/ppermute | solution.py:40
  52.6 25.5 %collective-permute-start.2 = (bf16[512,1024]{1,0:T(8,128)(2,1)}, bf16[512,1024]{1,0:T(8,128)(2,1)}, u32[]{:S(2)}, u32[]{:S(2)}) collective-permute-start(bf16[512,1024]{1,0:T(8,128)(2,1)} %get-tuple-element.22), channel_id=1, source_target_pairs={{0,2},{2,0},{1,3},{3,1},{4,6},{6,4},{5,7},{7,5},{8,10},{10,8},{9,1... | collective-permute-start | bytes 3145736 | tf_op jit(solution)/shard_map/ppermute | solution.py:40
  64.7 22.6 %collective-permute-start.9 = (bf16[512,1024]{1,0:T(8,128)(2,1)S(1)}, bf16[512,1024]{1,0:T(8,128)(2,1)S(1)}, u32[]{:S(2)}, u32[]{:S(2)}) collective-permute-start(bf16[512,1024]{1,0:T(8,128)(2,1)S(1)} %pad_maximum_fusion.4.first_ref), channel_id=1, source_target_pairs={{0,16},{16,0},{1,17},{17,1},{2,18},{18,2},{3,19},{19,3},{4,20},{20... | collective-permute-start | bytes 3145736 | tf_op jit(solution)/shard_map/ppermute | solution.py:40
  67.6 1.6 %copy-start.7 = (bf16[1024,1024]{1,0:T(8,128)(2,1)S(1)}, bf16[1024,1024]{1,0:T(8,128)(2,1)}, u32[]{:S(2)}) copy-start(bf16[1024,1024]{1,0:T(8,128)(2,1)} %get-tuple-element.23.own_ref) | copy-start | bytes 6291460
  69.2 18.0 %copy-start.6 = (bf16[1024,1024]{1,0:T(8,128)(2,1)S(1)}, bf16[1024,1024]{1,0:T(8,128)(2,1)}, u32[]{:S(2)}) copy-start(bf16[1024,1024]{1,0:T(8,128)(2,1)} %get-tuple-element.31.own_ref) | copy-start | bytes 6291460
  76.8 1.3 copy-start.1
  78.1 22.7 %collective-permute-start.8 = (bf16[512,1024]{1,0:T(8,128)(2,1)}, bf16[512,1024]{1,0:T(8,128)(2,1)}, u32[]{:S(2)}, u32[]{:S(2)}) collective-permute-start(bf16[512,1024]{1,0:T(8,128)(2,1)} %get-tuple-element.29), channel_id=1, source_target_pairs={{0,2},{2,0},{1,3},{3,1},{4,6},{6,4},{5,7},{7,5},{8,10},{10,8},{9,1... | collective-permute-start | bytes 3145736 | tf_op jit(solution)/shard_map/ppermute | solution.py:40
  80.3 21.9 %collective-permute-start.7 = (bf16[512,1024]{1,0:T(8,128)(2,1)}, bf16[512,1024]{1,0:T(8,128)(2,1)S(1)}, u32[]{:S(2)}, u32[]{:S(2)}) collective-permute-start(bf16[512,1024]{1,0:T(8,128)(2,1)} %collective-permute-done.2.first_ref), channel_id=1, source_target_pairs={{0,4},{4,0},{8,12},{12,8},{1,5},{5,1},{9,13},{13,9},{2,6},{6,2},{1... | collective-permute-start | bytes 3145736 | tf_op jit(solution)/shard_map/ppermute | solution.py:40
  93.5 1.4 copy-start.3
  100.8 21.8 %collective-permute-start.10 = (bf16[512,1024]{1,0:T(8,128)(2,1)}, bf16[512,1024]{1,0:T(8,128)(2,1)}, u32[]{:S(2)}, u32[]{:S(2)}) collective-permute-start(bf16[512,1024]{1,0:T(8,128)(2,1)} %collective-permute-done.8), channel_id=1, source_target_pairs={{0,16},{16,0},{1,17},{17,1},{2,18},{18,2},{3,19},{19,3},{4,20},{20... | collective-permute-start | bytes 3145736 | tf_op jit(solution)/shard_map/ppermute | solution.py:40
  101.7 7.1 %copy-start.2 = (bf16[1024,1024]{1,0:T(8,128)(2,1)S(1)}, bf16[1024,1024]{1,0:T(8,128)(2,1)}, u32[]{:S(2)}) copy-start(bf16[1024,1024]{1,0:T(8,128)(2,1)} %copy-done.1) | copy-start | bytes 6291460
  101.7 7.1 %copy-start.4 = (bf16[1024,1024]{1,0:T(8,128)(2,1)S(1)}, bf16[1024,1024]{1,0:T(8,128)(2,1)}, u32[]{:S(2)}) copy-start(bf16[1024,1024]{1,0:T(8,128)(2,1)} %copy-done.3) | copy-start | bytes 6291460
  102.3 1.9 %copy-start.9 = (bf16[1024,1024]{1,0:T(8,128)(2,1)S(1)}, bf16[1024,1024]{1,0:T(8,128)(2,1)}, u32[]{:S(2)}) copy-start(bf16[1024,1024]{1,0:T(8,128)(2,1)} %own_ref.1) | copy-start | bytes 6291460
  108.8 10.5 %copy-start.8 = (bf16[512,1024]{1,0:T(8,128)(2,1)}, bf16[512,1024]{1,0:T(8,128)(2,1)S(1)}, u32[]{:S(2)}) copy-start(bf16[512,1024]{1,0:T(8,128)(2,1)S(1)} %shard_map.74.q_ref) | copy-start | bytes 3145732
  119.3 1.4 copy-start.5
  138.8 5.4 %copy-start.12 = (bf16[1,512,2048]{2,1,0:T(8,128)(2,1)S(1)}, bf16[1,512,2048]{2,1,0:T(8,128)(2,1)}, u32[]{:S(2)}) copy-start(bf16[1,512,2048]{2,1,0:T(8,128)(2,1)} %param.7) | copy-start | bytes 6291460
  138.8 5.4 %copy-start.13 = (bf16[512,1024]{1,0:T(8,128)(2,1)S(1)}, bf16[512,1024]{1,0:T(8,128)(2,1)}, u32[]{:S(2)}) copy-start(bf16[512,1024]{1,0:T(8,128)(2,1)} %shard_map.78) | copy-start | bytes 3145732
  138.8 5.4 %copy-start.14 = (bf16[1024,1024]{1,0:T(8,128)(2,1)S(1)}, bf16[1024,1024]{1,0:T(8,128)(2,1)}, u32[]{:S(2)}) copy-start(bf16[1024,1024]{1,0:T(8,128)(2,1)} %param.11) | copy-start | bytes 6291460
  141.5 2.7 %collective-permute-start.11 = (bf16[512,1024]{1,0:T(8,128)(2,1)S(1)}, bf16[512,1024]{1,0:T(8,128)(2,1)S(1)}, u32[]{:S(2)}, u32[]{:S(2)}) collective-permute-start(bf16[512,1024]{1,0:T(8,128)(2,1)S(1)} %fusion.10), channel_id=1, source_target_pairs={{0,1},{1,0},{2,3},{3,2},{4,5},{5,4},{6,7},{7,6},{8,9},{9,8},{10,11... | collective-permute-start | bytes 3145736 | tf_op jit(solution)/shard_map/ppermute | solution.py:17
Sparse Core Ops, SparseCore 0:
  100.2 31.2 all-gather.2
